TPU v7x, 32 devices: a whole 2x2x4 slice. The times are simulated.
32 devices in a mesh: strat: 4 (over y, core), grp: 8 (over z, x).
Axes of the slice: x: 2, y: 2, z: 4, core: 2. Of those that a mesh axis runs over, the one named last changes fastest.
Arguments:
- user_factors: float32 [32768, 256], P(('strat', 'grp')), may hold values from -1.5 to 1.5
- item_factors: float32 [16384, 256], P('strat'), may hold values from -1.5 to 1.5
- tile_coords: int32 [4, 8, 3, 2, 16], P('strat', 'grp'), may hold values from 0 to 31, as said below
- tile_counts: int32 [4, 8, 3], P('strat', 'grp'), may hold values from 5 to 16, as said below
- tile_values: bfloat16 [4, 8, 3, 16, 128, 128], P('strat', 'grp'), may hold values from 0 to 10
Outputs:
- users_out: float32 [32768, 256], P(('strat', 'grp'))
- items_out: float32 [16384, 256], P('strat')
Inputs may be any that keep to these rules, and one draw needn't show every extreme that they name: `tile_coords`: each list names distinct tiles; user tiles lie below 8 and item tiles below 32; entries at and after the count are ignored. `tile_counts`: in every sub-epoch some device has exactly 16 live tiles.
All inputs are finite; a program needn't handle non-finite values.
Results may differ from a plain program's by a relative error of at most 0.0018.
Values sent between devices are 32-bit elements; how exact they have to be, the bound alone decides.
No kernel may reach another device: no remote copies, remote signals or barrier semaphores. Data moves between devices by JAX's collectives and lax.ppermute only.
A program may use at most 64 MiB of HBM per device.

v0:
```python
import jax
import jax.numpy as jnp
from jax import lax
from jax.sharding import PartitionSpec as P


def from_behind(block, axis, distance):
    devices = range(lax.axis_size(axis))
    route = [((i - distance) % len(devices), i) for i in devices]
    return lax.ppermute(block, axis, route)


def tile_terms(user_b, slab_b, coords, count, values):
    high = lax.Precision.HIGHEST
    side = values.shape[-1]
    width = user_b.shape[1]
    user_tiles = user_b.shape[0] // side
    item_tiles = slab_b.shape[0] // side
    urows = jnp.take(user_b.reshape(user_tiles, side, width), coords[0], axis=0)
    irows = jnp.take(slab_b.reshape(item_tiles, side, width), coords[1], axis=0)
    predicted = jnp.einsum("nrk,nck->nrc", urows, irows, preferred_element_type=jnp.float32)
    resid = (values.astype(jnp.float32) - predicted).astype(jnp.bfloat16)
    user_part = jnp.einsum("nrc,nck->nrk", resid, irows, preferred_element_type=jnp.float32)
    item_part = jnp.einsum("nrc,nrk->nck", resid, urows, preferred_element_type=jnp.float32)
    live = jnp.arange(coords.shape[1]) < count
    one_user = ((coords[0][:, None] == jnp.arange(user_tiles)[None, :]) & live[:, None]).astype(
        jnp.float32
    )
    one_item = ((coords[1][:, None] == jnp.arange(item_tiles)[None, :]) & live[:, None]).astype(
        jnp.float32
    )
    user_grad = jnp.einsum("nt,nrk->trk", one_user, user_part, precision=high).reshape(-1, width)
    item_grad = jnp.einsum("nt,nrk->trk", one_item, item_part, precision=high).reshape(-1, width)
    return (user_grad, item_grad)


def per_device(user_factors, item_factors, tile_coords, tile_counts, tile_values):
    users = user_factors
    slab = item_factors
    coords = tile_coords[0, 0]
    counts = tile_counts[0, 0]
    values = tile_values[0, 0]
    rounds = coords.shape[0]
    for sub in range(rounds):
        user_grad, item_grad = tile_terms(
            users.astype(jnp.bfloat16),
            slab.astype(jnp.bfloat16),
            coords[sub],
            counts[sub],
            values[sub],
        )
        users = users - 0.003 * (0.05 * users - user_grad)
        total = lax.psum(item_grad, "grp")
        slab = slab - 0.003 * (0.05 * slab - total)
        if sub + 1 < rounds:
            slab = from_behind(slab, "strat", -1)
    return (users, slab)


def solution(mesh):
    placed = (
        P(("strat", "grp"), None),
        P("strat", None),
        P("strat", "grp", None, None, None),
        P("strat", "grp", None),
        P("strat", "grp", None, None, None, None),
    )
    return jax.shard_map(
        per_device,
        mesh=mesh,
        in_specs=placed,
        out_specs=(P(("strat", "grp"), None), P("strat", None)),
        check_vma=False,
    )
```

profile of v0, /device:TPU:0, one launch (start us, length us, event | category | flops | bytes accessed | tf_op | source)
XLA Modules:
  0.0 650.7 jit_solution(3984815403233958206)
XLA Ops:
  7.2 0.0 all-reduce.4.cloned.1.call-start
  7.2 0.8 slice_bitcast_fusion
  8.0 0.8 compare_and_fusion
  8.8 1.4 fusion.68
  10.1 0.6 iota_compare_fusion.8
  10.8 1.3 convert_element_type.53
  12.1 2.4 convert_element_type.54
  14.5 1.6 gather_fusion
  16.1 0.6 gather_fusion.1
  16.7 0.0 copy-start.3
  16.7 2.0 fusion.12
  18.7 0.0 copy-done.3
  18.7 0.5 fusion.21
  19.2 2.9 fusion.8
  22.1 4.4 copy.8
  26.6 0.0 all-reduce.4.cloned.1.call-update
  26.6 0.0 all-reduce.6.cloned.1.call-start
  26.6 159.1 %all-reduce.4.cloned.1.call-done = f32[4096,256]{1,0:T(8,128)} async-done(((f32[4096,256]{1,0:T(8,128)}), f32[4096,256]{1,0:T(8,128)}) %all-reduce.4.cloned.1.call-update) | async-done | bytes 4194320 | tf_op jit(solution)/shard_map/psum | solution.py:53
  185.7 6.2 multiply_subtract_fusion.2
  191.9 0.9 collective-permute-start
  192.7 0.5 fusion.22
  193.3 0.0 copy-start
  193.3 2.0 fusion.10
  195.2 0.3 copy.7
  195.6 0.2 fusion.27
  195.8 1.6 gather_fusion.2
  197.4 0.6 iota_compare_fusion.7
  198.0 41.1 %collective-permute-done = f32[4096,256]{1,0:T(8,128)} collective-permute-done((f32[4096,256]{1,0:T(8,128)}, f32[4096,256]{1,0:T(8,128)}, u32[]{:S(2)}, u32[]{:S(2)}) %collective-permute-start) | collective-permute-done | bytes 4194336 | tf_op jit(solution)/shard_map/ppermute | solution.py:10
  239.1 3.7 convert_element_type.59
  242.8 2.2 gather_fusion.3
  245.0 0.0 copy-start.1
  245.0 2.0 fusion.13
  247.0 0.0 copy-start.4
  247.0 0.5 fusion.23
  247.5 0.3 copy-done.4
  247.8 2.9 fusion.4
  250.7 4.4 copy.10
  255.2 0.0 all-reduce.6.cloned.1.call-update
  255.2 0.0 all-reduce.8.cloned.1.call-start
  255.3 155.9 %all-reduce.6.cloned.1.call-done = f32[4096,256]{1,0:T(8,128)} async-done(((f32[4096,256]{1,0:T(8,128)}), f32[4096,256]{1,0:T(8,128)}) %all-reduce.6.cloned.1.call-update) | async-done | bytes 4194320 | tf_op jit(solution)/shard_map/psum | solution.py:53
  411.2 6.2 multiply_subtract_fusion.1
  417.4 0.9 collective-permute-start.1
  418.3 0.6 iota_compare_fusion.6
  418.9 0.5 fusion.24
  419.4 2.0 fusion.6
  421.4 0.3 copy.9
  421.7 1.1 fusion.67
  422.8 2.6 gather_fusion.4
  425.5 39.1 %collective-permute-done.1 = f32[4096,256]{1,0:T(8,128)} collective-permute-done((f32[4096,256]{1,0:T(8,128)}, f32[4096,256]{1,0:T(8,128)}, u32[]{:S(2)}, u32[]{:S(2)}) %collective-permute-start.1) | collective-permute-done | bytes 4194336 | tf_op jit(solution)/shard_map/ppermute | solution.py:10
  464.6 3.7 convert_element_type.64
  468.3 3.3 gather_fusion.5
  471.6 2.3 fusion.14
  473.9 0.0 copy-start.6
  473.9 0.5 fusion.25
  474.4 0.3 copy-done.6
  474.7 2.9 fusion
  477.6 4.4 copy.12
  482.0 0.0 all-reduce.8.cloned.1.call-update
  482.1 1.9 fusion.26
  484.0 2.0 fusion.2
  485.9 0.3 copy.11
  486.3 1.4 fusion.16
  487.7 150.4 %all-reduce.8.cloned.1.call-done = f32[4096,256]{1,0:T(8,128)} async-done(((f32[4096,256]{1,0:T(8,128)}), f32[4096,256]{1,0:T(8,128)}) %all-reduce.8.cloned.1.call-update) | async-done | bytes 4194320 | tf_op jit(solution)/shard_map/psum | solution.py:53
  638.0 6.2 multiply_subtract_fusion
  (9 shorter events, 0.0 us)
Async XLA Ops:
  7.2 178.6 %all-reduce.4.cloned.1.call-start = ((), (), s32[]{:S(2)}) async-start(), calls=%async_computation | async-start | bytes 8388608 | tf_op jit(solution)/shard_map/psum | solution.py:53
  16.7 2.0 copy-start.3
  26.6 384.6 %all-reduce.6.cloned.1.call-start = ((), (), s32[]{:S(2)}) async-start(), calls=%async_computation.1 | async-start | bytes 8388608 | tf_op jit(solution)/shard_map/psum | solution.py:53
  191.9 47.2 %collective-permute-start = (f32[4096,256]{1,0:T(8,128)}, f32[4096,256]{1,0:T(8,128)}, u32[]{:S(2)}, u32[]{:S(2)}) collective-permute-start(f32[4096,256]{1,0:T(8,128)} %multiply_subtract_fusion.2), channel_id=1, source_target_pairs={{8,0},{16,8},{24,16},{0,24},{9,1},{17,9},{25,17},{1,25},{10,2},{18... | collective-permute-start | bytes 12582920 | tf_op jit(solution)/shard_map/ppermute | solution.py:10
  193.3 2.4 copy-start
  245.0 2.0 copy-start.1
  247.0 0.8 copy-start.4
  255.2 382.8 %all-reduce.8.cloned.1.call-start = ((), (), s32[]{:S(2)}) async-start(), calls=%async_computation.2 | async-start | bytes 8388608 | tf_op jit(solution)/shard_map/psum | solution.py:53
  411.2 7.7 %copy-start.5 = (bf16[16,128,128]{2,1,0:T(8,128)(2,1)S(1)}, bf16[16,128,128]{2,1,0:T(8,128)(2,1)}, u32[]{:S(2)}) copy-start(bf16[16,128,128]{2,1,0:T(8,128)(2,1)} %copy-done.4) | copy-start | bytes 1572868
  417.4 47.2 %collective-permute-start.1 = (f32[4096,256]{1,0:T(8,128)}, f32[4096,256]{1,0:T(8,128)}, u32[]{:S(2)}, u32[]{:S(2)}) collective-permute-start(f32[4096,256]{1,0:T(8,128)} %multiply_subtract_fusion.1), channel_id=1, source_target_pairs={{8,0},{16,8},{24,16},{0,24},{9,1},{17,9},{25,17},{1,25},{10,2},{18... | collective-permute-start | bytes 12582920 | tf_op jit(solution)/shard_map/ppermute | solution.py:10
  471.6 2.3 copy-start.2
  473.9 0.8 copy-start.6
Sparse Core Ops, SparseCore 0:
  26.7 158.9 all-reduce.3
  255.3 155.8 all-reduce.5
  482.2 155.8 all-reduce.7
where the time goes:
time: 651 us
  waiting for transfers between devices  546 us (84%)
  other arithmetic  34.9 us (5%)
  local copies, waits for them, and re-layouts  28.9 us (4%)
  matrix products  25.3 us (4%)
  between operations  14 us (2%)
    psum x3, waiting for transfers between devices, per_device(): total = lax.psum(item_grad, 'grp')  465 us
    ppermute x2, waiting for transfers between devices, from_behind(): return lax.ppermute(block, axis, route)  80.2 us
    sub x3, other arithmetic, per_device(): slab = slab - 0.003 * (0.05 * slab - total)  18.5 us
    dot_general x3, local copies, waits for them, and re-layouts, tile_terms(): jnp.einsum('nt,nrk->trk', one_item, item_part, precision=high)  13.3 us
  transfers between devices with their start and end apart: 5, of which 5 were waited for; matrix products, arithmetic and copies ran while one was open for 3% of the time, Pallas kernels for 0%

commit v1 on v0

v1 whole, which is shorter than its diff:
```python
import functools

import jax
import jax.numpy as jnp
from jax import lax
from jax.experimental import pallas as pl
from jax.experimental.pallas import tpu as pltpu
from jax.sharding import PartitionSpec as P

RATE = 0.003
KEEP = 1.0 - 0.003 * 0.05
WAVES = 2
ANY = pl.BlockSpec(memory_space=pl.ANY)
VMEM = pl.BlockSpec(memory_space=pltpu.VMEM)
SMEM = pl.BlockSpec(memory_space=pltpu.SMEM)


def tile_kernel(sub, wave, side, n_own, *refs):
    fresh = sub == 0
    n_v = 1 if fresh else 2 * n_own
    coords, counts, place, users, running = refs[:5]
    slabs = refs[5 : 5 + n_v]
    values, out_u, near_f, near_b, far, own, held, grad, seen, mine, sems = refs[5 + n_v :]

    copies = []

    def copy(src, dst):
        c = pltpu.make_async_copy(src, dst, sems.at[len(copies)])
        c.start()
        copies.append(c)

    copy(values.at[sub], seen)
    if fresh:
        for way in range(2):
            copy(
                slabs[0].at[:, 2 * wave + way],
                held.at[pl.ds(way * n_own, n_own)],
            )
    else:
        for i, tile in enumerate(slabs):
            copy(tile, held.at[i])
    grad[...] = jnp.zeros_like(grad)
    if wave == 0:
        out_u[...] = users[...] * KEEP
    else:
        out_u[...] = running[...]
    for c in copies:
        c.wait()

    here = place[0]
    count = counts[sub]

    def one(n, carry):
        a = coords[sub, 0, n]
        b = coords[sub, 1, n]

        @pl.when((n < count) & (((b >> 1) & 1) == wave))
        def _():
            owner = b >> 2
            way = b & 1
            ahead = jnp.where(way == 0, here - owner, owner - here)
            slot = way * n_own + lax.rem(ahead + n_own, n_own)
            source = way * n_own + owner if fresh else slot
            rows = pl.ds(pl.multiple_of(a * side, side), side)
            ua = users[rows, :].astype(jnp.bfloat16)
            vb = held[source].astype(jnp.bfloat16)
            guess = lax.dot_general(
                ua, vb, (((1,), (1,)), ((), ())), preferred_element_type=jnp.float32
            )
            resid = (seen[n].astype(jnp.float32) - guess).astype(jnp.bfloat16)
            up = jnp.dot(resid, vb, preferred_element_type=jnp.float32)
            out_u[rows, :] += RATE * up
            ip = lax.dot_general(
                resid, ua, (((0,), (0,)), ((), ())), preferred_element_type=jnp.float32
            )
            grad[slot] += RATE * ip

        return carry

    lax.fori_loop(0, coords.shape[2], one, 0)

    copies.clear()
    copy(grad.at[1], near_f)
    copy(grad.at[n_own + 1], near_b)
    for way in range(2):
        copy(grad.at[pl.ds(way * n_own + 2, n_own - 2)], far.at[way])
    for way in range(2):
        source = way * n_own + here if fresh else way * n_own
        mine[way] = held[source] * KEEP + grad[way * n_own]
    copy(mine, own)
    for c in copies:
        c.wait()


def tile_step(sub, wave, n_own, coords, counts, place, users, running, slabs, values):
    side = values.shape[-1]
    width = users.shape[1]
    tile = jax.ShapeDtypeStruct((side, width), jnp.float32)
    slots = 2 * n_own
    return pl.pallas_call(
        functools.partial(tile_kernel, sub, wave, side, n_own),
        out_shape=(
            jax.ShapeDtypeStruct(users.shape, jnp.float32),
            tile,
            tile,
            jax.ShapeDtypeStruct((2, n_own - 2, side, width), jnp.float32),
            jax.ShapeDtypeStruct((2, side, width), jnp.float32),
        ),
        in_specs=[SMEM, SMEM, SMEM, VMEM, VMEM] + [ANY] * len(slabs) + [ANY],
        out_specs=(VMEM, ANY, ANY, ANY, ANY),
        scratch_shapes=[
            pltpu.VMEM((slots, side, width), jnp.float32),
            pltpu.VMEM((slots, side, width), jnp.float32),
            pltpu.VMEM(values.shape[1:], values.dtype),
            pltpu.VMEM((2, side, width), jnp.float32),
            pltpu.SemaphoreType.DMA((slots + 1,)),
        ],
        compiler_params=pltpu.CompilerParams(vmem_limit_bytes=24 * 2**20),
        cost_estimate=pl.CostEstimate(
            flops=8 * 3 * 2 * side * side * width,
            bytes_accessed=8 * 2**20,
            transcendentals=0,
        ),
        name=f"tiles_{sub}_{wave}",
    )(coords, counts, place, users, running, *slabs, values)


def lay_kernel(wave, n_own, carried, *refs):
    place = refs[0]
    tiles = refs[1 + carried : 1 + carried + 2 * n_own]
    out, sems = refs[1 + carried + 2 * n_own :]
    here = place[0]
    copies = []
    for way in range(2):
        for t in range(n_own):
            owner = lax.rem(here + (n_own - t if way == 0 else t), n_own)
            i = way * n_own + t
            c = pltpu.make_async_copy(tiles[i], out.at[owner, 2 * wave + way], sems.at[i])
            c.start()
            copies.append(c)
    for c in copies:
        c.wait()


def lay(wave, n_own, place, tiles, base):
    side, width = tiles[0].shape
    carried = () if base is None else (base,)
    return pl.pallas_call(
        functools.partial(lay_kernel, wave, n_own, len(carried)),
        out_shape=jax.ShapeDtypeStruct((n_own, 2 * WAVES, side, width), jnp.float32),
        in_specs=[SMEM] + [ANY] * (len(carried) + 2 * n_own),
        out_specs=ANY,
        scratch_shapes=[pltpu.SemaphoreType.DMA((2 * n_own,))],
        input_output_aliases={1: 0} if carried else {},
        cost_estimate=pl.CostEstimate(flops=0, bytes_accessed=4 * 2**20, transcendentals=0),
        name=f"lay_{wave}",
    )(place, *carried, *tiles)


def solution(mesh):
    n_strat = mesh.shape["strat"]
    n_grp = mesh.shape["grp"]
    at = list(range(0, n_grp, 2)) + list(range(n_grp - 1, 0, -2))
    ring = [
        [(at[r], at[(r + step) % n_grp]) for r in range(n_grp)] for step in (1, -1)
    ]
    last = [
        [
            (s * n_grp + i, ((s - 1) % n_strat) * n_grp + j)
            for s in range(n_strat)
            for i, j in hop
        ]
        for hop in ring
    ]
    turn = [(s, (s - 1) % n_strat) for s in range(n_strat)]

    def per_device(user_factors, item_factors, tile_coords, tile_counts, tile_values):
        coords = tile_coords[0, 0]
        counts = tile_counts[0, 0]
        values = tile_values[0, 0]
        rounds = coords.shape[0]
        side = values.shape[-1]
        width = user_factors.shape[1]
        g = lax.axis_index("grp").astype(jnp.int32)
        place = jnp.where(g % 2 == 0, g // 2, n_grp - 1 - g // 2).reshape(1)
        users = user_factors
        slab = item_factors.reshape(n_grp, 2 * WAVES, side, width)
        slabs = [[slab] for _ in range(WAVES)]
        for sub in range(rounds):
            final = sub + 1 == rounds
            after = users
            nexts = []
            for wave in range(WAVES):
                after, near_f, near_b, far, own = tile_step(
                    sub, wave, n_grp, coords, counts, place, users, after, slabs[wave], values
                )
                if not final:
                    own = lax.ppermute(own, "strat", turn)
                parts = [near_f, near_b]
                for t in range(1, n_grp):
                    for way in range(2):
                        part = parts[way]
                        if t > 1:
                            part = part + far[way, t - 2]
                        if t + 1 == n_grp and not final:
                            parts[way] = lax.ppermute(part, ("strat", "grp"), last[way])
                        else:
                            parts[way] = lax.ppermute(part, "grp", ring[way])
                got = [[own[way] + parts[way]] for way in range(2)]
                for t in range(1, n_grp):
                    for way in range(2):
                        got[way].append(lax.ppermute(got[way][-1], "grp", ring[way]))
                nexts.append(got[0] + got[1])
            users = after
            slabs = nexts
        items = None
        for wave in range(WAVES):
            items = lay(wave, n_grp, place, slabs[wave], items)
        return users, items.reshape(item_factors.shape)

    placed = (
        P(("strat", "grp"), None),
        P("strat", None),
        P("strat", "grp", None, None, None),
        P("strat", "grp", None),
        P("strat", "grp", None, None, None, None),
    )
    return jax.shard_map(
        per_device,
        mesh=mesh,
        in_specs=placed,
        out_specs=(P(("strat", "grp"), None), P("strat", None)),
        check_vma=False,
    )
```

time: 651 us -> 458 us (0.70)
  waiting for transfers between devices: 546 us -> 75.3 us
  starting transfers between devices: 1.87 us -> 204 us
  Pallas kernels: 0 us -> 168 us
  other arithmetic: 34.9 us -> 1.42 us
  matrix products: 25.3 us -> 0 us
  local copies, waits for them, and re-layouts: 28.9 us -> 8.2 us
  between operations: 14 us -> 1.54 us
    psum x3 -> x0, waiting for transfers between devices: 465 us -> none  [per_device(): total = lax.psum(item_grad, 'grp')]
    ppermute x2 -> x172, starting transfers between devices: 1.75 us -> 204 us  [the longest x84 100 us: per_device(): got[way].append(lax.ppermute(got[way][-1], 'grp', ring[way]))]
    pallas_call x0 -> x8, Pallas kernels: none -> 168 us  [the longest x2 130 us: lay(): pl.pallas_call(functools.partial(lay_kernel, wave, n_own, len(carried)),...]
    dot_general x15 -> x0, matrix products: 25.3 us -> none  [the longest x3 8.79 us: tile_terms(): jnp.einsum('nt,nrk->trk', one_item, item_part, precision=high)]
    sub x4 -> x0, other arithmetic: 19.9 us -> none  [the longest x3 18.5 us: per_device(): slab = slab - 0.003 * (0.05 * slab - total)]
    dot_general x6 -> x0, local copies, waits for them, and re-layouts: 14.3 us -> none  [the longest x3 13.3 us: tile_terms(): jnp.einsum('nt,nrk->trk', one_item, item_part, precision=high)]
    convert_element_type x6 -> x0, other arithmetic: 12.4 us -> none  [the longest x3 9.81 us: per_device(): slab.astype(jnp.bfloat16)]
    gather x6 -> x0, local copies, waits for them, and re-layouts: 11.9 us -> none  [the longest x3 6.08 us: tile_terms(): irows = jnp.take(slab_b.reshape(item_tiles, side, width), coords[1], axis=0)]
  transfers between devices with their start and end apart: 5 -> 172, of which waited for: 5 -> 97; matrix products, arithmetic and copies ran while one was open for 3% -> 0% of each run, Pallas kernels for 0% -> 21%
where the time goes in v1:
time: 458 us
  starting transfers between devices  204 us (45%)
  Pallas kernels  168 us (37%)
  waiting for transfers between devices  75.3 us (16%)
  local copies, waits for them, and re-layouts  8.2 us (2%)
    pallas_call x2, Pallas kernels, lay(): pl.pallas_call(functools.partial(lay_kernel, wave, n_own, len(carried)),...  130 us
    ppermute x84, starting transfers between devices, per_device(): got[way].append(lax.ppermute(got[way][-1], 'grp', ring[way]))  100 us
    ppermute x76, starting transfers between devices, per_device(): parts[way] = lax.ppermute(part, 'grp', ring[way])  93.9 us
    ppermute x76, waiting for transfers between devices, per_device(): parts[way] = lax.ppermute(part, 'grp', ring[way])  47.2 us
    pallas_call x6, Pallas kernels, tile_step(): pl.pallas_call(functools.partial(tile_kernel, sub, wave, side, n_own), ou...  38.3 us
    ppermute x84, waiting for transfers between devices, per_device(): got[way].append(lax.ppermute(got[way][-1], 'grp', ring[way]))  25.4 us
  transfers between devices with their start and end apart: 172, of which 97 were waited for; matrix products, arithmetic and copies ran while one was open for 0% of the time, Pallas kernels for 21%

profile of v1, /device:TPU:0, one launch (start us, length us, event | category | flops | bytes accessed | tf_op | source)
XLA Modules:
  0.0 458.2 jit_solution(10137688712144154392)
XLA Ops:
  2.1 2.2 copy-done.2
  6.8 6.0 %tiles_0_0.1 = (f32[1024,256]{1,0:T(8,128)S(1)}, f32[128,256]{1,0:T(8,128)S(1)}, f32[128,256]{1,0:T(8,128)S(1)}, f32[2,6,128,256]{3,2,1,0:T(8,128)S(1)}, f32[2,128,256]{2,1,0:T(8,128)S(1)}) custom-call(s32[3,2,16]{2,1,0:T(2,128)S(1)} %bitcast.198, s32[3]{0:T(128)S(1)} %bitcast.204, s32[1]{0:T(128)} %bitcast.2.refs_2_.refs_0_, f32[1024,256]{1,0:T(8,128)S(1)} %copy-done.3, ...), custom_call_target="tpu_custom_call" | custom-call | flops 201326592 | bytes 8388608 | tf_op jit(solution)/shard_map/tiles_0_0/pallas_call | solution.py:100
  15.1 3.8 tiles_0_1.1
  18.8 2.6 collective-permute-start.30
  23.0 2.0 collective-permute-done.30
  29.1 1.9 collective-permute-start.31
  34.9 1.9 collective-permute-start.46
  38.2 2.1 collective-permute-start.18
  41.3 2.2 collective-permute-start.4
  44.3 1.9 collective-permute-start.33
  53.1 1.9 collective-permute-start.34
  56.3 2.2 collective-permute-start.6
  61.6 2.6 collective-permute-done.49
  66.0 2.4 collective-permute-start.36
  72.0 1.8 collective-permute-start.51
  76.0 2.3 collective-permute-start.9
  99.9 2.0 collective-permute-start.27
  102.8 1.9 collective-permute-start.56
  109.1 2.0 collective-permute-start.57
  112.7 5.5 %tiles_1_0.1 = (f32[1024,256]{1,0:T(8,128)S(1)}, f32[128,256]{1,0:T(8,128)S(1)}, f32[128,256]{1,0:T(8,128)S(1)}, f32[2,6,128,256]{3,2,1,0:T(8,128)S(1)}, f32[2,128,256]{2,1,0:T(8,128)S(1)}) custom-call(s32[3,2,16]{2,1,0:T(2,128)S(1)} %bitcast.200, s32[3]{0:T(128)S(1)} %bitcast.206, s32[1]{0:T(128)} %bitcast.2.refs_2_.refs_0_, ...), custom_call_target="tpu_custom_call" | custom-call | flops 201326592 | bytes 8388608 | tf_op jit(solution)/shard_map/tiles_1_0/pallas_call | solution.py:100
  119.7 1.9 collective-permute-start.73
  121.6 6.6 %tiles_1_1.1 = (f32[1024,256]{1,0:T(8,128)S(1)}, f32[128,256]{1,0:T(8,128)S(1)}, f32[128,256]{1,0:T(8,128)S(1)}, f32[2,6,128,256]{3,2,1,0:T(8,128)S(1)}, f32[2,128,256]{2,1,0:T(8,128)S(1)}) custom-call(s32[3,2,16]{2,1,0:T(2,128)S(1)} %bitcast.201, s32[3]{0:T(128)S(1)} %bitcast.207, s32[1]{0:T(128)} %bitcast.2.refs_2_.refs_0_, ...), custom_call_target="tpu_custom_call" | custom-call | flops 201326592 | bytes 8388608 | tf_op jit(solution)/shard_map/tiles_1_1/pallas_call | solution.py:100
  128.3 3.1 collective-permute-start.102
  131.5 2.2 collective-permute-start.58
  137.4 1.9 collective-permute-done.74
  139.3 1.9 collective-permute-start.89
  141.8 2.3 collective-permute-start.61
  144.6 1.8 collective-permute-start.104
  157.5 1.8 collective-permute-start.63
  161.8 2.4 collective-permute-start.92
  178.0 2.2 collective-permute-start.80
  180.8 2.1 collective-permute-start.109
  184.1 2.1 collective-permute-start.81
  193.4 2.2 collective-permute-start.111
  222.1 5.9 %tiles_2_0.1 = (f32[1024,256]{1,0:T(8,128)S(1)}, f32[128,256]{1,0:T(8,128)S(1)}, f32[128,256]{1,0:T(8,128)S(1)}, f32[2,6,128,256]{3,2,1,0:T(8,128)S(1)}, f32[2,128,256]{2,1,0:T(8,128)S(1)}) custom-call(s32[3,2,16]{2,1,0:T(2,128)S(1)} %bitcast.202, s32[3]{0:T(128)S(1)} %bitcast.208, s32[1]{0:T(128)} %bitcast.2.refs_2_.refs_0_, ...), custom_call_target="tpu_custom_call" | custom-call | flops 201326592 | bytes 8388608 | tf_op jit(solution)/shard_map/tiles_2_0/pallas_call | solution.py:100
  228.0 3.3 collective-permute-start.116
  231.3 10.6 %tiles_2_1.1 = (f32[1024,256]{1,0:T(8,128)}, f32[128,256]{1,0:T(8,128)S(1)}, f32[128,256]{1,0:T(8,128)S(1)}, f32[2,6,128,256]{3,2,1,0:T(8,128)S(1)}, f32[2,128,256]{2,1,0:T(8,128)S(1)}) custom-call(s32[3,2,16]{2,1,0:T(2,128)S(1)} %bitcast.203, s32[3]{0:T(128)S(1)} %bitcast.209, s32[1]{0:T(128)} %bitcast.2.refs_2_.refs_0_, ...), custom_call_target="tpu_custom_call" | custom-call | flops 201326592 | bytes 8388608 | tf_op jit(solution)/shard_map/tiles_2_1/pallas_call | solution.py:100
  242.0 2.0 collective-permute-start.158
  244.1 2.0 collective-permute-start.117
  246.1 2.1 collective-permute-done.144
  248.3 2.1 collective-permute-start.159
  254.2 2.6 collective-permute-done.145
  256.8 2.0 collective-permute-start.146
  259.6 2.0 collective-permute-start.119
  272.3 1.8 collective-permute-start.121
  275.2 1.8 collective-permute-start.149
  278.8 2.0 collective-permute-start.122
  281.8 1.8 collective-permute-start.150
  284.6 2.2 collective-permute-start.137
  289.3 1.8 collective-permute-start.165
  291.4 2.1 collective-permute-start.138
  295.0 2.5 collective-permute-start.166
  297.8 2.1 collective-permute-start.139
  300.9 2.5 collective-permute-start.167
  304.2 1.9 collective-permute-start.140
  307.1 2.5 collective-permute-start.168
  309.8 2.0 collective-permute-start.141
  312.2 2.3 collective-permute-start.169
  314.8 2.0 collective-permute-start.142
  317.1 2.3 collective-permute-start.170
  319.8 2.0 collective-permute-start.143
  322.1 2.3 collective-permute-start.171
  327.0 64.8 %lay_0.1.refs_1_ = f32[8,4,128,256]{3,2,1,0:T(8,128)} custom-call(s32[1]{0:T(128)} %bitcast.2.refs_2_.refs_0_, f32[128,256]{1,0:T(8,128)} %copy-done.9, f32[128,256]{1,0:T(8,128)} %copy-done.25, f32[128,256]{1,0:T(8,128)} %copy-done.27, f32[128,256]{1,0:T(8,128)} %copy-done.29, f32[128,256]{1,0:T(8,128)} %copy-done.31, f32[128,256]{1,0:T(8,128)} %copy-done.33, ...), custom_call_target="tpu_custom_call" | custom-call | bytes 4194304 | tf_op jit(solution)/shard_map/lay_0/pallas_call | solution.py:148
  393.3 64.8 %lay_1.1 = f32[8,4,128,256]{3,2,1,0:T(8,128)} custom-call(s32[1]{0:T(128)} %bitcast.2.refs_2_.refs_0_, f32[8,4,128,256]{3,2,1,0:T(8,128)} %lay_0.1.refs_1_, f32[128,256]{1,0:T(8,128)} %copy-done.7, f32[128,256]{1,0:T(8,128)} %copy-done.11, f32[128,256]{1,0:T(8,128)} %copy-done.13, f32[128,256]{1,0:T(8,128)} %copy-done.15, ...), custom_call_target="tpu_custom_call", output_to_operand_aliasing={{}: (1, {})} | custom-call | bytes 4194304 | tf_op jit(solution)/shard_map/lay_1/pallas_call | solution.py:148
  (404 shorter events, 168.8 us)
Async XLA Ops:
  12.8 8.6 %collective-permute-start.1 = (f32[128,256]{1,0:T(8,128)S(1)}, f32[128,256]{1,0:T(8,128)S(1)}, u32[]{:S(2)}, u32[]{:S(2)}) collective-permute-start(f32[128,256]{1,0:T(8,128)S(1)} %get-tuple-element.35), channel_id=1, source_target_pairs={{0,2},{2,4},{4,6},{6,7},{7,5},{5,3},{3,1},{1,0},{8,10},{10,12},{12... | collective-permute-start | bytes 393224 | tf_op jit(solution)/shard_map/ppermute | solution.py:208
  13.7 8.3 %collective-permute-start.15 = (f32[128,256]{1,0:T(8,128)S(1)}, f32[128,256]{1,0:T(8,128)S(1)}, u32[]{:S(2)}, u32[]{:S(2)}) collective-permute-start(f32[128,256]{1,0:T(8,128)S(1)} %get-tuple-element.37), channel_id=1, source_target_pairs={{0,1},{2,0},{4,2},{6,4},{7,6},{5,7},{3,5},{1,3},{8,9},{10,8},{12,1... | collective-permute-start | bytes 393224 | tf_op jit(solution)/shard_map/ppermute | solution.py:208
  14.9 51.1 %collective-permute-start = (f32[2,128,256]{2,1,0:T(8,128)S(1)}, f32[2,128,256]{2,1,0:T(8,128)S(1)}, u32[]{:S(2)}, u32[]{:S(2)}) collective-permute-start(f32[2,128,256]{2,1,0:T(8,128)S(1)} %get-tuple-element.34), channel_id=1, source_target_pairs={{0,24},{8,0},{16,8},{24,16},{1,25},{9,1},{17,9},{25,17},{2,26},{10... | collective-permute-start | bytes 786440 | tf_op jit(solution)/shard_map/ppermute | solution.py:198
  21.4 50.5 %collective-permute-start.29 = (f32[2,128,256]{2,1,0:T(8,128)S(1)}, f32[2,128,256]{2,1,0:T(8,128)S(1)}, u32[]{:S(2)}, u32[]{:S(2)}) collective-permute-start(f32[2,128,256]{2,1,0:T(8,128)S(1)} %get-tuple-element.39), channel_id=1, source_target_pairs={{0,24},{8,0},{16,8},{24,16},{1,25},{9,1},{17,9},{25,17},{2,26},{10... | collective-permute-start | bytes 786440 | tf_op jit(solution)/shard_map/ppermute | solution.py:198
  22.0 7.1 %collective-permute-start.16 = (f32[128,256]{1,0:T(8,128)S(1)}, f32[128,256]{1,0:T(8,128)S(1)}, u32[]{:S(2)}, u32[]{:S(2)}) collective-permute-start(f32[128,256]{1,0:T(8,128)S(1)} %get-tuple-element.132), channel_id=1, source_target_pairs={{0,1},{2,0},{4,2},{6,4},{7,6},{5,7},{3,5},{1,3},{8,9},{10,8},{12,1... | collective-permute-start | bytes 393224 | tf_op jit(solution)/shard_map/ppermute | solution.py:208
  34.9 6.4 %collective-permute-start.46 = (f32[128,256]{1,0:T(8,128)S(1)}, f32[128,256]{1,0:T(8,128)S(1)}, u32[]{:S(2)}, u32[]{:S(2)}) collective-permute-start(f32[128,256]{1,0:T(8,128)S(1)} %get-tuple-element.118), channel_id=1, source_target_pairs={{0,1},{2,0},{4,2},{6,4},{7,6},{5,7},{3,5},{1,3},{8,9},{10,8},{12,1... | collective-permute-start | bytes 393224 | tf_op jit(solution)/shard_map/ppermute | solution.py:208
  36.8 6.8 %collective-permute-start.32 = (f32[128,256]{1,0:T(8,128)S(1)}, f32[128,256]{1,0:T(8,128)S(1)}, u32[]{:S(2)}, u32[]{:S(2)}) collective-permute-start(f32[128,256]{1,0:T(8,128)S(1)} %get-tuple-element.119), channel_id=1, source_target_pairs={{0,2},{2,4},{4,6},{6,7},{7,5},{5,3},{3,1},{1,0},{8,10},{10,12},{12... | collective-permute-start | bytes 393224 | tf_op jit(solution)/shard_map/ppermute | solution.py:208
  44.3 6.7 %collective-permute-start.33 = (f32[128,256]{1,0:T(8,128)S(1)}, f32[128,256]{1,0:T(8,128)S(1)}, u32[]{:S(2)}, u32[]{:S(2)}) collective-permute-start(f32[128,256]{1,0:T(8,128)S(1)} %get-tuple-element.117), channel_id=1, source_target_pairs={{0,2},{2,4},{4,6},{6,7},{7,5},{5,3},{3,1},{1,0},{8,10},{10,12},{12... | collective-permute-start | bytes 393224 | tf_op jit(solution)/shard_map/ppermute | solution.py:208
  61.5 6.9 %collective-permute-start.21 = (f32[128,256]{1,0:T(8,128)S(1)}, f32[128,256]{1,0:T(8,128)S(1)}, u32[]{:S(2)}, u32[]{:S(2)}) collective-permute-start(f32[128,256]{1,0:T(8,128)S(1)} %get-tuple-element.122), channel_id=1, source_target_pairs={{0,25},{2,24},{4,26},{6,28},{7,30},{5,31},{3,29},{1,27},{8,1},{10,... | collective-permute-start | bytes 393224 | tf_op jit(solution)/shard_map/ppermute | solution.py:206
  65.1 6.8 %collective-permute-start.50 = (f32[128,256]{1,0:T(8,128)S(1)}, f32[128,256]{1,0:T(8,128)S(1)}, u32[]{:S(2)}, u32[]{:S(2)}) collective-permute-start(f32[128,256]{1,0:T(8,128)S(1)} %get-tuple-element.110), channel_id=1, source_target_pairs={{0,25},{2,24},{4,26},{6,28},{7,30},{5,31},{3,29},{1,27},{8,1},{10,... | collective-permute-start | bytes 393224 | tf_op jit(solution)/shard_map/ppermute | solution.py:206
  76.0 6.9 %collective-permute-start.9 = (f32[128,256]{1,0:T(8,128)S(1)}, f32[128,256]{1,0:T(8,128)S(1)}, u32[]{:S(2)}, u32[]{:S(2)}) collective-permute-start(f32[128,256]{1,0:T(8,128)S(1)} %collective-permute-done.8.refs_6_), channel_id=1, source_target_pairs={{0,2},{2,4},{4,6},{6,7},{7,5},{5,3},{3,1},{1,0},{8,10},{10,12},{12... | collective-permute-start | bytes 393224 | tf_op jit(solution)/shard_map/ppermute | solution.py:212
  89.1 6.4 %collective-permute-start.11 = (f32[128,256]{1,0:T(8,128)S(1)}, f32[128,256]{1,0:T(8,128)S(1)}, u32[]{:S(2)}, u32[]{:S(2)}) collective-permute-start(f32[128,256]{1,0:T(8,128)S(1)} %collective-permute-done.10.refs_8_), channel_id=1, source_target_pairs={{0,2},{2,4},{4,6},{6,7},{7,5},{5,3},{3,1},{1,0},{8,10},{10,12},{12... | collective-permute-start | bytes 393224 | tf_op jit(solution)/shard_map/ppermute | solution.py:212
  91.9 6.4 %collective-permute-start.40 = (f32[128,256]{1,0:T(8,128)S(1)}, f32[128,256]{1,0:T(8,128)S(1)}, u32[]{:S(2)}, u32[]{:S(2)}) collective-permute-start(f32[128,256]{1,0:T(8,128)S(1)} %collective-permute-done.39.refs_8_), channel_id=1, source_target_pairs={{0,2},{2,4},{4,6},{6,7},{7,5},{5,3},{3,1},{1,0},{8,10},{10,12},{12... | collective-permute-start | bytes 393224 | tf_op jit(solution)/shard_map/ppermute | solution.py:212
  95.5 6.4 %collective-permute-start.12 = (f32[128,256]{1,0:T(8,128)S(1)}, f32[128,256]{1,0:T(8,128)S(1)}, u32[]{:S(2)}, u32[]{:S(2)}) collective-permute-start(f32[128,256]{1,0:T(8,128)S(1)} %collective-permute-done.11.refs_9_), channel_id=1, source_target_pairs={{0,2},{2,4},{4,6},{6,7},{7,5},{5,3},{3,1},{1,0},{8,10},{10,12},{12... | collective-permute-start | bytes 393224 | tf_op jit(solution)/shard_map/ppermute | solution.py:212
  98.3 6.4 %collective-permute-start.41 = (f32[128,256]{1,0:T(8,128)S(1)}, f32[128,256]{1,0:T(8,128)S(1)}, u32[]{:S(2)}, u32[]{:S(2)}) collective-permute-start(f32[128,256]{1,0:T(8,128)S(1)} %collective-permute-done.40.refs_9_), channel_id=1, source_target_pairs={{0,2},{2,4},{4,6},{6,7},{7,5},{5,3},{3,1},{1,0},{8,10},{10,12},{12... | collective-permute-start | bytes 393224 | tf_op jit(solution)/shard_map/ppermute | solution.py:212
  104.8 6.4 %collective-permute-start.42 = (f32[128,256]{1,0:T(8,128)S(1)}, f32[128,256]{1,0:T(8,128)S(1)}, u32[]{:S(2)}, u32[]{:S(2)}) collective-permute-start(f32[128,256]{1,0:T(8,128)S(1)} %collective-permute-done.41.refs_10_), channel_id=1, source_target_pairs={{0,2},{2,4},{4,6},{6,7},{7,5},{5,3},{3,1},{1,0},{8,10},{10,12},{12... | collective-permute-start | bytes 393224 | tf_op jit(solution)/shard_map/ppermute | solution.py:212
  109.1 12.5 %collective-permute-start.57 = (f32[128,256]{1,0:T(8,128)S(1)}, f32[128,256]{1,0:T(8,128)S(1)}, u32[]{:S(2)}, u32[]{:S(2)}) collective-permute-start(f32[128,256]{1,0:T(8,128)S(1)} %collective-permute-done.56.refs_19_), channel_id=1, source_target_pairs={{0,1},{2,0},{4,2},{6,4},{7,6},{5,7},{3,5},{1,3},{8,9},{10,8},{12,1... | collective-permute-start | bytes 393224 | tf_op jit(solution)/shard_map/ppermute | solution.py:212
  111.2 10.4 %collective-permute-start.43 = (f32[128,256]{1,0:T(8,128)S(1)}, f32[128,256]{1,0:T(8,128)S(1)}, u32[]{:S(2)}, u32[]{:S(2)}) collective-permute-start(f32[128,256]{1,0:T(8,128)S(1)} %collective-permute-done.42.refs_11_), channel_id=1, source_target_pairs={{0,2},{2,4},{4,6},{6,7},{7,5},{5,3},{3,1},{1,0},{8,10},{10,12},{12... | collective-permute-start | bytes 393224 | tf_op jit(solution)/shard_map/ppermute | solution.py:212
  118.2 13.3 %collective-permute-start.59 = (f32[128,256]{1,0:T(8,128)S(1)}, f32[128,256]{1,0:T(8,128)S(1)}, u32[]{:S(2)}, u32[]{:S(2)}) collective-permute-start(f32[128,256]{1,0:T(8,128)S(1)} %get-tuple-element.45), channel_id=1, source_target_pairs={{0,2},{2,4},{4,6},{6,7},{7,5},{5,3},{3,1},{1,0},{8,10},{10,12},{12... | collective-permute-start | bytes 393224 | tf_op jit(solution)/shard_map/ppermute | solution.py:208
  119.7 13.9 %collective-permute-start.73 = (f32[128,256]{1,0:T(8,128)S(1)}, f32[128,256]{1,0:T(8,128)S(1)}, u32[]{:S(2)}, u32[]{:S(2)}) collective-permute-start(f32[128,256]{1,0:T(8,128)S(1)} %get-tuple-element.47), channel_id=1, source_target_pairs={{0,1},{2,0},{4,2},{6,4},{7,6},{5,7},{3,5},{1,3},{8,9},{10,8},{12,1... | collective-permute-start | bytes 393224 | tf_op jit(solution)/shard_map/ppermute | solution.py:208
  128.3 7.4 %collective-permute-start.102 = (f32[128,256]{1,0:T(8,128)S(1)}, f32[128,256]{1,0:T(8,128)S(1)}, u32[]{:S(2)}, u32[]{:S(2)}) collective-permute-start(f32[128,256]{1,0:T(8,128)S(1)} %get-tuple-element.52), channel_id=1, source_target_pairs={{0,1},{2,0},{4,2},{6,4},{7,6},{5,7},{3,5},{1,3},{8,9},{10,8},{12,1... | collective-permute-start | bytes 393224 | tf_op jit(solution)/shard_map/ppermute | solution.py:208
  131.4 49.4 %collective-permute-start.87 = (f32[2,128,256]{2,1,0:T(8,128)S(1)}, f32[2,128,256]{2,1,0:T(8,128)S(1)}, u32[]{:S(2)}, u32[]{:S(2)}) collective-permute-start(f32[2,128,256]{2,1,0:T(8,128)S(1)} %get-tuple-element.49), channel_id=1, source_target_pairs={{0,24},{8,0},{16,8},{24,16},{1,25},{9,1},{17,9},{25,17},{2,26},{10... | collective-permute-start | bytes 786440 | tf_op jit(solution)/shard_map/ppermute | solution.py:198
  131.5 44.0 %collective-permute-start.58 = (f32[2,128,256]{2,1,0:T(8,128)S(1)}, f32[2,128,256]{2,1,0:T(8,128)S(1)}, u32[]{:S(2)}, u32[]{:S(2)}) collective-permute-start(f32[2,128,256]{2,1,0:T(8,128)S(1)} %get-tuple-element.44), channel_id=1, source_target_pairs={{0,24},{8,0},{16,8},{24,16},{1,25},{9,1},{17,9},{25,17},{2,26},{10... | collective-permute-start | bytes 786440 | tf_op jit(solution)/shard_map/ppermute | solution.py:198
  134.3 6.8 %collective-permute-start.60 = (f32[128,256]{1,0:T(8,128)S(1)}, f32[128,256]{1,0:T(8,128)S(1)}, u32[]{:S(2)}, u32[]{:S(2)}) collective-permute-start(f32[128,256]{1,0:T(8,128)S(1)} %get-tuple-element.109), channel_id=1, source_target_pairs={{0,2},{2,4},{4,6},{6,7},{7,5},{5,3},{3,1},{1,0},{8,10},{10,12},{12... | collective-permute-start | bytes 393224 | tf_op jit(solution)/shard_map/ppermute | solution.py:208
  141.8 6.6 %collective-permute-start.61 = (f32[128,256]{1,0:T(8,128)S(1)}, f32[128,256]{1,0:T(8,128)S(1)}, u32[]{:S(2)}, u32[]{:S(2)}) collective-permute-start(f32[128,256]{1,0:T(8,128)S(1)} %get-tuple-element.107), channel_id=1, source_target_pairs={{0,2},{2,4},{4,6},{6,7},{7,5},{5,3},{3,1},{1,0},{8,10},{10,12},{12... | collective-permute-start | bytes 393224 | tf_op jit(solution)/shard_map/ppermute | solution.py:208
  157.5 6.7 %collective-permute-start.63 = (f32[128,256]{1,0:T(8,128)S(1)}, f32[128,256]{1,0:T(8,128)S(1)}, u32[]{:S(2)}, u32[]{:S(2)}) collective-permute-start(f32[128,256]{1,0:T(8,128)S(1)} %get-tuple-element.103), channel_id=1, source_target_pairs={{0,2},{2,4},{4,6},{6,7},{7,5},{5,3},{3,1},{1,0},{8,10},{10,12},{12... | collective-permute-start | bytes 393224 | tf_op jit(solution)/shard_map/ppermute | solution.py:208
  174.5 6.3 %collective-permute-start.108 = (f32[128,256]{1,0:T(8,128)S(1)}, f32[128,256]{1,0:T(8,128)S(1)}, u32[]{:S(2)}, u32[]{:S(2)}) collective-permute-start(f32[128,256]{1,0:T(8,128)S(1)} %get-tuple-element.86), channel_id=1, source_target_pairs={{0,25},{2,24},{4,26},{6,28},{7,30},{5,31},{3,29},{1,27},{8,1},{10,... | collective-permute-start | bytes 393224 | tf_op jit(solution)/shard_map/ppermute | solution.py:206
  180.8 6.8 %collective-permute-start.109 = (f32[128,256]{1,0:T(8,128)S(1)}, f32[128,256]{1,0:T(8,128)S(1)}, u32[]{:S(2)}, u32[]{:S(2)}) collective-permute-start(f32[128,256]{1,0:T(8,128)S(1)} %get-tuple-element.138.refs_13_), channel_id=1, source_target_pairs={{0,1},{2,0},{4,2},{6,4},{7,6},{5,7},{3,5},{1,3},{8,9},{10,8},{12,1... | collective-permute-start | bytes 393224 | tf_op jit(solution)/shard_map/ppermute | solution.py:212
  182.9 6.4 %collective-permute-start.95 = (f32[128,256]{1,0:T(8,128)S(1)}, f32[128,256]{1,0:T(8,128)S(1)}, u32[]{:S(2)}, u32[]{:S(2)}) collective-permute-start(f32[128,256]{1,0:T(8,128)S(1)} %get-tuple-element.139.refs_5_), channel_id=1, source_target_pairs={{0,2},{2,4},{4,6},{6,7},{7,5},{5,3},{3,1},{1,0},{8,10},{10,12},{12... | collective-permute-start | bytes 393224 | tf_op jit(solution)/shard_map/ppermute | solution.py:212
  184.1 6.4 %collective-permute-start.81 = (f32[128,256]{1,0:T(8,128)S(1)}, f32[128,256]{1,0:T(8,128)S(1)}, u32[]{:S(2)}, u32[]{:S(2)}) collective-permute-start(f32[128,256]{1,0:T(8,128)S(1)} %collective-permute-done.80.refs_14_), channel_id=1, source_target_pairs={{0,1},{2,0},{4,2},{6,4},{7,6},{5,7},{3,5},{1,3},{8,9},{10,8},{12,1... | collective-permute-start | bytes 393224 | tf_op jit(solution)/shard_map/ppermute | solution.py:212
  189.3 6.4 %collective-permute-start.96 = (f32[128,256]{1,0:T(8,128)S(1)}, f32[128,256]{1,0:T(8,128)S(1)}, u32[]{:S(2)}, u32[]{:S(2)}) collective-permute-start(f32[128,256]{1,0:T(8,128)S(1)} %collective-permute-done.95.refs_6_), channel_id=1, source_target_pairs={{0,2},{2,4},{4,6},{6,7},{7,5},{5,3},{3,1},{1,0},{8,10},{10,12},{12... | collective-permute-start | bytes 393224 | tf_op jit(solution)/shard_map/ppermute | solution.py:212
  190.5 6.4 %collective-permute-start.82 = (f32[128,256]{1,0:T(8,128)S(1)}, f32[128,256]{1,0:T(8,128)S(1)}, u32[]{:S(2)}, u32[]{:S(2)}) collective-permute-start(f32[128,256]{1,0:T(8,128)S(1)} %collective-permute-done.81.refs_15_), channel_id=1, source_target_pairs={{0,1},{2,0},{4,2},{6,4},{7,6},{5,7},{3,5},{1,3},{8,9},{10,8},{12,1... | collective-permute-start | bytes 393224 | tf_op jit(solution)/shard_map/ppermute | solution.py:212
  192.2 6.3 %collective-permute-start.68 = (f32[128,256]{1,0:T(8,128)S(1)}, f32[128,256]{1,0:T(8,128)S(1)}, u32[]{:S(2)}, u32[]{:S(2)}) collective-permute-start(f32[128,256]{1,0:T(8,128)S(1)} %collective-permute-done.67.refs_7_), channel_id=1, source_target_pairs={{0,2},{2,4},{4,6},{6,7},{7,5},{5,3},{3,1},{1,0},{8,10},{10,12},{12... | collective-permute-start | bytes 393224 | tf_op jit(solution)/shard_map/ppermute | solution.py:212
  193.4 7.1 %collective-permute-start.111 = (f32[128,256]{1,0:T(8,128)S(1)}, f32[128,256]{1,0:T(8,128)S(1)}, u32[]{:S(2)}, u32[]{:S(2)}) collective-permute-start(f32[128,256]{1,0:T(8,128)S(1)} %collective-permute-done.110.refs_15_), channel_id=1, source_target_pairs={{0,1},{2,0},{4,2},{6,4},{7,6},{5,7},{3,5},{1,3},{8,9},{10,8},{12,1... | collective-permute-start | bytes 393224 | tf_op jit(solution)/shard_map/ppermute | solution.py:212
  196.9 6.3 %collective-permute-start.83 = (f32[128,256]{1,0:T(8,128)S(1)}, f32[128,256]{1,0:T(8,128)S(1)}, u32[]{:S(2)}, u32[]{:S(2)}) collective-permute-start(f32[128,256]{1,0:T(8,128)S(1)} %collective-permute-done.82.refs_16_), channel_id=1, source_target_pairs={{0,1},{2,0},{4,2},{6,4},{7,6},{5,7},{3,5},{1,3},{8,9},{10,8},{12,1... | collective-permute-start | bytes 393224 | tf_op jit(solution)/shard_map/ppermute | solution.py:212
  201.5 6.3 %collective-permute-start.98 = (f32[128,256]{1,0:T(8,128)S(1)}, f32[128,256]{1,0:T(8,128)S(1)}, u32[]{:S(2)}, u32[]{:S(2)}) collective-permute-start(f32[128,256]{1,0:T(8,128)S(1)} %collective-permute-done.97.refs_8_), channel_id=1, source_target_pairs={{0,2},{2,4},{4,6},{6,7},{7,5},{5,3},{3,1},{1,0},{8,10},{10,12},{12... | collective-permute-start | bytes 393224 | tf_op jit(solution)/shard_map/ppermute | solution.py:212
  203.3 6.5 %collective-permute-start.84 = (f32[128,256]{1,0:T(8,128)S(1)}, f32[128,256]{1,0:T(8,128)S(1)}, u32[]{:S(2)}, u32[]{:S(2)}) collective-permute-start(f32[128,256]{1,0:T(8,128)S(1)} %collective-permute-done.83.refs_17_), channel_id=1, source_target_pairs={{0,1},{2,0},{4,2},{6,4},{7,6},{5,7},{3,5},{1,3},{8,9},{10,8},{12,1... | collective-permute-start | bytes 393224 | tf_op jit(solution)/shard_map/ppermute | solution.py:212
  204.8 6.3 %collective-permute-start.70 = (f32[128,256]{1,0:T(8,128)S(1)}, f32[128,256]{1,0:T(8,128)S(1)}, u32[]{:S(2)}, u32[]{:S(2)}) collective-permute-start(f32[128,256]{1,0:T(8,128)S(1)} %collective-permute-done.69.refs_9_), channel_id=1, source_target_pairs={{0,2},{2,4},{4,6},{6,7},{7,5},{5,3},{3,1},{1,0},{8,10},{10,12},{12... | collective-permute-start | bytes 393224 | tf_op jit(solution)/shard_map/ppermute | solution.py:212
  206.2 6.4 %collective-permute-start.113 = (f32[128,256]{1,0:T(8,128)S(1)}, f32[128,256]{1,0:T(8,128)S(1)}, u32[]{:S(2)}, u32[]{:S(2)}) collective-permute-start(f32[128,256]{1,0:T(8,128)S(1)} %collective-permute-done.112.refs_17_), channel_id=1, source_target_pairs={{0,1},{2,0},{4,2},{6,4},{7,6},{5,7},{3,5},{1,3},{8,9},{10,8},{12,1... | collective-permute-start | bytes 393224 | tf_op jit(solution)/shard_map/ppermute | solution.py:212
  209.7 6.4 %collective-permute-start.85 = (f32[128,256]{1,0:T(8,128)S(1)}, f32[128,256]{1,0:T(8,128)S(1)}, u32[]{:S(2)}, u32[]{:S(2)}) collective-permute-start(f32[128,256]{1,0:T(8,128)S(1)} %collective-permute-done.84.refs_18_), channel_id=1, source_target_pairs={{0,1},{2,0},{4,2},{6,4},{7,6},{5,7},{3,5},{1,3},{8,9},{10,8},{12,1... | collective-permute-start | bytes 393224 | tf_op jit(solution)/shard_map/ppermute | solution.py:212
  218.7 12.6 %collective-permute-start.115 = (f32[128,256]{1,0:T(8,128)S(1)}, f32[128,256]{1,0:T(8,128)S(1)}, u32[]{:S(2)}, u32[]{:S(2)}) collective-permute-start(f32[128,256]{1,0:T(8,128)S(1)} %collective-permute-done.114.refs_19_), channel_id=1, source_target_pairs={{0,1},{2,0},{4,2},{6,4},{7,6},{5,7},{3,5},{1,3},{8,9},{10,8},{12,1... | collective-permute-start | bytes 393224 | tf_op jit(solution)/shard_map/ppermute | solution.py:212
  219.6 11.7 %collective-permute-start.101 = (f32[128,256]{1,0:T(8,128)S(1)}, f32[128,256]{1,0:T(8,128)S(1)}, u32[]{:S(2)}, u32[]{:S(2)}) collective-permute-start(f32[128,256]{1,0:T(8,128)S(1)} %collective-permute-done.100.refs_11_), channel_id=1, source_target_pairs={{0,2},{2,4},{4,6},{6,7},{7,5},{5,3},{3,1},{1,0},{8,10},{10,12},{12... | collective-permute-start | bytes 393224 | tf_op jit(solution)/shard_map/ppermute | solution.py:212
  228.0 16.0 %collective-permute-start.116 = (f32[128,256]{1,0:T(8,128)S(1)}, f32[128,256]{1,0:T(8,128)S(1)}, u32[]{:S(2)}, u32[]{:S(2)}) collective-permute-start(f32[128,256]{1,0:T(8,128)S(1)} %get-tuple-element.55), channel_id=1, source_target_pairs={{0,2},{2,4},{4,6},{6,7},{7,5},{5,3},{3,1},{1,0},{8,10},{10,12},{12... | collective-permute-start | bytes 393224 | tf_op jit(solution)/shard_map/ppermute | solution.py:208
  231.3 12.7 %collective-permute-start.130 = (f32[128,256]{1,0:T(8,128)S(1)}, f32[128,256]{1,0:T(8,128)S(1)}, u32[]{:S(2)}, u32[]{:S(2)}) collective-permute-start(f32[128,256]{1,0:T(8,128)S(1)} %get-tuple-element.57), channel_id=1, source_target_pairs={{0,1},{2,0},{4,2},{6,4},{7,6},{5,7},{3,5},{1,3},{8,9},{10,8},{12,1... | collective-permute-start | bytes 393224 | tf_op jit(solution)/shard_map/ppermute | solution.py:208
  244.0 6.3 %collective-permute-start.131 = (f32[128,256]{1,0:T(8,128)S(1)}, f32[128,256]{1,0:T(8,128)S(1)}, u32[]{:S(2)}, u32[]{:S(2)}) collective-permute-start(f32[128,256]{1,0:T(8,128)S(1)} %get-tuple-element.84), channel_id=1, source_target_pairs={{0,1},{2,0},{4,2},{6,4},{7,6},{5,7},{3,5},{1,3},{8,9},{10,8},{12,1... | collective-permute-start | bytes 393224 | tf_op jit(solution)/shard_map/ppermute | solution.py:208
  244.1 6.9 %collective-permute-start.117 = (f32[128,256]{1,0:T(8,128)S(1)}, f32[128,256]{1,0:T(8,128)S(1)}, u32[]{:S(2)}, u32[]{:S(2)}) collective-permute-start(f32[128,256]{1,0:T(8,128)S(1)} %get-tuple-element.85), channel_id=1, source_target_pairs={{0,2},{2,4},{4,6},{6,7},{7,5},{5,3},{3,1},{1,0},{8,10},{10,12},{12... | collective-permute-start | bytes 393224 | tf_op jit(solution)/shard_map/ppermute | solution.py:208
  250.4 6.4 %collective-permute-start.145 = (f32[128,256]{1,0:T(8,128)S(1)}, f32[128,256]{1,0:T(8,128)S(1)}, u32[]{:S(2)}, u32[]{:S(2)}) collective-permute-start(f32[128,256]{1,0:T(8,128)S(1)} %get-tuple-element.73), channel_id=1, source_target_pairs={{0,2},{2,4},{4,6},{6,7},{7,5},{5,3},{3,1},{1,0},{8,10},{10,12},{12... | collective-permute-start | bytes 393224 | tf_op jit(solution)/shard_map/ppermute | solution.py:208
  251.1 7.8 %collective-permute-start.132 = (f32[128,256]{1,0:T(8,128)S(1)}, f32[128,256]{1,0:T(8,128)S(1)}, u32[]{:S(2)}, u32[]{:S(2)}) collective-permute-start(f32[128,256]{1,0:T(8,128)S(1)} %get-tuple-element.82), channel_id=1, source_target_pairs={{0,1},{2,0},{4,2},{6,4},{7,6},{5,7},{3,5},{1,3},{8,9},{10,8},{12,1... | collective-permute-start | bytes 393224 | tf_op jit(solution)/shard_map/ppermute | solution.py:208
  252.5 7.0 %collective-permute-start.118 = (f32[128,256]{1,0:T(8,128)S(1)}, f32[128,256]{1,0:T(8,128)S(1)}, u32[]{:S(2)}, u32[]{:S(2)}) collective-permute-start(f32[128,256]{1,0:T(8,128)S(1)} %get-tuple-element.83), channel_id=1, source_target_pairs={{0,2},{2,4},{4,6},{6,7},{7,5},{5,3},{3,1},{1,0},{8,10},{10,12},{12... | collective-permute-start | bytes 393224 | tf_op jit(solution)/shard_map/ppermute | solution.py:208
  272.0 6.4 %collective-permute-start.135 = (f32[128,256]{1,0:T(8,128)S(1)}, f32[128,256]{1,0:T(8,128)S(1)}, u32[]{:S(2)}, u32[]{:S(2)}) collective-permute-start(f32[128,256]{1,0:T(8,128)S(1)} %get-tuple-element.76), channel_id=1, source_target_pairs={{0,1},{2,0},{4,2},{6,4},{7,6},{5,7},{3,5},{1,3},{8,9},{10,8},{12,1... | collective-permute-start | bytes 393224 | tf_op jit(solution)/shard_map/ppermute | solution.py:208
  272.3 6.4 %collective-permute-start.121 = (f32[128,256]{1,0:T(8,128)S(1)}, f32[128,256]{1,0:T(8,128)S(1)}, u32[]{:S(2)}, u32[]{:S(2)}) collective-permute-start(f32[128,256]{1,0:T(8,128)S(1)} %get-tuple-element.77), channel_id=1, source_target_pairs={{0,2},{2,4},{4,6},{6,7},{7,5},{5,3},{3,1},{1,0},{8,10},{10,12},{12... | collective-permute-start | bytes 393224 | tf_op jit(solution)/shard_map/ppermute | solution.py:208
  274.9 6.3 %collective-permute-start.163 = (f32[128,256]{1,0:T(8,128)S(1)}, f32[128,256]{1,0:T(8,128)S(1)}, u32[]{:S(2)}, u32[]{:S(2)}) collective-permute-start(f32[128,256]{1,0:T(8,128)S(1)} %get-tuple-element.64), channel_id=1, source_target_pairs={{0,1},{2,0},{4,2},{6,4},{7,6},{5,7},{3,5},{1,3},{8,9},{10,8},{12,1... | collective-permute-start | bytes 393224 | tf_op jit(solution)/shard_map/ppermute | solution.py:208
  281.5 6.5 %collective-permute-start.164 = (f32[128,256]{1,0:T(8,128)S(1)}, f32[128,256]{1,0:T(8,128)S(1)}, u32[]{:S(2)}, u32[]{:S(2)}) collective-permute-start(f32[128,256]{1,0:T(8,128)S(1)} %get-tuple-element.62), channel_id=1, source_target_pairs={{0,1},{2,0},{4,2},{6,4},{7,6},{5,7},{3,5},{1,3},{8,9},{10,8},{12,1... | collective-permute-start | bytes 393224 | tf_op jit(solution)/shard_map/ppermute | solution.py:208
  281.8 7.4 %collective-permute-start.150 = (f32[128,256]{1,0:T(8,128)S(1)}, f32[128,256]{1,0:T(8,128)S(1)}, u32[]{:S(2)}, u32[]{:S(2)}) collective-permute-start(f32[128,256]{1,0:T(8,128)S(1)} %get-tuple-element.63), channel_id=1, source_target_pairs={{0,2},{2,4},{4,6},{6,7},{7,5},{5,3},{3,1},{1,0},{8,10},{10,12},{12... | collective-permute-start | bytes 393224 | tf_op jit(solution)/shard_map/ppermute | solution.py:208
  284.6 6.8 %collective-permute-start.137 = (f32[128,256]{1,0:T(8,128)S(1)}, f32[128,256]{1,0:T(8,128)S(1)}, u32[]{:S(2)}, u32[]{:S(2)}) collective-permute-start(f32[128,256]{1,0:T(8,128)S(1)} %get-tuple-element.136.refs_9_), channel_id=1, source_target_pairs={{0,1},{2,0},{4,2},{6,4},{7,6},{5,7},{3,5},{1,3},{8,9},{10,8},{12,1... | collective-permute-start | bytes 393224 | tf_op jit(solution)/shard_map/ppermute | solution.py:212
  286.8 6.7 %collective-permute-start.123 = (f32[128,256]{1,0:T(8,128)S(1)}, f32[128,256]{1,0:T(8,128)S(1)}, u32[]{:S(2)}, u32[]{:S(2)}) collective-permute-start(f32[128,256]{1,0:T(8,128)S(1)} %get-tuple-element.137.refs_1_), channel_id=1, source_target_pairs={{0,2},{2,4},{4,6},{6,7},{7,5},{5,3},{3,1},{1,0},{8,10},{10,12},{12... | collective-permute-start | bytes 393224 | tf_op jit(solution)/shard_map/ppermute | solution.py:212
  291.2 6.3 %collective-permute-start.151 = (f32[128,256]{1,0:T(8,128)S(1)}, f32[128,256]{1,0:T(8,128)S(1)}, u32[]{:S(2)}, u32[]{:S(2)}) collective-permute-start(f32[128,256]{1,0:T(8,128)S(1)} %get-tuple-element.135.refs_2_), channel_id=1, source_target_pairs={{0,2},{2,4},{4,6},{6,7},{7,5},{5,3},{3,1},{1,0},{8,10},{10,12},{12... | collective-permute-start | bytes 393224 | tf_op jit(solution)/shard_map/ppermute | solution.py:212
  291.4 6.4 %collective-permute-start.138 = (f32[128,256]{1,0:T(8,128)S(1)}, f32[128,256]{1,0:T(8,128)S(1)}, u32[]{:S(2)}, u32[]{:S(2)}) collective-permute-start(f32[128,256]{1,0:T(8,128)S(1)} %collective-permute-done.137.refs_10_), channel_id=1, source_target_pairs={{0,1},{2,0},{4,2},{6,4},{7,6},{5,7},{3,5},{1,3},{8,9},{10,8},{12,1... | collective-permute-start | bytes 393224 | tf_op jit(solution)/shard_map/ppermute | solution.py:212
  293.5 6.4 %collective-permute-start.124 = (f32[128,256]{1,0:T(8,128)S(1)}, f32[128,256]{1,0:T(8,128)S(1)}, u32[]{:S(2)}, u32[]{:S(2)}) collective-permute-start(f32[128,256]{1,0:T(8,128)S(1)} %collective-permute-done.123.refs_2_), channel_id=1, source_target_pairs={{0,2},{2,4},{4,6},{6,7},{7,5},{5,3},{3,1},{1,0},{8,10},{10,12},{12... | collective-permute-start | bytes 393224 | tf_op jit(solution)/shard_map/ppermute | solution.py:212
  297.5 6.6 %collective-permute-start.152 = (f32[128,256]{1,0:T(8,128)S(1)}, f32[128,256]{1,0:T(8,128)S(1)}, u32[]{:S(2)}, u32[]{:S(2)}) collective-permute-start(f32[128,256]{1,0:T(8,128)S(1)} %collective-permute-done.151.refs_3_), channel_id=1, source_target_pairs={{0,2},{2,4},{4,6},{6,7},{7,5},{5,3},{3,1},{1,0},{8,10},{10,12},{12... | collective-permute-start | bytes 393224 | tf_op jit(solution)/shard_map/ppermute | solution.py:212
  297.8 6.4 %collective-permute-start.139 = (f32[128,256]{1,0:T(8,128)S(1)}, f32[128,256]{1,0:T(8,128)S(1)}, u32[]{:S(2)}, u32[]{:S(2)}) collective-permute-start(f32[128,256]{1,0:T(8,128)S(1)} %collective-permute-done.138.refs_11_), channel_id=1, source_target_pairs={{0,1},{2,0},{4,2},{6,4},{7,6},{5,7},{3,5},{1,3},{8,9},{10,8},{12,1... | collective-permute-start | bytes 393224 | tf_op jit(solution)/shard_map/ppermute | solution.py:212
  299.9 7.1 %collective-permute-start.125 = (f32[128,256]{1,0:T(8,128)S(1)}, f32[128,256]{1,0:T(8,128)S(1)}, u32[]{:S(2)}, u32[]{:S(2)}) collective-permute-start(f32[128,256]{1,0:T(8,128)S(1)} %collective-permute-done.124.refs_3_), channel_id=1, source_target_pairs={{0,2},{2,4},{4,6},{6,7},{7,5},{5,3},{3,1},{1,0},{8,10},{10,12},{12... | collective-permute-start | bytes 393224 | tf_op jit(solution)/shard_map/ppermute | solution.py:212
  322.1 69.8 %collective-permute-start.171 = (f32[128,256]{1,0:T(8,128)S(1)}, f32[128,256]{1,0:T(8,128)S(1)}, u32[]{:S(2)}, u32[]{:S(2)}) collective-permute-start(f32[128,256]{1,0:T(8,128)S(1)} %collective-permute-done.170.refs_16_), channel_id=1, source_target_pairs={{0,1},{2,0},{4,2},{6,4},{7,6},{5,7},{3,5},{1,3},{8,9},{10,8},{12,1... | collective-permute-start | bytes 393224 | tf_op jit(solution)/shard_map/ppermute | solution.py:212
  324.7 67.3 %collective-permute-start.157 = (f32[128,256]{1,0:T(8,128)S(1)}, f32[128,256]{1,0:T(8,128)S(1)}, u32[]{:S(2)}, u32[]{:S(2)}) collective-permute-start(f32[128,256]{1,0:T(8,128)S(1)} %collective-permute-done.156.refs_8_), channel_id=1, source_target_pairs={{0,2},{2,4},{4,6},{6,7},{7,5},{5,3},{3,1},{1,0},{8,10},{10,12},{12... | collective-permute-start | bytes 393224 | tf_op jit(solution)/shard_map/ppermute | solution.py:212
  (145 other events, 2167.1 us)

commit v2 on v1

--- a/solution.py
+++ b/solution.py
@@ -20,7 +20,7 @@
     n_v = 1 if fresh else 2 * n_own
     coords, counts, place, users, running = refs[:5]
     slabs = refs[5 : 5 + n_v]
-    values, out_u, near_f, near_b, far, own, held, grad, seen, mine, sems = refs[5 + n_v :]
+    values, out_u, near_f, near_b, far, own, held, grad, seen, sems = refs[5 + n_v :]
 
     copies = []
 
@@ -38,7 +38,7 @@
             )
     else:
         for i, tile in enumerate(slabs):
-            copy(tile, held.at[i])
+            held[i] = tile[...]
     grad[...] = jnp.zeros_like(grad)
     if wave == 0:
         out_u[...] = users[...] * KEEP
@@ -79,17 +79,12 @@
 
     lax.fori_loop(0, coords.shape[2], one, 0)
 
-    copies.clear()
-    copy(grad.at[1], near_f)
-    copy(grad.at[n_own + 1], near_b)
+    near_f[...] = grad[1]
+    near_b[...] = grad[n_own + 1]
     for way in range(2):
-        copy(grad.at[pl.ds(way * n_own + 2, n_own - 2)], far.at[way])
-    for way in range(2):
+        far[way] = grad[way * n_own + 2 : (way + 1) * n_own]
         source = way * n_own + here if fresh else way * n_own
-        mine[way] = held[source] * KEEP + grad[way * n_own]
-    copy(mine, own)
-    for c in copies:
-        c.wait()
+        own[way] = held[source] * KEEP + grad[way * n_own]
 
 
 def tile_step(sub, wave, n_own, coords, counts, place, users, running, slabs, values):
@@ -106,14 +101,15 @@
             jax.ShapeDtypeStruct((2, n_own - 2, side, width), jnp.float32),
             jax.ShapeDtypeStruct((2, side, width), jnp.float32),
         ),
-        in_specs=[SMEM, SMEM, SMEM, VMEM, VMEM] + [ANY] * len(slabs) + [ANY],
-        out_specs=(VMEM, ANY, ANY, ANY, ANY),
+        in_specs=[SMEM, SMEM, SMEM, VMEM, VMEM]
+        + [VMEM if sub else ANY] * len(slabs)
+        + [ANY],
+        out_specs=(VMEM,) * 5,
         scratch_shapes=[
             pltpu.VMEM((slots, side, width), jnp.float32),
             pltpu.VMEM((slots, side, width), jnp.float32),
             pltpu.VMEM(values.shape[1:], values.dtype),
-            pltpu.VMEM((2, side, width), jnp.float32),
-            pltpu.SemaphoreType.DMA((slots + 1,)),
+            pltpu.SemaphoreType.DMA((3,)),
         ],
         compiler_params=pltpu.CompilerParams(vmem_limit_bytes=24 * 2**20),
         cost_estimate=pl.CostEstimate(
@@ -148,7 +144,7 @@
     return pl.pallas_call(
         functools.partial(lay_kernel, wave, n_own, len(carried)),
         out_shape=jax.ShapeDtypeStruct((n_own, 2 * WAVES, side, width), jnp.float32),
-        in_specs=[SMEM] + [ANY] * (len(carried) + 2 * n_own),
+        in_specs=[SMEM] + [ANY] * len(carried) + [VMEM] * (2 * n_own),
         out_specs=ANY,
         scratch_shapes=[pltpu.SemaphoreType.DMA((2 * n_own,))],
         input_output_aliases={1: 0} if carried else {},

time: 458 us -> 321 us (0.70)
  Pallas kernels: 168 us -> 33.5 us
  starting transfers between devices: 204 us -> 189 us
  waiting for transfers between devices: 75.3 us -> 88.4 us
    pallas_call x2, Pallas kernels: 130 us -> 6.08 us  [lay(): pl.pallas_call(functools.partial(lay_kernel, wave, n_own, len(carried)),...]
    pallas_call x6, Pallas kernels: 38.3 us -> 27.5 us  [tile_step(): pl.pallas_call(functools.partial(tile_kernel, sub, wave, side, n_own), ou...]
    ppermute x84, waiting for transfers between devices: 25.4 us -> 33.8 us  [per_device(): got[way].append(lax.ppermute(got[way][-1], 'grp', ring[way]))]
    ppermute x84, starting transfers between devices: 100 us -> 92.2 us  [per_device(): got[way].append(lax.ppermute(got[way][-1], 'grp', ring[way]))]
  transfers between devices with their start and end apart: 172 -> 172, of which waited for: 97 -> 114; matrix products, arithmetic and copies ran while one was open for 0% -> 0% of each run, Pallas kernels for 21% -> 8%
where the time goes in v2:
time: 321 us; the launch traced here: 322 us
  starting transfers between devices  189 us (59%)
  waiting for transfers between devices  88.4 us (28%)
  Pallas kernels  33.5 us (10%)
  local copies, waits for them, and re-layouts  8.2 us (3%)
    ppermute x84, starting transfers between devices, per_device(): got[way].append(lax.ppermute(got[way][-1], 'grp', ring[way]))  92.2 us
    ppermute x76, starting transfers between devices, per_device(): parts[way] = lax.ppermute(part, 'grp', ring[way])  90.9 us
    ppermute x76, waiting for transfers between devices, per_device(): parts[way] = lax.ppermute(part, 'grp', ring[way])  51 us
    ppermute x84, waiting for transfers between devices, per_device(): got[way].append(lax.ppermute(got[way][-1], 'grp', ring[way]))  33.8 us
    pallas_call x6, Pallas kernels, tile_step(): pl.pallas_call(functools.partial(tile_kernel, sub, wave, side, n_own), ou...  27.5 us
    unnamed x74, local copies, waits for them, and re-layouts  8.2 us
  transfers between devices with their start and end apart: 172, of which 114 were waited for; matrix products, arithmetic and copies ran while one was open for 0% of the time, Pallas kernels for 8%

profile of v2, /device:TPU:0, one launch (start us, length us, event | category | flops | bytes accessed | tf_op | source)
XLA Modules:
  0.0 322.1 jit_solution(15866188527035155741)
XLA Ops:
  2.1 2.2 copy-done.2
  6.8 4.4 %tiles_0_0.1 = (f32[1024,256]{1,0:T(8,128)S(1)}, f32[128,256]{1,0:T(8,128)S(1)}, f32[128,256]{1,0:T(8,128)S(1)}, f32[2,6,128,256]{3,2,1,0:T(8,128)S(1)}, f32[2,128,256]{2,1,0:T(8,128)S(1)}) custom-call(s32[3,2,16]{2,1,0:T(2,128)S(1)} %bitcast.198, s32[3]{0:T(128)S(1)} %bitcast.204, s32[1]{0:T(128)} %bitcast.2.refs_2_.refs_0_, f32[1024,256]{1,0:T(8,128)S(1)} %copy-done.3, ...), custom_call_target="tpu_custom_call" | custom-call | flops 201326592 | bytes 8388608 | tf_op jit(solution)/shard_map/tiles_0_0/pallas_call | solution.py:95
  11.2 4.2 %collective-permute-start.1 = (f32[128,256]{1,0:T(8,128)S(1)}, f32[128,256]{1,0:T(8,128)S(1)}, u32[]{:S(2)}, u32[]{:S(2)}) collective-permute-start(f32[128,256]{1,0:T(8,128)S(1)} %get-tuple-element.35), channel_id=1, source_target_pairs={{0,2},{2,4},{4,6},{6,7},{7,5},{5,3},{3,1},{1,0},{8,10},{10,12},{12... | collective-permute-start | bytes 393224 | tf_op jit(solution)/shard_map/ppermute | solution.py:204
  15.4 4.4 %tiles_0_1.1 = (f32[1024,256]{1,0:T(8,128)S(1)}, f32[128,256]{1,0:T(8,128)S(1)}, f32[128,256]{1,0:T(8,128)S(1)}, f32[2,6,128,256]{3,2,1,0:T(8,128)S(1)}, f32[2,128,256]{2,1,0:T(8,128)S(1)}) custom-call(s32[3,2,16]{2,1,0:T(2,128)S(1)} %bitcast.199, s32[3]{0:T(128)S(1)} %bitcast.205, s32[1]{0:T(128)} %bitcast.2.refs_2_.refs_0_, f32[1024,256]{1,0:T(8,128)S(1)} %copy-done.3, ...), custom_call_target="tpu_custom_call" | custom-call | flops 201326592 | bytes 8388608 | tf_op jit(solution)/shard_map/tiles_0_1/pallas_call | solution.py:95
  22.0 2.8 collective-permute-done.30
  26.3 2.1 collective-permute-start.45
  29.0 2.4 collective-permute-start.31
  32.4 2.0 collective-permute-start.3
  35.5 2.1 collective-permute-done.17
  44.5 2.0 collective-permute-start.33
  54.6 2.2 collective-permute-done.48
  56.8 1.7 collective-permute-start.6
  59.5 2.0 collective-permute-start.35
  61.9 1.7 collective-permute-done.49
  64.5 1.7 collective-permute-start.50
  69.1 1.8 collective-permute-start.8
  112.1 3.7 %tiles_1_0.1 = (f32[1024,256]{1,0:T(8,128)S(1)}, f32[128,256]{1,0:T(8,128)S(1)}, f32[128,256]{1,0:T(8,128)S(1)}, f32[2,6,128,256]{3,2,1,0:T(8,128)S(1)}, f32[2,128,256]{2,1,0:T(8,128)S(1)}) custom-call(s32[3,2,16]{2,1,0:T(2,128)S(1)} %bitcast.200, s32[3]{0:T(128)S(1)} %bitcast.206, s32[1]{0:T(128)} %bitcast.2.refs_2_.refs_0_, ...), custom_call_target="tpu_custom_call" | custom-call | flops 201326592 | bytes 8388608 | tf_op jit(solution)/shard_map/tiles_1_0/pallas_call | solution.py:95
  115.9 2.0 collective-permute-start.73
  117.9 5.2 %tiles_1_1.1 = (f32[1024,256]{1,0:T(8,128)S(1)}, f32[128,256]{1,0:T(8,128)S(1)}, f32[128,256]{1,0:T(8,128)S(1)}, f32[2,6,128,256]{3,2,1,0:T(8,128)S(1)}, f32[2,128,256]{2,1,0:T(8,128)S(1)}) custom-call(s32[3,2,16]{2,1,0:T(2,128)S(1)} %bitcast.201, s32[3]{0:T(128)S(1)} %bitcast.207, s32[1]{0:T(128)} %bitcast.2.refs_2_.refs_0_, ...), custom_call_target="tpu_custom_call" | custom-call | flops 201326592 | bytes 8388608 | tf_op jit(solution)/shard_map/tiles_1_1/pallas_call | solution.py:95
  123.2 2.0 collective-permute-start.102
  126.3 2.0 collective-permute-start.74
  129.1 2.5 collective-permute-start.103
  134.7 2.0 collective-permute-start.61
  148.6 3.4 %collective-permute-start.77 = (f32[128,256]{1,0:T(8,128)S(1)}, f32[128,256]{1,0:T(8,128)S(1)}, u32[]{:S(2)}, u32[]{:S(2)}) collective-permute-start(f32[128,256]{1,0:T(8,128)S(1)} %get-tuple-element.102), channel_id=1, source_target_pairs={{0,1},{2,0},{4,2},{6,4},{7,6},{5,7},{3,5},{1,3},{8,9},{10,8},{12,1... | collective-permute-start | bytes 393224 | tf_op jit(solution)/shard_map/ppermute | solution.py:204
  161.1 2.1 collective-permute-start.107
  164.3 1.7 collective-permute-done.107
  166.4 1.8 collective-permute-done.93
  168.5 1.7 collective-permute-start.94
  171.0 2.6 collective-permute-start.80
  173.8 2.5 collective-permute-start.109
  176.9 1.9 collective-permute-start.81
  180.1 2.5 collective-permute-start.110
  183.1 2.3 collective-permute-start.82
  186.2 2.2 collective-permute-start.111
  189.4 2.5 collective-permute-start.83
  192.4 2.3 collective-permute-start.112
  195.6 2.1 collective-permute-start.84
  198.6 2.5 collective-permute-start.113
  201.7 2.3 collective-permute-start.85
  204.9 2.5 collective-permute-start.114
  207.9 2.4 collective-permute-start.86
  211.3 1.8 collective-permute-start.115
  215.3 5.2 %tiles_2_0.1 = (f32[1024,256]{1,0:T(8,128)S(1)}, f32[128,256]{1,0:T(8,128)S(1)}, f32[128,256]{1,0:T(8,128)S(1)}, f32[2,6,128,256]{3,2,1,0:T(8,128)S(1)}, f32[2,128,256]{2,1,0:T(8,128)S(1)}) custom-call(s32[3,2,16]{2,1,0:T(2,128)S(1)} %bitcast.202, s32[3]{0:T(128)S(1)} %bitcast.208, s32[1]{0:T(128)} %bitcast.2.refs_2_.refs_0_, ...), custom_call_target="tpu_custom_call" | custom-call | flops 201326592 | bytes 8388608 | tf_op jit(solution)/shard_map/tiles_2_0/pallas_call | solution.py:95
  220.5 2.0 collective-permute-start.130
  222.6 4.6 %tiles_2_1.1 = (f32[1024,256]{1,0:T(8,128)}, f32[128,256]{1,0:T(8,128)S(1)}, f32[128,256]{1,0:T(8,128)S(1)}, f32[2,6,128,256]{3,2,1,0:T(8,128)S(1)}, f32[2,128,256]{2,1,0:T(8,128)S(1)}) custom-call(s32[3,2,16]{2,1,0:T(2,128)S(1)} %bitcast.203, s32[3]{0:T(128)S(1)} %bitcast.209, s32[1]{0:T(128)} %bitcast.2.refs_2_.refs_0_, ...), custom_call_target="tpu_custom_call" | custom-call | flops 201326592 | bytes 8388608 | tf_op jit(solution)/shard_map/tiles_2_1/pallas_call | solution.py:95
  229.3 2.0 collective-permute-start.117
  231.3 2.2 collective-permute-done.144
  234.3 1.7 collective-permute-start.145
  245.7 2.5 collective-permute-start.161
  249.1 1.8 collective-permute-start.134
  251.7 2.1 collective-permute-done.147
  253.8 1.9 collective-permute-start.162
  256.1 2.1 collective-permute-start.135
  258.2 2.1 collective-permute-done.162
  281.5 2.1 collective-permute-start.166
  287.7 2.3 collective-permute-start.167
  297.2 2.1 collective-permute-start.141
  299.6 1.7 collective-permute-start.169
  302.2 2.1 collective-permute-start.142
  304.6 1.7 collective-permute-start.170
  307.2 2.1 collective-permute-start.143
  309.5 1.8 collective-permute-start.171
  314.4 3.0 lay_0.1.refs_1_
  318.9 3.0 lay_1.1
  (404 shorter events, 166.2 us)
Async XLA Ops:
  11.2 10.7 %collective-permute-start.1 = (f32[128,256]{1,0:T(8,128)S(1)}, f32[128,256]{1,0:T(8,128)S(1)}, u32[]{:S(2)}, u32[]{:S(2)}) collective-permute-start(f32[128,256]{1,0:T(8,128)S(1)} %get-tuple-element.35), channel_id=1, source_target_pairs={{0,2},{2,4},{4,6},{6,7},{7,5},{5,3},{3,1},{1,0},{8,10},{10,12},{12... | collective-permute-start | bytes 393224 | tf_op jit(solution)/shard_map/ppermute | solution.py:204
  15.4 6.5 %collective-permute-start.15 = (f32[128,256]{1,0:T(8,128)S(1)}, f32[128,256]{1,0:T(8,128)S(1)}, u32[]{:S(2)}, u32[]{:S(2)}) collective-permute-start(f32[128,256]{1,0:T(8,128)S(1)} %get-tuple-element.37), channel_id=1, source_target_pairs={{0,1},{2,0},{4,2},{6,4},{7,6},{5,7},{3,5},{1,3},{8,9},{10,8},{12,1... | collective-permute-start | bytes 393224 | tf_op jit(solution)/shard_map/ppermute | solution.py:204
  15.4 50.8 %collective-permute-start = (f32[2,128,256]{2,1,0:T(8,128)S(1)}, f32[2,128,256]{2,1,0:T(8,128)S(1)}, u32[]{:S(2)}, u32[]{:S(2)}) collective-permute-start(f32[2,128,256]{2,1,0:T(8,128)S(1)} %get-tuple-element.34), channel_id=1, source_target_pairs={{0,24},{8,0},{16,8},{24,16},{1,25},{9,1},{17,9},{25,17},{2,26},{10... | collective-permute-start | bytes 786440 | tf_op jit(solution)/shard_map/ppermute | solution.py:194
  21.9 49.0 %collective-permute-start.29 = (f32[2,128,256]{2,1,0:T(8,128)S(1)}, f32[2,128,256]{2,1,0:T(8,128)S(1)}, u32[]{:S(2)}, u32[]{:S(2)}) collective-permute-start(f32[2,128,256]{2,1,0:T(8,128)S(1)} %get-tuple-element.39), channel_id=1, source_target_pairs={{0,24},{8,0},{16,8},{24,16},{1,25},{9,1},{17,9},{25,17},{2,26},{10... | collective-permute-start | bytes 786440 | tf_op jit(solution)/shard_map/ppermute | solution.py:194
  22.0 7.1 %collective-permute-start.16 = (f32[128,256]{1,0:T(8,128)S(1)}, f32[128,256]{1,0:T(8,128)S(1)}, u32[]{:S(2)}, u32[]{:S(2)}) collective-permute-start(f32[128,256]{1,0:T(8,128)S(1)} %get-tuple-element.132), channel_id=1, source_target_pairs={{0,1},{2,0},{4,2},{6,4},{7,6},{5,7},{3,5},{1,3},{8,9},{10,8},{12,1... | collective-permute-start | bytes 393224 | tf_op jit(solution)/shard_map/ppermute | solution.py:204
  24.8 6.6 %collective-permute-start.2 = (f32[128,256]{1,0:T(8,128)S(1)}, f32[128,256]{1,0:T(8,128)S(1)}, u32[]{:S(2)}, u32[]{:S(2)}) collective-permute-start(f32[128,256]{1,0:T(8,128)S(1)} %get-tuple-element.133), channel_id=1, source_target_pairs={{0,2},{2,4},{4,6},{6,7},{7,5},{5,3},{3,1},{1,0},{8,10},{10,12},{12... | collective-permute-start | bytes 393224 | tf_op jit(solution)/shard_map/ppermute | solution.py:204
  32.4 6.4 %collective-permute-start.3 = (f32[128,256]{1,0:T(8,128)S(1)}, f32[128,256]{1,0:T(8,128)S(1)}, u32[]{:S(2)}, u32[]{:S(2)}) collective-permute-start(f32[128,256]{1,0:T(8,128)S(1)} %get-tuple-element.131), channel_id=1, source_target_pairs={{0,2},{2,4},{4,6},{6,7},{7,5},{5,3},{3,1},{1,0},{8,10},{10,12},{12... | collective-permute-start | bytes 393224 | tf_op jit(solution)/shard_map/ppermute | solution.py:204
  34.6 6.4 %collective-permute-start.46 = (f32[128,256]{1,0:T(8,128)S(1)}, f32[128,256]{1,0:T(8,128)S(1)}, u32[]{:S(2)}, u32[]{:S(2)}) collective-permute-start(f32[128,256]{1,0:T(8,128)S(1)} %get-tuple-element.118), channel_id=1, source_target_pairs={{0,1},{2,0},{4,2},{6,4},{7,6},{5,7},{3,5},{1,3},{8,9},{10,8},{12,1... | collective-permute-start | bytes 393224 | tf_op jit(solution)/shard_map/ppermute | solution.py:204
  50.3 6.5 %collective-permute-start.48 = (f32[128,256]{1,0:T(8,128)S(1)}, f32[128,256]{1,0:T(8,128)S(1)}, u32[]{:S(2)}, u32[]{:S(2)}) collective-permute-start(f32[128,256]{1,0:T(8,128)S(1)} %get-tuple-element.114), channel_id=1, source_target_pairs={{0,1},{2,0},{4,2},{6,4},{7,6},{5,7},{3,5},{1,3},{8,9},{10,8},{12,1... | collective-permute-start | bytes 393224 | tf_op jit(solution)/shard_map/ppermute | solution.py:204
  64.5 6.4 %collective-permute-start.50 = (f32[128,256]{1,0:T(8,128)S(1)}, f32[128,256]{1,0:T(8,128)S(1)}, u32[]{:S(2)}, u32[]{:S(2)}) collective-permute-start(f32[128,256]{1,0:T(8,128)S(1)} %get-tuple-element.110), channel_id=1, source_target_pairs={{0,25},{2,24},{4,26},{6,28},{7,30},{5,31},{3,29},{1,27},{8,1},{10,... | collective-permute-start | bytes 393224 | tf_op jit(solution)/shard_map/ppermute | solution.py:202
  69.1 7.2 %collective-permute-start.8 = (f32[128,256]{1,0:T(8,128)S(1)}, f32[128,256]{1,0:T(8,128)S(1)}, u32[]{:S(2)}, u32[]{:S(2)}) collective-permute-start(f32[128,256]{1,0:T(8,128)S(1)} %get-tuple-element.145.refs_5_), channel_id=1, source_target_pairs={{0,2},{2,4},{4,6},{6,7},{7,5},{5,3},{3,1},{1,0},{8,10},{10,12},{12... | collective-permute-start | bytes 393224 | tf_op jit(solution)/shard_map/ppermute | solution.py:208
  71.5 6.4 %collective-permute-start.51 = (f32[128,256]{1,0:T(8,128)S(1)}, f32[128,256]{1,0:T(8,128)S(1)}, u32[]{:S(2)}, u32[]{:S(2)}) collective-permute-start(f32[128,256]{1,0:T(8,128)S(1)} %get-tuple-element.142.refs_13_), channel_id=1, source_target_pairs={{0,1},{2,0},{4,2},{6,4},{7,6},{5,7},{3,5},{1,3},{8,9},{10,8},{12,1... | collective-permute-start | bytes 393224 | tf_op jit(solution)/shard_map/ppermute | solution.py:208
  72.2 6.9 %collective-permute-start.37 = (f32[128,256]{1,0:T(8,128)S(1)}, f32[128,256]{1,0:T(8,128)S(1)}, u32[]{:S(2)}, u32[]{:S(2)}) collective-permute-start(f32[128,256]{1,0:T(8,128)S(1)} %get-tuple-element.143.refs_5_), channel_id=1, source_target_pairs={{0,2},{2,4},{4,6},{6,7},{7,5},{5,3},{3,1},{1,0},{8,10},{10,12},{12... | collective-permute-start | bytes 393224 | tf_op jit(solution)/shard_map/ppermute | solution.py:208
  74.4 6.4 %collective-permute-start.23 = (f32[128,256]{1,0:T(8,128)S(1)}, f32[128,256]{1,0:T(8,128)S(1)}, u32[]{:S(2)}, u32[]{:S(2)}) collective-permute-start(f32[128,256]{1,0:T(8,128)S(1)} %collective-permute-done.22.refs_14_), channel_id=1, source_target_pairs={{0,1},{2,0},{4,2},{6,4},{7,6},{5,7},{3,5},{1,3},{8,9},{10,8},{12,1... | collective-permute-start | bytes 393224 | tf_op jit(solution)/shard_map/ppermute | solution.py:208
  79.1 6.6 %collective-permute-start.38 = (f32[128,256]{1,0:T(8,128)S(1)}, f32[128,256]{1,0:T(8,128)S(1)}, u32[]{:S(2)}, u32[]{:S(2)}) collective-permute-start(f32[128,256]{1,0:T(8,128)S(1)} %collective-permute-done.37.refs_6_), channel_id=1, source_target_pairs={{0,2},{2,4},{4,6},{6,7},{7,5},{5,3},{3,1},{1,0},{8,10},{10,12},{12... | collective-permute-start | bytes 393224 | tf_op jit(solution)/shard_map/ppermute | solution.py:208
  80.8 6.4 %collective-permute-start.24 = (f32[128,256]{1,0:T(8,128)S(1)}, f32[128,256]{1,0:T(8,128)S(1)}, u32[]{:S(2)}, u32[]{:S(2)}) collective-permute-start(f32[128,256]{1,0:T(8,128)S(1)} %collective-permute-done.23.refs_15_), channel_id=1, source_target_pairs={{0,1},{2,0},{4,2},{6,4},{7,6},{5,7},{3,5},{1,3},{8,9},{10,8},{12,1... | collective-permute-start | bytes 393224 | tf_op jit(solution)/shard_map/ppermute | solution.py:208
  81.9 6.6 %collective-permute-start.10 = (f32[128,256]{1,0:T(8,128)S(1)}, f32[128,256]{1,0:T(8,128)S(1)}, u32[]{:S(2)}, u32[]{:S(2)}) collective-permute-start(f32[128,256]{1,0:T(8,128)S(1)} %collective-permute-done.9.refs_7_), channel_id=1, source_target_pairs={{0,2},{2,4},{4,6},{6,7},{7,5},{5,3},{3,1},{1,0},{8,10},{10,12},{12... | collective-permute-start | bytes 393224 | tf_op jit(solution)/shard_map/ppermute | solution.py:208
  83.6 6.4 %collective-permute-start.53 = (f32[128,256]{1,0:T(8,128)S(1)}, f32[128,256]{1,0:T(8,128)S(1)}, u32[]{:S(2)}, u32[]{:S(2)}) collective-permute-start(f32[128,256]{1,0:T(8,128)S(1)} %collective-permute-done.52.refs_15_), channel_id=1, source_target_pairs={{0,1},{2,0},{4,2},{6,4},{7,6},{5,7},{3,5},{1,3},{8,9},{10,8},{12,1... | collective-permute-start | bytes 393224 | tf_op jit(solution)/shard_map/ppermute | solution.py:208
  87.3 6.4 %collective-permute-start.25 = (f32[128,256]{1,0:T(8,128)S(1)}, f32[128,256]{1,0:T(8,128)S(1)}, u32[]{:S(2)}, u32[]{:S(2)}) collective-permute-start(f32[128,256]{1,0:T(8,128)S(1)} %collective-permute-done.24.refs_16_), channel_id=1, source_target_pairs={{0,1},{2,0},{4,2},{6,4},{7,6},{5,7},{3,5},{1,3},{8,9},{10,8},{12,1... | collective-permute-start | bytes 393224 | tf_op jit(solution)/shard_map/ppermute | solution.py:208
  88.5 6.3 %collective-permute-start.11 = (f32[128,256]{1,0:T(8,128)S(1)}, f32[128,256]{1,0:T(8,128)S(1)}, u32[]{:S(2)}, u32[]{:S(2)}) collective-permute-start(f32[128,256]{1,0:T(8,128)S(1)} %collective-permute-done.10.refs_8_), channel_id=1, source_target_pairs={{0,2},{2,4},{4,6},{6,7},{7,5},{5,3},{3,1},{1,0},{8,10},{10,12},{12... | collective-permute-start | bytes 393224 | tf_op jit(solution)/shard_map/ppermute | solution.py:208
  90.0 6.3 %collective-permute-start.54 = (f32[128,256]{1,0:T(8,128)S(1)}, f32[128,256]{1,0:T(8,128)S(1)}, u32[]{:S(2)}, u32[]{:S(2)}) collective-permute-start(f32[128,256]{1,0:T(8,128)S(1)} %collective-permute-done.53.refs_16_), channel_id=1, source_target_pairs={{0,1},{2,0},{4,2},{6,4},{7,6},{5,7},{3,5},{1,3},{8,9},{10,8},{12,1... | collective-permute-start | bytes 393224 | tf_op jit(solution)/shard_map/ppermute | solution.py:208
  96.3 6.4 %collective-permute-start.55 = (f32[128,256]{1,0:T(8,128)S(1)}, f32[128,256]{1,0:T(8,128)S(1)}, u32[]{:S(2)}, u32[]{:S(2)}) collective-permute-start(f32[128,256]{1,0:T(8,128)S(1)} %collective-permute-done.54.refs_17_), channel_id=1, source_target_pairs={{0,1},{2,0},{4,2},{6,4},{7,6},{5,7},{3,5},{1,3},{8,9},{10,8},{12,1... | collective-permute-start | bytes 393224 | tf_op jit(solution)/shard_map/ppermute | solution.py:208
  97.7 6.4 %collective-permute-start.41 = (f32[128,256]{1,0:T(8,128)S(1)}, f32[128,256]{1,0:T(8,128)S(1)}, u32[]{:S(2)}, u32[]{:S(2)}) collective-permute-start(f32[128,256]{1,0:T(8,128)S(1)} %collective-permute-done.40.refs_9_), channel_id=1, source_target_pairs={{0,2},{2,4},{4,6},{6,7},{7,5},{5,3},{3,1},{1,0},{8,10},{10,12},{12... | collective-permute-start | bytes 393224 | tf_op jit(solution)/shard_map/ppermute | solution.py:208
  99.2 6.3 %collective-permute-start.27 = (f32[128,256]{1,0:T(8,128)S(1)}, f32[128,256]{1,0:T(8,128)S(1)}, u32[]{:S(2)}, u32[]{:S(2)}) collective-permute-start(f32[128,256]{1,0:T(8,128)S(1)} %collective-permute-done.26.refs_18_), channel_id=1, source_target_pairs={{0,1},{2,0},{4,2},{6,4},{7,6},{5,7},{3,5},{1,3},{8,9},{10,8},{12,1... | collective-permute-start | bytes 393224 | tf_op jit(solution)/shard_map/ppermute | solution.py:208
  108.9 9.0 %collective-permute-start.57 = (f32[128,256]{1,0:T(8,128)S(1)}, f32[128,256]{1,0:T(8,128)S(1)}, u32[]{:S(2)}, u32[]{:S(2)}) collective-permute-start(f32[128,256]{1,0:T(8,128)S(1)} %collective-permute-done.56.refs_19_), channel_id=1, source_target_pairs={{0,1},{2,0},{4,2},{6,4},{7,6},{5,7},{3,5},{1,3},{8,9},{10,8},{12,1... | collective-permute-start | bytes 393224 | tf_op jit(solution)/shard_map/ppermute | solution.py:208
  109.9 8.0 %collective-permute-start.43 = (f32[128,256]{1,0:T(8,128)S(1)}, f32[128,256]{1,0:T(8,128)S(1)}, u32[]{:S(2)}, u32[]{:S(2)}) collective-permute-start(f32[128,256]{1,0:T(8,128)S(1)} %collective-permute-done.42.refs_11_), channel_id=1, source_target_pairs={{0,2},{2,4},{4,6},{6,7},{7,5},{5,3},{3,1},{1,0},{8,10},{10,12},{12... | collective-permute-start | bytes 393224 | tf_op jit(solution)/shard_map/ppermute | solution.py:208
  115.8 9.4 %collective-permute-start.59 = (f32[128,256]{1,0:T(8,128)S(1)}, f32[128,256]{1,0:T(8,128)S(1)}, u32[]{:S(2)}, u32[]{:S(2)}) collective-permute-start(f32[128,256]{1,0:T(8,128)S(1)} %get-tuple-element.45), channel_id=1, source_target_pairs={{0,2},{2,4},{4,6},{6,7},{7,5},{5,3},{3,1},{1,0},{8,10},{10,12},{12... | collective-permute-start | bytes 393224 | tf_op jit(solution)/shard_map/ppermute | solution.py:204
  115.9 10.3 %collective-permute-start.73 = (f32[128,256]{1,0:T(8,128)S(1)}, f32[128,256]{1,0:T(8,128)S(1)}, u32[]{:S(2)}, u32[]{:S(2)}) collective-permute-start(f32[128,256]{1,0:T(8,128)S(1)} %get-tuple-element.47), channel_id=1, source_target_pairs={{0,1},{2,0},{4,2},{6,4},{7,6},{5,7},{3,5},{1,3},{8,9},{10,8},{12,1... | collective-permute-start | bytes 393224 | tf_op jit(solution)/shard_map/ppermute | solution.py:204
  125.2 48.4 %collective-permute-start.87 = (f32[2,128,256]{2,1,0:T(8,128)S(1)}, f32[2,128,256]{2,1,0:T(8,128)S(1)}, u32[]{:S(2)}, u32[]{:S(2)}) collective-permute-start(f32[2,128,256]{2,1,0:T(8,128)S(1)} %get-tuple-element.49), channel_id=1, source_target_pairs={{0,24},{8,0},{16,8},{24,16},{1,25},{9,1},{17,9},{25,17},{2,26},{10... | collective-permute-start | bytes 786440 | tf_op jit(solution)/shard_map/ppermute | solution.py:194
  125.2 43.3 %collective-permute-start.58 = (f32[2,128,256]{2,1,0:T(8,128)S(1)}, f32[2,128,256]{2,1,0:T(8,128)S(1)}, u32[]{:S(2)}, u32[]{:S(2)}) collective-permute-start(f32[2,128,256]{2,1,0:T(8,128)S(1)} %get-tuple-element.44), channel_id=1, source_target_pairs={{0,24},{8,0},{16,8},{24,16},{1,25},{9,1},{17,9},{25,17},{2,26},{10... | collective-permute-start | bytes 786440 | tf_op jit(solution)/shard_map/ppermute | solution.py:194
  126.3 6.3 %collective-permute-start.74 = (f32[128,256]{1,0:T(8,128)S(1)}, f32[128,256]{1,0:T(8,128)S(1)}, u32[]{:S(2)}, u32[]{:S(2)}) collective-permute-start(f32[128,256]{1,0:T(8,128)S(1)} %get-tuple-element.108), channel_id=1, source_target_pairs={{0,1},{2,0},{4,2},{6,4},{7,6},{5,7},{3,5},{1,3},{8,9},{10,8},{12,1... | collective-permute-start | bytes 393224 | tf_op jit(solution)/shard_map/ppermute | solution.py:204
  146.2 6.3 %collective-permute-start.105 = (f32[128,256]{1,0:T(8,128)S(1)}, f32[128,256]{1,0:T(8,128)S(1)}, u32[]{:S(2)}, u32[]{:S(2)}) collective-permute-start(f32[128,256]{1,0:T(8,128)S(1)} %get-tuple-element.92), channel_id=1, source_target_pairs={{0,1},{2,0},{4,2},{6,4},{7,6},{5,7},{3,5},{1,3},{8,9},{10,8},{12,1... | collective-permute-start | bytes 393224 | tf_op jit(solution)/shard_map/ppermute | solution.py:204
  148.6 7.0 %collective-permute-start.77 = (f32[128,256]{1,0:T(8,128)S(1)}, f32[128,256]{1,0:T(8,128)S(1)}, u32[]{:S(2)}, u32[]{:S(2)}) collective-permute-start(f32[128,256]{1,0:T(8,128)S(1)} %get-tuple-element.102), channel_id=1, source_target_pairs={{0,1},{2,0},{4,2},{6,4},{7,6},{5,7},{3,5},{1,3},{8,9},{10,8},{12,1... | collective-permute-start | bytes 393224 | tf_op jit(solution)/shard_map/ppermute | solution.py:204
  173.8 6.3 %collective-permute-start.109 = (f32[128,256]{1,0:T(8,128)S(1)}, f32[128,256]{1,0:T(8,128)S(1)}, u32[]{:S(2)}, u32[]{:S(2)}) collective-permute-start(f32[128,256]{1,0:T(8,128)S(1)} %get-tuple-element.138.refs_13_), channel_id=1, source_target_pairs={{0,1},{2,0},{4,2},{6,4},{7,6},{5,7},{3,5},{1,3},{8,9},{10,8},{12,1... | collective-permute-start | bytes 393224 | tf_op jit(solution)/shard_map/ppermute | solution.py:208
  176.3 6.4 %collective-permute-start.95 = (f32[128,256]{1,0:T(8,128)S(1)}, f32[128,256]{1,0:T(8,128)S(1)}, u32[]{:S(2)}, u32[]{:S(2)}) collective-permute-start(f32[128,256]{1,0:T(8,128)S(1)} %get-tuple-element.139.refs_5_), channel_id=1, source_target_pairs={{0,2},{2,4},{4,6},{6,7},{7,5},{5,3},{3,1},{1,0},{8,10},{10,12},{12... | collective-permute-start | bytes 393224 | tf_op jit(solution)/shard_map/ppermute | solution.py:208
  178.8 6.6 %collective-permute-start.67 = (f32[128,256]{1,0:T(8,128)S(1)}, f32[128,256]{1,0:T(8,128)S(1)}, u32[]{:S(2)}, u32[]{:S(2)}) collective-permute-start(f32[128,256]{1,0:T(8,128)S(1)} %collective-permute-done.66.refs_6_), channel_id=1, source_target_pairs={{0,2},{2,4},{4,6},{6,7},{7,5},{5,3},{3,1},{1,0},{8,10},{10,12},{12... | collective-permute-start | bytes 393224 | tf_op jit(solution)/shard_map/ppermute | solution.py:208
  185.4 6.4 %collective-permute-start.68 = (f32[128,256]{1,0:T(8,128)S(1)}, f32[128,256]{1,0:T(8,128)S(1)}, u32[]{:S(2)}, u32[]{:S(2)}) collective-permute-start(f32[128,256]{1,0:T(8,128)S(1)} %collective-permute-done.67.refs_7_), channel_id=1, source_target_pairs={{0,2},{2,4},{4,6},{6,7},{7,5},{5,3},{3,1},{1,0},{8,10},{10,12},{12... | collective-permute-start | bytes 393224 | tf_op jit(solution)/shard_map/ppermute | solution.py:208
  194.7 6.4 %collective-permute-start.98 = (f32[128,256]{1,0:T(8,128)S(1)}, f32[128,256]{1,0:T(8,128)S(1)}, u32[]{:S(2)}, u32[]{:S(2)}) collective-permute-start(f32[128,256]{1,0:T(8,128)S(1)} %collective-permute-done.97.refs_8_), channel_id=1, source_target_pairs={{0,2},{2,4},{4,6},{6,7},{7,5},{5,3},{3,1},{1,0},{8,10},{10,12},{12... | collective-permute-start | bytes 393224 | tf_op jit(solution)/shard_map/ppermute | solution.py:208
  198.6 6.3 %collective-permute-start.113 = (f32[128,256]{1,0:T(8,128)S(1)}, f32[128,256]{1,0:T(8,128)S(1)}, u32[]{:S(2)}, u32[]{:S(2)}) collective-permute-start(f32[128,256]{1,0:T(8,128)S(1)} %collective-permute-done.112.refs_17_), channel_id=1, source_target_pairs={{0,1},{2,0},{4,2},{6,4},{7,6},{5,7},{3,5},{1,3},{8,9},{10,8},{12,1... | collective-permute-start | bytes 393224 | tf_op jit(solution)/shard_map/ppermute | solution.py:208
  201.1 6.3 %collective-permute-start.99 = (f32[128,256]{1,0:T(8,128)S(1)}, f32[128,256]{1,0:T(8,128)S(1)}, u32[]{:S(2)}, u32[]{:S(2)}) collective-permute-start(f32[128,256]{1,0:T(8,128)S(1)} %collective-permute-done.98.refs_9_), channel_id=1, source_target_pairs={{0,2},{2,4},{4,6},{6,7},{7,5},{5,3},{3,1},{1,0},{8,10},{10,12},{12... | collective-permute-start | bytes 393224 | tf_op jit(solution)/shard_map/ppermute | solution.py:208
  204.9 6.4 %collective-permute-start.114 = (f32[128,256]{1,0:T(8,128)S(1)}, f32[128,256]{1,0:T(8,128)S(1)}, u32[]{:S(2)}, u32[]{:S(2)}) collective-permute-start(f32[128,256]{1,0:T(8,128)S(1)} %collective-permute-done.113.refs_18_), channel_id=1, source_target_pairs={{0,1},{2,0},{4,2},{6,4},{7,6},{5,7},{3,5},{1,3},{8,9},{10,8},{12,1... | collective-permute-start | bytes 393224 | tf_op jit(solution)/shard_map/ppermute | solution.py:208
  211.3 11.3 %collective-permute-start.115 = (f32[128,256]{1,0:T(8,128)S(1)}, f32[128,256]{1,0:T(8,128)S(1)}, u32[]{:S(2)}, u32[]{:S(2)}) collective-permute-start(f32[128,256]{1,0:T(8,128)S(1)} %collective-permute-done.114.refs_19_), channel_id=1, source_target_pairs={{0,1},{2,0},{4,2},{6,4},{7,6},{5,7},{3,5},{1,3},{8,9},{10,8},{12,1... | collective-permute-start | bytes 393224 | tf_op jit(solution)/shard_map/ppermute | solution.py:208
  213.1 9.5 %collective-permute-start.101 = (f32[128,256]{1,0:T(8,128)S(1)}, f32[128,256]{1,0:T(8,128)S(1)}, u32[]{:S(2)}, u32[]{:S(2)}) collective-permute-start(f32[128,256]{1,0:T(8,128)S(1)} %collective-permute-done.100.refs_11_), channel_id=1, source_target_pairs={{0,2},{2,4},{4,6},{6,7},{7,5},{5,3},{3,1},{1,0},{8,10},{10,12},{12... | collective-permute-start | bytes 393224 | tf_op jit(solution)/shard_map/ppermute | solution.py:208
  220.5 8.7 %collective-permute-start.116 = (f32[128,256]{1,0:T(8,128)S(1)}, f32[128,256]{1,0:T(8,128)S(1)}, u32[]{:S(2)}, u32[]{:S(2)}) collective-permute-start(f32[128,256]{1,0:T(8,128)S(1)} %get-tuple-element.55), channel_id=1, source_target_pairs={{0,2},{2,4},{4,6},{6,7},{7,5},{5,3},{3,1},{1,0},{8,10},{10,12},{12... | collective-permute-start | bytes 393224 | tf_op jit(solution)/shard_map/ppermute | solution.py:204
  220.5 8.7 %collective-permute-start.130 = (f32[128,256]{1,0:T(8,128)S(1)}, f32[128,256]{1,0:T(8,128)S(1)}, u32[]{:S(2)}, u32[]{:S(2)}) collective-permute-start(f32[128,256]{1,0:T(8,128)S(1)} %get-tuple-element.57), channel_id=1, source_target_pairs={{0,1},{2,0},{4,2},{6,4},{7,6},{5,7},{3,5},{1,3},{8,9},{10,8},{12,1... | collective-permute-start | bytes 393224 | tf_op jit(solution)/shard_map/ppermute | solution.py:204
  227.1 6.4 %collective-permute-start.144 = (f32[128,256]{1,0:T(8,128)S(1)}, f32[128,256]{1,0:T(8,128)S(1)}, u32[]{:S(2)}, u32[]{:S(2)}) collective-permute-start(f32[128,256]{1,0:T(8,128)S(1)} %get-tuple-element.59), channel_id=1, source_target_pairs={{0,2},{2,4},{4,6},{6,7},{7,5},{5,3},{3,1},{1,0},{8,10},{10,12},{12... | collective-permute-start | bytes 393224 | tf_op jit(solution)/shard_map/ppermute | solution.py:204
  229.3 6.7 %collective-permute-start.131 = (f32[128,256]{1,0:T(8,128)S(1)}, f32[128,256]{1,0:T(8,128)S(1)}, u32[]{:S(2)}, u32[]{:S(2)}) collective-permute-start(f32[128,256]{1,0:T(8,128)S(1)} %get-tuple-element.84), channel_id=1, source_target_pairs={{0,1},{2,0},{4,2},{6,4},{7,6},{5,7},{3,5},{1,3},{8,9},{10,8},{12,1... | collective-permute-start | bytes 393224 | tf_op jit(solution)/shard_map/ppermute | solution.py:204
  229.3 6.7 %collective-permute-start.117 = (f32[128,256]{1,0:T(8,128)S(1)}, f32[128,256]{1,0:T(8,128)S(1)}, u32[]{:S(2)}, u32[]{:S(2)}) collective-permute-start(f32[128,256]{1,0:T(8,128)S(1)} %get-tuple-element.85), channel_id=1, source_target_pairs={{0,2},{2,4},{4,6},{6,7},{7,5},{5,3},{3,1},{1,0},{8,10},{10,12},{12... | collective-permute-start | bytes 393224 | tf_op jit(solution)/shard_map/ppermute | solution.py:204
  236.0 6.3 %collective-permute-start.132 = (f32[128,256]{1,0:T(8,128)S(1)}, f32[128,256]{1,0:T(8,128)S(1)}, u32[]{:S(2)}, u32[]{:S(2)}) collective-permute-start(f32[128,256]{1,0:T(8,128)S(1)} %get-tuple-element.82), channel_id=1, source_target_pairs={{0,1},{2,0},{4,2},{6,4},{7,6},{5,7},{3,5},{1,3},{8,9},{10,8},{12,1... | collective-permute-start | bytes 393224 | tf_op jit(solution)/shard_map/ppermute | solution.py:204
  242.7 6.4 %collective-permute-start.133 = (f32[128,256]{1,0:T(8,128)S(1)}, f32[128,256]{1,0:T(8,128)S(1)}, u32[]{:S(2)}, u32[]{:S(2)}) collective-permute-start(f32[128,256]{1,0:T(8,128)S(1)} %get-tuple-element.80), channel_id=1, source_target_pairs={{0,1},{2,0},{4,2},{6,4},{7,6},{5,7},{3,5},{1,3},{8,9},{10,8},{12,1... | collective-permute-start | bytes 393224 | tf_op jit(solution)/shard_map/ppermute | solution.py:204
  249.1 6.8 %collective-permute-start.134 = (f32[128,256]{1,0:T(8,128)S(1)}, f32[128,256]{1,0:T(8,128)S(1)}, u32[]{:S(2)}, u32[]{:S(2)}) collective-permute-start(f32[128,256]{1,0:T(8,128)S(1)} %get-tuple-element.78), channel_id=1, source_target_pairs={{0,1},{2,0},{4,2},{6,4},{7,6},{5,7},{3,5},{1,3},{8,9},{10,8},{12,1... | collective-permute-start | bytes 393224 | tf_op jit(solution)/shard_map/ppermute | solution.py:204
  253.8 6.4 %collective-permute-start.162 = (f32[128,256]{1,0:T(8,128)S(1)}, f32[128,256]{1,0:T(8,128)S(1)}, u32[]{:S(2)}, u32[]{:S(2)}) collective-permute-start(f32[128,256]{1,0:T(8,128)S(1)} %get-tuple-element.66), channel_id=1, source_target_pairs={{0,1},{2,0},{4,2},{6,4},{7,6},{5,7},{3,5},{1,3},{8,9},{10,8},{12,1... | collective-permute-start | bytes 393224 | tf_op jit(solution)/shard_map/ppermute | solution.py:204
  256.1 7.9 %collective-permute-start.135 = (f32[128,256]{1,0:T(8,128)S(1)}, f32[128,256]{1,0:T(8,128)S(1)}, u32[]{:S(2)}, u32[]{:S(2)}) collective-permute-start(f32[128,256]{1,0:T(8,128)S(1)} %get-tuple-element.76), channel_id=1, source_target_pairs={{0,1},{2,0},{4,2},{6,4},{7,6},{5,7},{3,5},{1,3},{8,9},{10,8},{12,1... | collective-permute-start | bytes 393224 | tf_op jit(solution)/shard_map/ppermute | solution.py:204
  258.2 6.5 %collective-permute-start.121 = (f32[128,256]{1,0:T(8,128)S(1)}, f32[128,256]{1,0:T(8,128)S(1)}, u32[]{:S(2)}, u32[]{:S(2)}) collective-permute-start(f32[128,256]{1,0:T(8,128)S(1)} %get-tuple-element.77), channel_id=1, source_target_pairs={{0,2},{2,4},{4,6},{6,7},{7,5},{5,3},{3,1},{1,0},{8,10},{10,12},{12... | collective-permute-start | bytes 393224 | tf_op jit(solution)/shard_map/ppermute | solution.py:204
  261.9 6.3 %collective-permute-start.163 = (f32[128,256]{1,0:T(8,128)S(1)}, f32[128,256]{1,0:T(8,128)S(1)}, u32[]{:S(2)}, u32[]{:S(2)}) collective-permute-start(f32[128,256]{1,0:T(8,128)S(1)} %get-tuple-element.64), channel_id=1, source_target_pairs={{0,1},{2,0},{4,2},{6,4},{7,6},{5,7},{3,5},{1,3},{8,9},{10,8},{12,1... | collective-permute-start | bytes 393224 | tf_op jit(solution)/shard_map/ppermute | solution.py:204
  262.8 6.3 %collective-permute-start.149 = (f32[128,256]{1,0:T(8,128)S(1)}, f32[128,256]{1,0:T(8,128)S(1)}, u32[]{:S(2)}, u32[]{:S(2)}) collective-permute-start(f32[128,256]{1,0:T(8,128)S(1)} %get-tuple-element.65), channel_id=1, source_target_pairs={{0,2},{2,4},{4,6},{6,7},{7,5},{5,3},{3,1},{1,0},{8,10},{10,12},{12... | collective-permute-start | bytes 393224 | tf_op jit(solution)/shard_map/ppermute | solution.py:204
  264.7 6.5 %collective-permute-start.136 = (f32[128,256]{1,0:T(8,128)S(1)}, f32[128,256]{1,0:T(8,128)S(1)}, u32[]{:S(2)}, u32[]{:S(2)}) collective-permute-start(f32[128,256]{1,0:T(8,128)S(1)} %get-tuple-element.74), channel_id=1, source_target_pairs={{0,1},{2,0},{4,2},{6,4},{7,6},{5,7},{3,5},{1,3},{8,9},{10,8},{12,1... | collective-permute-start | bytes 393224 | tf_op jit(solution)/shard_map/ppermute | solution.py:204
  271.8 6.6 %collective-permute-start.137 = (f32[128,256]{1,0:T(8,128)S(1)}, f32[128,256]{1,0:T(8,128)S(1)}, u32[]{:S(2)}, u32[]{:S(2)}) collective-permute-start(f32[128,256]{1,0:T(8,128)S(1)} %get-tuple-element.136.refs_9_), channel_id=1, source_target_pairs={{0,1},{2,0},{4,2},{6,4},{7,6},{5,7},{3,5},{1,3},{8,9},{10,8},{12,1... | collective-permute-start | bytes 393224 | tf_op jit(solution)/shard_map/ppermute | solution.py:208
  278.4 6.3 %collective-permute-start.138 = (f32[128,256]{1,0:T(8,128)S(1)}, f32[128,256]{1,0:T(8,128)S(1)}, u32[]{:S(2)}, u32[]{:S(2)}) collective-permute-start(f32[128,256]{1,0:T(8,128)S(1)} %collective-permute-done.137.refs_10_), channel_id=1, source_target_pairs={{0,1},{2,0},{4,2},{6,4},{7,6},{5,7},{3,5},{1,3},{8,9},{10,8},{12,1... | collective-permute-start | bytes 393224 | tf_op jit(solution)/shard_map/ppermute | solution.py:208
  279.6 7.1 %collective-permute-start.124 = (f32[128,256]{1,0:T(8,128)S(1)}, f32[128,256]{1,0:T(8,128)S(1)}, u32[]{:S(2)}, u32[]{:S(2)}) collective-permute-start(f32[128,256]{1,0:T(8,128)S(1)} %collective-permute-done.123.refs_2_), channel_id=1, source_target_pairs={{0,2},{2,4},{4,6},{6,7},{7,5},{5,3},{3,1},{1,0},{8,10},{10,12},{12... | collective-permute-start | bytes 393224 | tf_op jit(solution)/shard_map/ppermute | solution.py:208
  284.8 6.4 %collective-permute-start.139 = (f32[128,256]{1,0:T(8,128)S(1)}, f32[128,256]{1,0:T(8,128)S(1)}, u32[]{:S(2)}, u32[]{:S(2)}) collective-permute-start(f32[128,256]{1,0:T(8,128)S(1)} %collective-permute-done.138.refs_11_), channel_id=1, source_target_pairs={{0,1},{2,0},{4,2},{6,4},{7,6},{5,7},{3,5},{1,3},{8,9},{10,8},{12,1... | collective-permute-start | bytes 393224 | tf_op jit(solution)/shard_map/ppermute | solution.py:208
  287.7 6.3 %collective-permute-start.167 = (f32[128,256]{1,0:T(8,128)S(1)}, f32[128,256]{1,0:T(8,128)S(1)}, u32[]{:S(2)}, u32[]{:S(2)}) collective-permute-start(f32[128,256]{1,0:T(8,128)S(1)} %collective-permute-done.166.refs_12_), channel_id=1, source_target_pairs={{0,1},{2,0},{4,2},{6,4},{7,6},{5,7},{3,5},{1,3},{8,9},{10,8},{12,1... | collective-permute-start | bytes 393224 | tf_op jit(solution)/shard_map/ppermute | solution.py:208
  292.9 6.4 %collective-permute-start.126 = (f32[128,256]{1,0:T(8,128)S(1)}, f32[128,256]{1,0:T(8,128)S(1)}, u32[]{:S(2)}, u32[]{:S(2)}) collective-permute-start(f32[128,256]{1,0:T(8,128)S(1)} %collective-permute-done.125.refs_4_), channel_id=1, source_target_pairs={{0,2},{2,4},{4,6},{6,7},{7,5},{5,3},{3,1},{1,0},{8,10},{10,12},{12... | collective-permute-start | bytes 393224 | tf_op jit(solution)/shard_map/ppermute | solution.py:208
  309.5 8.1 %collective-permute-start.171 = (f32[128,256]{1,0:T(8,128)S(1)}, f32[128,256]{1,0:T(8,128)S(1)}, u32[]{:S(2)}, u32[]{:S(2)}) collective-permute-start(f32[128,256]{1,0:T(8,128)S(1)} %collective-permute-done.170.refs_16_), channel_id=1, source_target_pairs={{0,1},{2,0},{4,2},{6,4},{7,6},{5,7},{3,5},{1,3},{8,9},{10,8},{12,1... | collective-permute-start | bytes 393224 | tf_op jit(solution)/shard_map/ppermute | solution.py:208
  (145 other events, 1311.5 us)

commit v3 on v2

--- a/solution.py
+++ b/solution.py
@@ -10,17 +10,21 @@
 RATE = 0.003
 KEEP = 1.0 - 0.003 * 0.05
 WAVES = 2
+GROUP = 4
 ANY = pl.BlockSpec(memory_space=pl.ANY)
+HBM = pl.BlockSpec(memory_space=pltpu.HBM)
 VMEM = pl.BlockSpec(memory_space=pltpu.VMEM)
 SMEM = pl.BlockSpec(memory_space=pltpu.SMEM)
 
 
 def tile_kernel(sub, wave, side, n_own, *refs):
     fresh = sub == 0
-    n_v = 1 if fresh else 2 * n_own
-    coords, counts, place, users, running = refs[:5]
-    slabs = refs[5 : 5 + n_v]
-    values, out_u, near_f, near_b, far, own, held, grad, seen, sems = refs[5 + n_v :]
+    refs = list(refs)
+    coords, counts, place, users = (refs.pop(0) for _ in range(4))
+    running = refs.pop(0) if wave else None
+    slabs = [refs.pop(0) for _ in range(1 if fresh else 2 * n_own)]
+    values, out_u, near_f, near_b, far_f, far_b, own = (refs.pop(0) for _ in range(7))
+    held, grad, seen, order, sems = (refs.pop(0) for _ in range(5))
 
     copies = []
 
@@ -29,33 +33,42 @@
         c.start()
         copies.append(c)
 
-    copy(values.at[sub], seen)
     if fresh:
+        (mine,) = refs
+        copy(users, mine)
+        users = mine
         for way in range(2):
             copy(
                 slabs[0].at[:, 2 * wave + way],
                 held.at[pl.ds(way * n_own, n_own)],
             )
-    else:
+    copy(values.at[sub], seen)
+    if not fresh:
         for i, tile in enumerate(slabs):
             held[i] = tile[...]
     grad[...] = jnp.zeros_like(grad)
-    if wave == 0:
-        out_u[...] = users[...] * KEEP
-    else:
-        out_u[...] = running[...]
+
+    count = counts[sub]
+
+    def gather(n, total):
+        order[total] = n
+        hit = (n < count) & (((coords[sub, 1, n] >> 1) & 1) == wave)
+        return total + hit.astype(jnp.int32)
+
+    total = lax.fori_loop(0, coords.shape[2], gather, 0)
     for c in copies:
         c.wait()
-
+    out_u[...] = running[...] if wave else users[...] * KEEP
     here = place[0]
-    count = counts[sub]
-
-    def one(n, carry):
-        a = coords[sub, 0, n]
-        b = coords[sub, 1, n]
-
-        @pl.when((n < count) & (((b >> 1) & 1) == wave))
-        def _():
+
+    def some(i, carry):
+        done = []
+        for j in range(GROUP):
+            at = i * GROUP + j
+            n = order[jnp.minimum(at, total - 1)]
+            rate = jnp.where(at < total, RATE, 0.0)
+            a = coords[sub, 0, n]
+            b = coords[sub, 1, n]
             owner = b >> 2
             way = b & 1
             ahead = jnp.where(way == 0, here - owner, owner - here)
@@ -69,20 +82,22 @@
             )
             resid = (seen[n].astype(jnp.float32) - guess).astype(jnp.bfloat16)
             up = jnp.dot(resid, vb, preferred_element_type=jnp.float32)
-            out_u[rows, :] += RATE * up
             ip = lax.dot_general(
                 resid, ua, (((0,), (0,)), ((), ())), preferred_element_type=jnp.float32
             )
-            grad[slot] += RATE * ip
-
+            done.append((rows, slot, rate * up, rate * ip))
+        for rows, slot, up, ip in done:
+            out_u[rows, :] += up
+            grad[slot] += ip
         return carry
 
-    lax.fori_loop(0, coords.shape[2], one, 0)
+    lax.fori_loop(0, (total + GROUP - 1) // GROUP, some, 0)
 
     near_f[...] = grad[1]
     near_b[...] = grad[n_own + 1]
+    far_f[...] = grad[2:n_own]
+    far_b[...] = grad[n_own + 2 : 2 * n_own]
     for way in range(2):
-        far[way] = grad[way * n_own + 2 : (way + 1) * n_own]
         source = way * n_own + here if fresh else way * n_own
         own[way] = held[source] * KEEP + grad[way * n_own]
 
@@ -91,34 +106,41 @@
     side = values.shape[-1]
     width = users.shape[1]
     tile = jax.ShapeDtypeStruct((side, width), jnp.float32)
+    far = jax.ShapeDtypeStruct((n_own - 2, side, width), jnp.float32)
     slots = 2 * n_own
+    carried = (running,) if wave else ()
     return pl.pallas_call(
         functools.partial(tile_kernel, sub, wave, side, n_own),
         out_shape=(
             jax.ShapeDtypeStruct(users.shape, jnp.float32),
             tile,
             tile,
-            jax.ShapeDtypeStruct((2, n_own - 2, side, width), jnp.float32),
+            far,
+            far,
             jax.ShapeDtypeStruct((2, side, width), jnp.float32),
         ),
-        in_specs=[SMEM, SMEM, SMEM, VMEM, VMEM]
-        + [VMEM if sub else ANY] * len(slabs)
-        + [ANY],
-        out_specs=(VMEM,) * 5,
+        in_specs=[SMEM, SMEM, SMEM, VMEM if sub else HBM]
+        + [VMEM] * len(carried)
+        + [VMEM if sub else HBM] * len(slabs)
+        + [HBM],
+        out_specs=(VMEM,) * 6,
+        input_output_aliases={4: 0} if wave else {},
         scratch_shapes=[
             pltpu.VMEM((slots, side, width), jnp.float32),
             pltpu.VMEM((slots, side, width), jnp.float32),
             pltpu.VMEM(values.shape[1:], values.dtype),
-            pltpu.SemaphoreType.DMA((3,)),
-        ],
-        compiler_params=pltpu.CompilerParams(vmem_limit_bytes=24 * 2**20),
+            pltpu.SMEM((coords.shape[2] + 1,), jnp.int32),
+            pltpu.SemaphoreType.DMA((4,)),
+        ]
+        + ([] if sub else [pltpu.VMEM(users.shape, jnp.float32)]),
+        compiler_params=pltpu.CompilerParams(vmem_limit_bytes=(50 if sub + wave == 0 else 24) * 2**20),
         cost_estimate=pl.CostEstimate(
             flops=8 * 3 * 2 * side * side * width,
             bytes_accessed=8 * 2**20,
             transcendentals=0,
         ),
         name=f"tiles_{sub}_{wave}",
-    )(coords, counts, place, users, running, *slabs, values)
+    )(coords, counts, place, users, *carried, *slabs, values)
 
 
 def lay_kernel(wave, n_own, carried, *refs):
@@ -148,6 +170,7 @@
         out_specs=ANY,
         scratch_shapes=[pltpu.SemaphoreType.DMA((2 * n_own,))],
         input_output_aliases={1: 0} if carried else {},
+        compiler_params=pltpu.CompilerParams(vmem_limit_bytes=16 * 2**20),
         cost_estimate=pl.CostEstimate(flops=0, bytes_accessed=4 * 2**20, transcendentals=0),
         name=f"lay_{wave}",
     )(place, *carried, *tiles)
@@ -184,25 +207,31 @@
         slabs = [[slab] for _ in range(WAVES)]
         for sub in range(rounds):
             final = sub + 1 == rounds
-            after = users
+            after = None
+            sums = []
+            owns = []
+            for wave in range(WAVES):
+                after, *near, far_f, far_b, own = tile_step(
+                    sub, wave, n_grp, coords, counts, place, users, after, slabs[wave], values
+                )
+                sums.append((near, (far_f, far_b)))
+                owns.append(own)
+            if not final:
+                owns = [lax.ppermute(own, "strat", turn) for own in owns]
+            owns = [[lax.optimization_barrier(own[way]) for way in range(2)] for own in owns]
             nexts = []
             for wave in range(WAVES):
-                after, near_f, near_b, far, own = tile_step(
-                    sub, wave, n_grp, coords, counts, place, users, after, slabs[wave], values
-                )
-                if not final:
-                    own = lax.ppermute(own, "strat", turn)
-                parts = [near_f, near_b]
+                parts, far = sums[wave]
                 for t in range(1, n_grp):
                     for way in range(2):
                         part = parts[way]
                         if t > 1:
-                            part = part + far[way, t - 2]
+                            part = part + far[way][t - 2]
                         if t + 1 == n_grp and not final:
                             parts[way] = lax.ppermute(part, ("strat", "grp"), last[way])
                         else:
                             parts[way] = lax.ppermute(part, "grp", ring[way])
-                got = [[own[way] + parts[way]] for way in range(2)]
+                got = [[owns[wave][way] + parts[way]] for way in range(2)]
                 for t in range(1, n_grp):
                     for way in range(2):
                         got[way].append(lax.ppermute(got[way][-1], "grp", ring[way]))

time: 321 us -> 294 us (0.916)
  Pallas kernels: 33.5 us -> 21.3 us
  starting transfers between devices: 189 us -> 182 us
  local copies, waits for them, and re-layouts: 8.2 us -> 2.02 us
  waiting for transfers between devices: 88.4 us -> 84.6 us
    ppermute x76, waiting for transfers between devices: 51 us -> 38.1 us  [per_device(): parts[way] = lax.ppermute(part, 'grp', ring[way])]
    ppermute x84, waiting for transfers between devices: 33.8 us -> 44 us  [per_device(): got[way].append(lax.ppermute(got[way][-1], 'grp', ring[way]))]
    pallas_call x6, Pallas kernels: 27.5 us -> 18.5 us  [tile_step(): pl.pallas_call(functools.partial(tile_kernel, sub, wave, side, n_own), ou...]
    ppermute x84, starting transfers between devices: 92.2 us -> 84.4 us  [per_device(): got[way].append(lax.ppermute(got[way][-1], 'grp', ring[way]))]
    unnamed x74 -> x10, local copies, waits for them, and re-layouts: 8.2 us -> 1.91 us
  transfers between devices with their start and end apart: 172 -> 172, of which waited for: 114 -> 122; matrix products, arithmetic and copies ran while one was open for 0% -> 1% of each run, Pallas kernels for 8% -> 3%
where the time goes in v3:
time: 294 us; the launch traced here: 293 us
  starting transfers between devices  182 us (62%)
  waiting for transfers between devices  84.6 us (29%)
  Pallas kernels  21.3 us (7%)
    ppermute x76, starting transfers between devices, per_device(): parts[way] = lax.ppermute(part, 'grp', ring[way])  90.1 us
    ppermute x84, starting transfers between devices, per_device(): got[way].append(lax.ppermute(got[way][-1], 'grp', ring[way]))  84.4 us
    ppermute x84, waiting for transfers between devices, per_device(): got[way].append(lax.ppermute(got[way][-1], 'grp', ring[way]))  44 us
    ppermute x76, waiting for transfers between devices, per_device(): parts[way] = lax.ppermute(part, 'grp', ring[way])  38.1 us
    pallas_call x6, Pallas kernels, tile_step(): pl.pallas_call(functools.partial(tile_kernel, sub, wave, side, n_own), ou...  18.5 us
    ppermute x8, starting transfers between devices, per_device(): parts[way] = lax.ppermute(part, ('strat', 'grp'), last[way])  6.61 us
  transfers between devices with their start and end apart: 172, of which 122 were waited for; matrix products, arithmetic and copies ran while one was open for 1% of the time, Pallas kernels for 3%

profile of v3, /device:TPU:0, one launch (start us, length us, event | category | flops | bytes accessed | tf_op | source)
XLA Modules:
  0.0 293.1 jit_solution(4484604773548538500)
XLA Ops:
  2.6 4.4 %tiles_0_0.1 = (f32[1024,256]{1,0:T(8,128)S(1)}, f32[128,256]{1,0:T(8,128)S(1)}, f32[128,256]{1,0:T(8,128)S(1)}, f32[6,128,256]{2,1,0:T(8,128)S(1)}, f32[6,128,2...) custom-call(s32[3,2,16]{2,1,0:T(2,128)S(1)} %bitcast.182, s32[3]{0:T(128)S(1)} %bitcast.188, s32[1]{0:T(128)} %bitcast.2.refs_2_.refs_0_, ...), custom_call_target="tpu_custom_call" | custom-call | flops 201326592 | bytes 8388608 | tf_op jit(solution)/shard_map/tiles_0_0/pallas_call | solution.py:112
  7.0 2.3 collective-permute-start.1
  9.3 1.6 collective-permute-start.15
  11.6 2.3 tiles_0_1.1
  13.9 3.4 %collective-permute-start.30 = (f32[128,256]{1,0:T(8,128)S(1)}, f32[128,256]{1,0:T(8,128)S(1)}, u32[]{:S(2)}, u32[]{:S(2)}) collective-permute-start(f32[128,256]{1,0:T(8,128)S(1)} %get-tuple-element.47), channel_id=1, source_target_pairs={{0,2},{2,4},{4,6},{6,7},{7,5},{5,3},{3,1},{1,0},{8,10},{10,12},{12... | collective-permute-start | bytes 393224 | tf_op jit(solution)/shard_map/ppermute | solution.py:233
  17.3 2.1 collective-permute-start.2
  25.5 1.7 collective-permute-start.3
  27.7 1.7 collective-permute-start.32
  30.4 1.3 collective-permute-done.3
  31.7 1.8 collective-permute-start.4
  34.6 1.8 collective-permute-start.33
  37.7 1.5 collective-permute-start.5
  41.1 1.7 collective-permute-start.34
  43.9 1.7 collective-permute-start.6
  50.7 1.5 collective-permute-start.21
  53.6 1.5 collective-permute-start.50
  55.1 1.3 collective-permute-start.8
  59.2 1.4 collective-permute-start.51
  65.7 1.3 collective-permute-start.52
  68.5 1.3 collective-permute-start.24
  81.2 1.3 collective-permute-start.26
  90.4 1.4 collective-permute-start.56
  98.8 2.2 tiles_1_0.1
  101.7 2.2 tiles_1_1.1
  103.9 2.3 collective-permute-start.88
  106.2 2.0 collective-permute-start.59
  109.3 1.8 collective-permute-done.102
  111.1 1.7 collective-permute-start.89
  113.6 1.5 collective-permute-start.60
  115.3 2.0 collective-permute-start.74
  117.4 1.7 collective-permute-start.90
  119.5 1.7 collective-permute-start.61
  121.2 2.3 collective-permute-start.75
  123.6 1.4 collective-permute-start.91
  125.1 1.3 collective-permute-start.105
  127.7 1.9 collective-permute-start.76
  131.2 1.6 collective-permute-start.106
  134.2 1.4 collective-permute-start.77
  137.4 1.6 collective-permute-start.107
  140.6 1.4 collective-permute-start.78
  142.2 2.1 collective-permute-done.64
  146.5 2.1 collective-permute-start.108
  148.6 1.7 collective-permute-done.65
  151.5 1.5 collective-permute-start.80
  153.8 1.9 collective-permute-start.109
  157.9 1.4 collective-permute-start.81
  164.6 1.3 collective-permute-done.96.refs_7_
  193.6 3.8 %tiles_2_0.1 = (f32[1024,256]{1,0:T(8,128)}, f32[128,256]{1,0:T(8,128)S(1)}, f32[128,256]{1,0:T(8,128)S(1)}, f32[6,128,256]{2,1,0:T(8,128)S(1)}, f32[6,128,256]{2,1,0:T(8,128)S(1)}, /*index=5*/f32[2,128,256]{2,1,0:T(8,128)S(1)}) custom-call(s32[3,2,16]{2,1,0:T(2,128)S(1)} %bitcast.186, s32[3]{0:T(128)S(1)} %bitcast.192, s32[1]{0:T(128)} %bitcast.2.refs_2_.refs_0_, ...), custom_call_target="tpu_custom_call" | custom-call | flops 201326592 | bytes 8388608 | tf_op jit(solution)/shard_map/tiles_2_0/pallas_call | solution.py:112
  197.4 3.6 %tiles_2_1.1 = (f32[1024,256]{1,0:T(8,128)}, f32[128,256]{1,0:T(8,128)S(1)}, f32[128,256]{1,0:T(8,128)S(1)}, f32[6,128,256]{2,1,0:T(8,128)S(1)}, f32[6,128,256]{2,1,0:T(8,128)S(1)}, /*index=5*/f32[2,128,256]{2,1,0:T(8,128)S(1)}) custom-call(s32[3,2,16]{2,1,0:T(2,128)S(1)} %bitcast.187, s32[3]{0:T(128)S(1)} %bitcast.193, ...), custom_call_target="tpu_custom_call", output_to_operand_aliasing={{0}: (4, {})} | custom-call | flops 201326592 | bytes 8388608 | tf_op jit(solution)/shard_map/tiles_2_1/pallas_call | solution.py:112
  203.2 1.7 collective-permute-start.116
  206.9 1.5 collective-permute-start.145
  210.0 1.4 collective-permute-start.117
  211.4 1.4 collective-permute-start.131
  212.8 1.4 collective-permute-done.145
  215.2 1.3 collective-permute-start.160
  228.1 1.8 collective-permute-done.119
  239.2 1.5 collective-permute-start.164
  244.3 3.4 %collective-permute-done.122 = f32[128,256]{1,0:T(8,128)S(1)} collective-permute-done((f32[128,256]{1,0:T(8,128)S(1)}, f32[128,256]{1,0:T(8,128)S(1)}, u32[]{:S(2)}, u32[]{:S(2)}) %collective-permute-start.122) | collective-permute-done | bytes 131104 | tf_op jit(solution)/shard_map/ppermute | solution.py:233
  261.5 1.5 collective-permute-start.139
  269.2 1.3 collective-permute-start.154
  270.8 1.5 collective-permute-start.168
  287.5 1.9 collective-permute-done.143.refs_16_
  289.4 1.4 lay_0.1.refs_1_
  291.5 1.4 lay_1.1
  (388 shorter events, 175.2 us)
Async XLA Ops:
  7.0 10.2 %collective-permute-start.1 = (f32[128,256]{1,0:T(8,128)S(1)}, f32[128,256]{1,0:T(8,128)S(1)}, u32[]{:S(2)}, u32[]{:S(2)}) collective-permute-start(f32[128,256]{1,0:T(8,128)S(1)} %get-tuple-element.41), channel_id=1, source_target_pairs={{0,2},{2,4},{4,6},{6,7},{7,5},{5,3},{3,1},{1,0},{8,10},{10,12},{12... | collective-permute-start | bytes 393224 | tf_op jit(solution)/shard_map/ppermute | solution.py:233
  9.3 8.0 %collective-permute-start.15 = (f32[128,256]{1,0:T(8,128)S(1)}, f32[128,256]{1,0:T(8,128)S(1)}, u32[]{:S(2)}, u32[]{:S(2)}) collective-permute-start(f32[128,256]{1,0:T(8,128)S(1)} %get-tuple-element.43), channel_id=1, source_target_pairs={{0,1},{2,0},{4,2},{6,4},{7,6},{5,7},{3,5},{1,3},{8,9},{10,8},{12,1... | collective-permute-start | bytes 393224 | tf_op jit(solution)/shard_map/ppermute | solution.py:233
  10.9 16.3 %collective-permute-start = (f32[2,128,256]{2,1,0:T(8,128)S(1)}, f32[2,128,256]{2,1,0:T(8,128)S(1)}, u32[]{:S(2)}, u32[]{:S(2)}) collective-permute-start(f32[2,128,256]{2,1,0:T(8,128)S(1)} %get-tuple-element.40), channel_id=1, source_target_pairs={{0,24},{8,0},{16,8},{24,16},{1,25},{9,1},{17,9},{25,17},{2,26},{10... | collective-permute-start | bytes 786440 | tf_op jit(solution)/shard_map/ppermute | solution.py:220
  17.3 40.3 %collective-permute-start.29 = (f32[2,128,256]{2,1,0:T(8,128)S(1)}, f32[2,128,256]{2,1,0:T(8,128)S(1)}, u32[]{:S(2)}, u32[]{:S(2)}) collective-permute-start(f32[2,128,256]{2,1,0:T(8,128)S(1)} %get-tuple-element.46), channel_id=1, source_target_pairs={{0,24},{8,0},{16,8},{24,16},{1,25},{9,1},{17,9},{25,17},{2,26},{10... | collective-permute-start | bytes 786440 | tf_op jit(solution)/shard_map/ppermute | solution.py:220
  23.3 6.6 %collective-permute-start.45 = (f32[128,256]{1,0:T(8,128)S(1)}, f32[128,256]{1,0:T(8,128)S(1)}, u32[]{:S(2)}, u32[]{:S(2)}) collective-permute-start(f32[128,256]{1,0:T(8,128)S(1)} %bitcast_add_fusion.53), channel_id=1, source_target_pairs={{0,1},{2,0},{4,2},{6,4},{7,6},{5,7},{3,5},{1,3},{8,9},{10,8},{12,1... | collective-permute-start | bytes 393224 | tf_op jit(solution)/shard_map/ppermute | solution.py:233
  27.2 6.3 %collective-permute-start.17 = (f32[128,256]{1,0:T(8,128)S(1)}, f32[128,256]{1,0:T(8,128)S(1)}, u32[]{:S(2)}, u32[]{:S(2)}) collective-permute-start(f32[128,256]{1,0:T(8,128)S(1)} %bitcast_add_fusion.64), channel_id=1, source_target_pairs={{0,1},{2,0},{4,2},{6,4},{7,6},{5,7},{3,5},{1,3},{8,9},{10,8},{12,1... | collective-permute-start | bytes 393224 | tf_op jit(solution)/shard_map/ppermute | solution.py:233
  27.7 6.8 %collective-permute-start.32 = (f32[128,256]{1,0:T(8,128)S(1)}, f32[128,256]{1,0:T(8,128)S(1)}, u32[]{:S(2)}, u32[]{:S(2)}) collective-permute-start(f32[128,256]{1,0:T(8,128)S(1)} %bitcast_add_fusion.58), channel_id=1, source_target_pairs={{0,2},{2,4},{4,6},{6,7},{7,5},{5,3},{3,1},{1,0},{8,10},{10,12},{12... | collective-permute-start | bytes 393224 | tf_op jit(solution)/shard_map/ppermute | solution.py:233
  29.9 6.5 %collective-permute-start.46 = (f32[128,256]{1,0:T(8,128)S(1)}, f32[128,256]{1,0:T(8,128)S(1)}, u32[]{:S(2)}, u32[]{:S(2)}) collective-permute-start(f32[128,256]{1,0:T(8,128)S(1)} %bitcast_add_fusion.52), channel_id=1, source_target_pairs={{0,1},{2,0},{4,2},{6,4},{7,6},{5,7},{3,5},{1,3},{8,9},{10,8},{12,1... | collective-permute-start | bytes 393224 | tf_op jit(solution)/shard_map/ppermute | solution.py:233
  34.6 6.6 %collective-permute-start.33 = (f32[128,256]{1,0:T(8,128)S(1)}, f32[128,256]{1,0:T(8,128)S(1)}, u32[]{:S(2)}, u32[]{:S(2)}) collective-permute-start(f32[128,256]{1,0:T(8,128)S(1)} %bitcast_add_fusion.57), channel_id=1, source_target_pairs={{0,2},{2,4},{4,6},{6,7},{7,5},{5,3},{3,1},{1,0},{8,10},{10,12},{12... | collective-permute-start | bytes 393224 | tf_op jit(solution)/shard_map/ppermute | solution.py:233
  36.4 6.5 %collective-permute-start.47 = (f32[128,256]{1,0:T(8,128)S(1)}, f32[128,256]{1,0:T(8,128)S(1)}, u32[]{:S(2)}, u32[]{:S(2)}) collective-permute-start(f32[128,256]{1,0:T(8,128)S(1)} %bitcast_add_fusion.51), channel_id=1, source_target_pairs={{0,1},{2,0},{4,2},{6,4},{7,6},{5,7},{3,5},{1,3},{8,9},{10,8},{12,1... | collective-permute-start | bytes 393224 | tf_op jit(solution)/shard_map/ppermute | solution.py:233
  39.3 6.4 %collective-permute-start.19 = (f32[128,256]{1,0:T(8,128)S(1)}, f32[128,256]{1,0:T(8,128)S(1)}, u32[]{:S(2)}, u32[]{:S(2)}) collective-permute-start(f32[128,256]{1,0:T(8,128)S(1)} %bitcast_add_fusion.62), channel_id=1, source_target_pairs={{0,1},{2,0},{4,2},{6,4},{7,6},{5,7},{3,5},{1,3},{8,9},{10,8},{12,1... | collective-permute-start | bytes 393224 | tf_op jit(solution)/shard_map/ppermute | solution.py:233
  57.9 6.5 %collective-permute-start.37 = (f32[128,256]{1,0:T(8,128)S(1)}, f32[128,256]{1,0:T(8,128)S(1)}, u32[]{:S(2)}, u32[]{:S(2)}) collective-permute-start(f32[128,256]{1,0:T(8,128)S(1)} %add.278.refs_5_), channel_id=1, source_target_pairs={{0,2},{2,4},{4,6},{6,7},{7,5},{5,3},{3,1},{1,0},{8,10},{10,12},{12... | collective-permute-start | bytes 393224 | tf_op jit(solution)/shard_map/ppermute | solution.py:237
  59.2 6.4 %collective-permute-start.51 = (f32[128,256]{1,0:T(8,128)S(1)}, f32[128,256]{1,0:T(8,128)S(1)}, u32[]{:S(2)}, u32[]{:S(2)}) collective-permute-start(f32[128,256]{1,0:T(8,128)S(1)} %add.285.refs_13_), channel_id=1, source_target_pairs={{0,1},{2,0},{4,2},{6,4},{7,6},{5,7},{3,5},{1,3},{8,9},{10,8},{12,1... | collective-permute-start | bytes 393224 | tf_op jit(solution)/shard_map/ppermute | solution.py:237
  64.4 6.5 %collective-permute-start.38 = (f32[128,256]{1,0:T(8,128)S(1)}, f32[128,256]{1,0:T(8,128)S(1)}, u32[]{:S(2)}, u32[]{:S(2)}) collective-permute-start(f32[128,256]{1,0:T(8,128)S(1)} %collective-permute-done.37.refs_6_), channel_id=1, source_target_pairs={{0,2},{2,4},{4,6},{6,7},{7,5},{5,3},{3,1},{1,0},{8,10},{10,12},{12... | collective-permute-start | bytes 393224 | tf_op jit(solution)/shard_map/ppermute | solution.py:237
  68.5 6.4 %collective-permute-start.24 = (f32[128,256]{1,0:T(8,128)S(1)}, f32[128,256]{1,0:T(8,128)S(1)}, u32[]{:S(2)}, u32[]{:S(2)}) collective-permute-start(f32[128,256]{1,0:T(8,128)S(1)} %collective-permute-done.23.refs_14_), channel_id=1, source_target_pairs={{0,1},{2,0},{4,2},{6,4},{7,6},{5,7},{3,5},{1,3},{8,9},{10,8},{12,1... | collective-permute-start | bytes 393224 | tf_op jit(solution)/shard_map/ppermute | solution.py:237
  72.0 6.4 %collective-permute-start.53 = (f32[128,256]{1,0:T(8,128)S(1)}, f32[128,256]{1,0:T(8,128)S(1)}, u32[]{:S(2)}, u32[]{:S(2)}) collective-permute-start(f32[128,256]{1,0:T(8,128)S(1)} %collective-permute-done.52.refs_15_), channel_id=1, source_target_pairs={{0,1},{2,0},{4,2},{6,4},{7,6},{5,7},{3,5},{1,3},{8,9},{10,8},{12,1... | collective-permute-start | bytes 393224 | tf_op jit(solution)/shard_map/ppermute | solution.py:237
  73.8 6.5 %collective-permute-start.11 = (f32[128,256]{1,0:T(8,128)S(1)}, f32[128,256]{1,0:T(8,128)S(1)}, u32[]{:S(2)}, u32[]{:S(2)}) collective-permute-start(f32[128,256]{1,0:T(8,128)S(1)} %collective-permute-done.10.refs_7_), channel_id=1, source_target_pairs={{0,2},{2,4},{4,6},{6,7},{7,5},{5,3},{3,1},{1,0},{8,10},{10,12},{12... | collective-permute-start | bytes 393224 | tf_op jit(solution)/shard_map/ppermute | solution.py:237
  90.4 6.4 %collective-permute-start.56 = (f32[128,256]{1,0:T(8,128)S(1)}, f32[128,256]{1,0:T(8,128)S(1)}, u32[]{:S(2)}, u32[]{:S(2)}) collective-permute-start(f32[128,256]{1,0:T(8,128)S(1)} %collective-permute-done.55.refs_18_), channel_id=1, source_target_pairs={{0,1},{2,0},{4,2},{6,4},{7,6},{5,7},{3,5},{1,3},{8,9},{10,8},{12,1... | collective-permute-start | bytes 393224 | tf_op jit(solution)/shard_map/ppermute | solution.py:237
  106.2 6.7 %collective-permute-start.59 = (f32[128,256]{1,0:T(8,128)S(1)}, f32[128,256]{1,0:T(8,128)S(1)}, u32[]{:S(2)}, u32[]{:S(2)}) collective-permute-start(f32[128,256]{1,0:T(8,128)S(1)} %get-tuple-element.53), channel_id=1, source_target_pairs={{0,2},{2,4},{4,6},{6,7},{7,5},{5,3},{3,1},{1,0},{8,10},{10,12},{12... | collective-permute-start | bytes 393224 | tf_op jit(solution)/shard_map/ppermute | solution.py:233
  108.6 44.4 %collective-permute-start.87 = (f32[2,128,256]{2,1,0:T(8,128)S(1)}, f32[2,128,256]{2,1,0:T(8,128)S(1)}, u32[]{:S(2)}, u32[]{:S(2)}) collective-permute-start(f32[2,128,256]{2,1,0:T(8,128)S(1)} %get-tuple-element.58), channel_id=1, source_target_pairs={{0,24},{8,0},{16,8},{24,16},{1,25},{9,1},{17,9},{25,17},{2,26},{10... | collective-permute-start | bytes 786440 | tf_op jit(solution)/shard_map/ppermute | solution.py:220
  119.5 6.9 %collective-permute-start.61 = (f32[128,256]{1,0:T(8,128)S(1)}, f32[128,256]{1,0:T(8,128)S(1)}, u32[]{:S(2)}, u32[]{:S(2)}) collective-permute-start(f32[128,256]{1,0:T(8,128)S(1)} %bitcast_add_fusion.46), channel_id=1, source_target_pairs={{0,2},{2,4},{4,6},{6,7},{7,5},{5,3},{3,1},{1,0},{8,10},{10,12},{12... | collective-permute-start | bytes 393224 | tf_op jit(solution)/shard_map/ppermute | solution.py:233
  121.2 6.4 %collective-permute-start.75 = (f32[128,256]{1,0:T(8,128)S(1)}, f32[128,256]{1,0:T(8,128)S(1)}, u32[]{:S(2)}, u32[]{:S(2)}) collective-permute-start(f32[128,256]{1,0:T(8,128)S(1)} %bitcast_add_fusion.40), channel_id=1, source_target_pairs={{0,1},{2,0},{4,2},{6,4},{7,6},{5,7},{3,5},{1,3},{8,9},{10,8},{12,1... | collective-permute-start | bytes 393224 | tf_op jit(solution)/shard_map/ppermute | solution.py:233
  126.4 6.4 %collective-permute-start.62 = (f32[128,256]{1,0:T(8,128)S(1)}, f32[128,256]{1,0:T(8,128)S(1)}, u32[]{:S(2)}, u32[]{:S(2)}) collective-permute-start(f32[128,256]{1,0:T(8,128)S(1)} %bitcast_add_fusion.45), channel_id=1, source_target_pairs={{0,2},{2,4},{4,6},{6,7},{7,5},{5,3},{3,1},{1,0},{8,10},{10,12},{12... | collective-permute-start | bytes 393224 | tf_op jit(solution)/shard_map/ppermute | solution.py:233
  127.7 6.5 %collective-permute-start.76 = (f32[128,256]{1,0:T(8,128)S(1)}, f32[128,256]{1,0:T(8,128)S(1)}, u32[]{:S(2)}, u32[]{:S(2)}) collective-permute-start(f32[128,256]{1,0:T(8,128)S(1)} %bitcast_add_fusion.39), channel_id=1, source_target_pairs={{0,1},{2,0},{4,2},{6,4},{7,6},{5,7},{3,5},{1,3},{8,9},{10,8},{12,1... | collective-permute-start | bytes 393224 | tf_op jit(solution)/shard_map/ppermute | solution.py:233
  132.9 6.4 %collective-permute-start.63 = (f32[128,256]{1,0:T(8,128)S(1)}, f32[128,256]{1,0:T(8,128)S(1)}, u32[]{:S(2)}, u32[]{:S(2)}) collective-permute-start(f32[128,256]{1,0:T(8,128)S(1)} %bitcast_add_fusion.44), channel_id=1, source_target_pairs={{0,2},{2,4},{4,6},{6,7},{7,5},{5,3},{3,1},{1,0},{8,10},{10,12},{12... | collective-permute-start | bytes 393224 | tf_op jit(solution)/shard_map/ppermute | solution.py:233
  134.2 6.4 %collective-permute-start.77 = (f32[128,256]{1,0:T(8,128)S(1)}, f32[128,256]{1,0:T(8,128)S(1)}, u32[]{:S(2)}, u32[]{:S(2)}) collective-permute-start(f32[128,256]{1,0:T(8,128)S(1)} %bitcast_add_fusion.38), channel_id=1, source_target_pairs={{0,1},{2,0},{4,2},{6,4},{7,6},{5,7},{3,5},{1,3},{8,9},{10,8},{12,1... | collective-permute-start | bytes 393224 | tf_op jit(solution)/shard_map/ppermute | solution.py:233
  135.6 6.4 %collective-permute-start.93 = (f32[128,256]{1,0:T(8,128)S(1)}, f32[128,256]{1,0:T(8,128)S(1)}, u32[]{:S(2)}, u32[]{:S(2)}) collective-permute-start(f32[128,256]{1,0:T(8,128)S(1)} %bitcast_add_fusion.31), channel_id=1, source_target_pairs={{0,2},{2,4},{4,6},{6,7},{7,5},{5,3},{3,1},{1,0},{8,10},{10,12},{12... | collective-permute-start | bytes 393224 | tf_op jit(solution)/shard_map/ppermute | solution.py:233
  137.4 9.1 %collective-permute-start.107 = (f32[128,256]{1,0:T(8,128)S(1)}, f32[128,256]{1,0:T(8,128)S(1)}, u32[]{:S(2)}, u32[]{:S(2)}) collective-permute-start(f32[128,256]{1,0:T(8,128)S(1)} %bitcast_add_fusion.25), channel_id=1, source_target_pairs={{0,1},{2,0},{4,2},{6,4},{7,6},{5,7},{3,5},{1,3},{8,9},{10,8},{12,1... | collective-permute-start | bytes 393224 | tf_op jit(solution)/shard_map/ppermute | solution.py:233
  142.1 10.9 %collective-permute-start.94 = (f32[128,256]{1,0:T(8,128)S(1)}, f32[128,256]{1,0:T(8,128)S(1)}, u32[]{:S(2)}, u32[]{:S(2)}) collective-permute-start(f32[128,256]{1,0:T(8,128)S(1)} %bitcast_add_fusion.30), channel_id=1, source_target_pairs={{0,26},{2,28},{4,30},{6,31},{7,29},{5,27},{3,25},{1,24},{8,2},{10,... | collective-permute-start | bytes 393224 | tf_op jit(solution)/shard_map/ppermute | solution.py:231
  146.5 7.3 %collective-permute-start.108 = (f32[128,256]{1,0:T(8,128)S(1)}, f32[128,256]{1,0:T(8,128)S(1)}, u32[]{:S(2)}, u32[]{:S(2)}) collective-permute-start(f32[128,256]{1,0:T(8,128)S(1)} %bitcast_add_fusion.24), channel_id=1, source_target_pairs={{0,25},{2,24},{4,26},{6,28},{7,30},{5,31},{3,29},{1,27},{8,1},{10,... | collective-permute-start | bytes 393224 | tf_op jit(solution)/shard_map/ppermute | solution.py:231
  150.3 6.4 %collective-permute-start.66 = (f32[128,256]{1,0:T(8,128)S(1)}, f32[128,256]{1,0:T(8,128)S(1)}, u32[]{:S(2)}, u32[]{:S(2)}) collective-permute-start(f32[128,256]{1,0:T(8,128)S(1)} %add.292.refs_4_), channel_id=1, source_target_pairs={{0,2},{2,4},{4,6},{6,7},{7,5},{5,3},{3,1},{1,0},{8,10},{10,12},{12... | collective-permute-start | bytes 393224 | tf_op jit(solution)/shard_map/ppermute | solution.py:237
  151.5 6.4 %collective-permute-start.80 = (f32[128,256]{1,0:T(8,128)S(1)}, f32[128,256]{1,0:T(8,128)S(1)}, u32[]{:S(2)}, u32[]{:S(2)}) collective-permute-start(f32[128,256]{1,0:T(8,128)S(1)} %add.299.refs_12_), channel_id=1, source_target_pairs={{0,1},{2,0},{4,2},{6,4},{7,6},{5,7},{3,5},{1,3},{8,9},{10,8},{12,1... | collective-permute-start | bytes 393224 | tf_op jit(solution)/shard_map/ppermute | solution.py:237
  153.0 6.5 %collective-permute-start.95 = (f32[128,256]{1,0:T(8,128)S(1)}, f32[128,256]{1,0:T(8,128)S(1)}, u32[]{:S(2)}, u32[]{:S(2)}) collective-permute-start(f32[128,256]{1,0:T(8,128)S(1)} %add.306.refs_5_), channel_id=1, source_target_pairs={{0,2},{2,4},{4,6},{6,7},{7,5},{5,3},{3,1},{1,0},{8,10},{10,12},{12... | collective-permute-start | bytes 393224 | tf_op jit(solution)/shard_map/ppermute | solution.py:237
  153.8 6.9 %collective-permute-start.109 = (f32[128,256]{1,0:T(8,128)S(1)}, f32[128,256]{1,0:T(8,128)S(1)}, u32[]{:S(2)}, u32[]{:S(2)}) collective-permute-start(f32[128,256]{1,0:T(8,128)S(1)} %add.313.refs_13_), channel_id=1, source_target_pairs={{0,1},{2,0},{4,2},{6,4},{7,6},{5,7},{3,5},{1,3},{8,9},{10,8},{12,1... | collective-permute-start | bytes 393224 | tf_op jit(solution)/shard_map/ppermute | solution.py:237
  159.5 6.4 %collective-permute-start.96 = (f32[128,256]{1,0:T(8,128)S(1)}, f32[128,256]{1,0:T(8,128)S(1)}, u32[]{:S(2)}, u32[]{:S(2)}) collective-permute-start(f32[128,256]{1,0:T(8,128)S(1)} %collective-permute-done.95.refs_6_), channel_id=1, source_target_pairs={{0,2},{2,4},{4,6},{6,7},{7,5},{5,3},{3,1},{1,0},{8,10},{10,12},{12... | collective-permute-start | bytes 393224 | tf_op jit(solution)/shard_map/ppermute | solution.py:237
  160.7 6.4 %collective-permute-start.110 = (f32[128,256]{1,0:T(8,128)S(1)}, f32[128,256]{1,0:T(8,128)S(1)}, u32[]{:S(2)}, u32[]{:S(2)}) collective-permute-start(f32[128,256]{1,0:T(8,128)S(1)} %collective-permute-done.109.refs_14_), channel_id=1, source_target_pairs={{0,1},{2,0},{4,2},{6,4},{7,6},{5,7},{3,5},{1,3},{8,9},{10,8},{12,1... | collective-permute-start | bytes 393224 | tf_op jit(solution)/shard_map/ppermute | solution.py:237
  162.4 6.4 %collective-permute-start.68 = (f32[128,256]{1,0:T(8,128)S(1)}, f32[128,256]{1,0:T(8,128)S(1)}, u32[]{:S(2)}, u32[]{:S(2)}) collective-permute-start(f32[128,256]{1,0:T(8,128)S(1)} %collective-permute-done.67.refs_6_), channel_id=1, source_target_pairs={{0,2},{2,4},{4,6},{6,7},{7,5},{5,3},{3,1},{1,0},{8,10},{10,12},{12... | collective-permute-start | bytes 393224 | tf_op jit(solution)/shard_map/ppermute | solution.py:237
  163.5 6.4 %collective-permute-start.82 = (f32[128,256]{1,0:T(8,128)S(1)}, f32[128,256]{1,0:T(8,128)S(1)}, u32[]{:S(2)}, u32[]{:S(2)}) collective-permute-start(f32[128,256]{1,0:T(8,128)S(1)} %collective-permute-done.81.refs_14_), channel_id=1, source_target_pairs={{0,1},{2,0},{4,2},{6,4},{7,6},{5,7},{3,5},{1,3},{8,9},{10,8},{12,1... | collective-permute-start | bytes 393224 | tf_op jit(solution)/shard_map/ppermute | solution.py:237
  190.6 6.7 %collective-permute-start.101 = (f32[128,256]{1,0:T(8,128)S(1)}, f32[128,256]{1,0:T(8,128)S(1)}, u32[]{:S(2)}, u32[]{:S(2)}) collective-permute-start(f32[128,256]{1,0:T(8,128)S(1)} %collective-permute-done.100.refs_11_), channel_id=1, source_target_pairs={{0,2},{2,4},{4,6},{6,7},{7,5},{5,3},{3,1},{1,0},{8,10},{10,12},{12... | collective-permute-start | bytes 393224 | tf_op jit(solution)/shard_map/ppermute | solution.py:237
  202.0 7.2 %collective-permute-start.158 = (f32[128,256]{1,0:T(8,128)S(1)}, f32[128,256]{1,0:T(8,128)S(1)}, u32[]{:S(2)}, u32[]{:S(2)}) collective-permute-start(f32[128,256]{1,0:T(8,128)S(1)} %get-tuple-element.72), channel_id=1, source_target_pairs={{0,1},{2,0},{4,2},{6,4},{7,6},{5,7},{3,5},{1,3},{8,9},{10,8},{12,1... | collective-permute-start | bytes 393224 | tf_op jit(solution)/shard_map/ppermute | solution.py:233
  203.2 6.8 %collective-permute-start.116 = (f32[128,256]{1,0:T(8,128)S(1)}, f32[128,256]{1,0:T(8,128)S(1)}, u32[]{:S(2)}, u32[]{:S(2)}) collective-permute-start(f32[128,256]{1,0:T(8,128)S(1)} %get-tuple-element.65), channel_id=1, source_target_pairs={{0,2},{2,4},{4,6},{6,7},{7,5},{5,3},{3,1},{1,0},{8,10},{10,12},{12... | collective-permute-start | bytes 393224 | tf_op jit(solution)/shard_map/ppermute | solution.py:233
  204.9 6.5 %collective-permute-start.130 = (f32[128,256]{1,0:T(8,128)S(1)}, f32[128,256]{1,0:T(8,128)S(1)}, u32[]{:S(2)}, u32[]{:S(2)}) collective-permute-start(f32[128,256]{1,0:T(8,128)S(1)} %get-tuple-element.67), channel_id=1, source_target_pairs={{0,1},{2,0},{4,2},{6,4},{7,6},{5,7},{3,5},{1,3},{8,9},{10,8},{12,1... | collective-permute-start | bytes 393224 | tf_op jit(solution)/shard_map/ppermute | solution.py:233
  206.9 7.3 %collective-permute-start.145 = (f32[128,256]{1,0:T(8,128)S(1)}, f32[128,256]{1,0:T(8,128)S(1)}, u32[]{:S(2)}, u32[]{:S(2)}) collective-permute-start(f32[128,256]{1,0:T(8,128)S(1)} %bitcast_add_fusion.11), channel_id=1, source_target_pairs={{0,2},{2,4},{4,6},{6,7},{7,5},{5,3},{3,1},{1,0},{8,10},{10,12},{12... | collective-permute-start | bytes 393224 | tf_op jit(solution)/shard_map/ppermute | solution.py:233
  210.0 7.0 %collective-permute-start.117 = (f32[128,256]{1,0:T(8,128)S(1)}, f32[128,256]{1,0:T(8,128)S(1)}, u32[]{:S(2)}, u32[]{:S(2)}) collective-permute-start(f32[128,256]{1,0:T(8,128)S(1)} %bitcast_add_fusion.23), channel_id=1, source_target_pairs={{0,2},{2,4},{4,6},{6,7},{7,5},{5,3},{3,1},{1,0},{8,10},{10,12},{12... | collective-permute-start | bytes 393224 | tf_op jit(solution)/shard_map/ppermute | solution.py:233
  211.4 6.6 %collective-permute-start.131 = (f32[128,256]{1,0:T(8,128)S(1)}, f32[128,256]{1,0:T(8,128)S(1)}, u32[]{:S(2)}, u32[]{:S(2)}) collective-permute-start(f32[128,256]{1,0:T(8,128)S(1)} %bitcast_add_fusion.17), channel_id=1, source_target_pairs={{0,1},{2,0},{4,2},{6,4},{7,6},{5,7},{3,5},{1,3},{8,9},{10,8},{12,1... | collective-permute-start | bytes 393224 | tf_op jit(solution)/shard_map/ppermute | solution.py:233
  215.2 6.4 %collective-permute-start.160 = (f32[128,256]{1,0:T(8,128)S(1)}, f32[128,256]{1,0:T(8,128)S(1)}, u32[]{:S(2)}, u32[]{:S(2)}) collective-permute-start(f32[128,256]{1,0:T(8,128)S(1)} %bitcast_add_fusion.4), channel_id=1, source_target_pairs={{0,1},{2,0},{4,2},{6,4},{7,6},{5,7},{3,5},{1,3},{8,9},{10,8},{12,1... | collective-permute-start | bytes 393224 | tf_op jit(solution)/shard_map/ppermute | solution.py:233
  218.0 6.4 %collective-permute-start.132 = (f32[128,256]{1,0:T(8,128)S(1)}, f32[128,256]{1,0:T(8,128)S(1)}, u32[]{:S(2)}, u32[]{:S(2)}) collective-permute-start(f32[128,256]{1,0:T(8,128)S(1)} %bitcast_add_fusion.16), channel_id=1, source_target_pairs={{0,1},{2,0},{4,2},{6,4},{7,6},{5,7},{3,5},{1,3},{8,9},{10,8},{12,1... | collective-permute-start | bytes 393224 | tf_op jit(solution)/shard_map/ppermute | solution.py:233
  223.0 6.9 %collective-permute-start.119 = (f32[128,256]{1,0:T(8,128)S(1)}, f32[128,256]{1,0:T(8,128)S(1)}, u32[]{:S(2)}, u32[]{:S(2)}) collective-permute-start(f32[128,256]{1,0:T(8,128)S(1)} %bitcast_add_fusion.21), channel_id=1, source_target_pairs={{0,2},{2,4},{4,6},{6,7},{7,5},{5,3},{3,1},{1,0},{8,10},{10,12},{12... | collective-permute-start | bytes 393224 | tf_op jit(solution)/shard_map/ppermute | solution.py:233
  224.5 6.4 %collective-permute-start.133 = (f32[128,256]{1,0:T(8,128)S(1)}, f32[128,256]{1,0:T(8,128)S(1)}, u32[]{:S(2)}, u32[]{:S(2)}) collective-permute-start(f32[128,256]{1,0:T(8,128)S(1)} %bitcast_add_fusion.15), channel_id=1, source_target_pairs={{0,1},{2,0},{4,2},{6,4},{7,6},{5,7},{3,5},{1,3},{8,9},{10,8},{12,1... | collective-permute-start | bytes 393224 | tf_op jit(solution)/shard_map/ppermute | solution.py:233
  225.8 7.0 %collective-permute-start.148 = (f32[128,256]{1,0:T(8,128)S(1)}, f32[128,256]{1,0:T(8,128)S(1)}, u32[]{:S(2)}, u32[]{:S(2)}) collective-permute-start(f32[128,256]{1,0:T(8,128)S(1)} %bitcast_add_fusion.8), channel_id=1, source_target_pairs={{0,2},{2,4},{4,6},{6,7},{7,5},{5,3},{3,1},{1,0},{8,10},{10,12},{12... | collective-permute-start | bytes 393224 | tf_op jit(solution)/shard_map/ppermute | solution.py:233
  227.3 6.4 %collective-permute-start.162 = (f32[128,256]{1,0:T(8,128)S(1)}, f32[128,256]{1,0:T(8,128)S(1)}, u32[]{:S(2)}, u32[]{:S(2)}) collective-permute-start(f32[128,256]{1,0:T(8,128)S(1)} %bitcast_add_fusion.2), channel_id=1, source_target_pairs={{0,1},{2,0},{4,2},{6,4},{7,6},{5,7},{3,5},{1,3},{8,9},{10,8},{12,1... | collective-permute-start | bytes 393224 | tf_op jit(solution)/shard_map/ppermute | solution.py:233
  237.0 6.4 %collective-permute-start.135 = (f32[128,256]{1,0:T(8,128)S(1)}, f32[128,256]{1,0:T(8,128)S(1)}, u32[]{:S(2)}, u32[]{:S(2)}) collective-permute-start(f32[128,256]{1,0:T(8,128)S(1)} %bitcast_add_fusion.13), channel_id=1, source_target_pairs={{0,1},{2,0},{4,2},{6,4},{7,6},{5,7},{3,5},{1,3},{8,9},{10,8},{12,1... | collective-permute-start | bytes 393224 | tf_op jit(solution)/shard_map/ppermute | solution.py:233
  238.1 12.4 %collective-permute-start.150 = (f32[128,256]{1,0:T(8,128)S(1)}, f32[128,256]{1,0:T(8,128)S(1)}, u32[]{:S(2)}, u32[]{:S(2)}) collective-permute-start(f32[128,256]{1,0:T(8,128)S(1)} %bitcast_add_fusion.6), channel_id=1, source_target_pairs={{0,2},{2,4},{4,6},{6,7},{7,5},{5,3},{3,1},{1,0},{8,10},{10,12},{12... | collective-permute-start | bytes 393224 | tf_op jit(solution)/shard_map/ppermute | solution.py:233
  239.2 12.5 %collective-permute-start.164 = (f32[128,256]{1,0:T(8,128)S(1)}, f32[128,256]{1,0:T(8,128)S(1)}, u32[]{:S(2)}, u32[]{:S(2)}) collective-permute-start(f32[128,256]{1,0:T(8,128)S(1)} %bitcast_add_fusion), channel_id=1, source_target_pairs={{0,1},{2,0},{4,2},{6,4},{7,6},{5,7},{3,5},{1,3},{8,9},{10,8},{12,1... | collective-permute-start | bytes 393224 | tf_op jit(solution)/shard_map/ppermute | solution.py:233
  241.1 6.6 %collective-permute-start.122 = (f32[128,256]{1,0:T(8,128)S(1)}, f32[128,256]{1,0:T(8,128)S(1)}, u32[]{:S(2)}, u32[]{:S(2)}) collective-permute-start(f32[128,256]{1,0:T(8,128)S(1)} %bitcast_add_fusion.18), channel_id=1, source_target_pairs={{0,2},{2,4},{4,6},{6,7},{7,5},{5,3},{3,1},{1,0},{8,10},{10,12},{12... | collective-permute-start | bytes 393224 | tf_op jit(solution)/shard_map/ppermute | solution.py:233
  249.3 6.4 %collective-permute-start.137 = (f32[128,256]{1,0:T(8,128)S(1)}, f32[128,256]{1,0:T(8,128)S(1)}, u32[]{:S(2)}, u32[]{:S(2)}) collective-permute-start(f32[128,256]{1,0:T(8,128)S(1)} %add.327.refs_9_), channel_id=1, source_target_pairs={{0,1},{2,0},{4,2},{6,4},{7,6},{5,7},{3,5},{1,3},{8,9},{10,8},{12,1... | collective-permute-start | bytes 393224 | tf_op jit(solution)/shard_map/ppermute | solution.py:237
  250.5 6.5 %collective-permute-start.151 = (f32[128,256]{1,0:T(8,128)S(1)}, f32[128,256]{1,0:T(8,128)S(1)}, u32[]{:S(2)}, u32[]{:S(2)}) collective-permute-start(f32[128,256]{1,0:T(8,128)S(1)} %add.334.refs_2_), channel_id=1, source_target_pairs={{0,2},{2,4},{4,6},{6,7},{7,5},{5,3},{3,1},{1,0},{8,10},{10,12},{12... | collective-permute-start | bytes 393224 | tf_op jit(solution)/shard_map/ppermute | solution.py:237
  251.7 6.8 %collective-permute-start.165 = (f32[128,256]{1,0:T(8,128)S(1)}, f32[128,256]{1,0:T(8,128)S(1)}, u32[]{:S(2)}, u32[]{:S(2)}) collective-permute-start(f32[128,256]{1,0:T(8,128)S(1)} %add.341.refs_10_), channel_id=1, source_target_pairs={{0,1},{2,0},{4,2},{6,4},{7,6},{5,7},{3,5},{1,3},{8,9},{10,8},{12,1... | collective-permute-start | bytes 393224 | tf_op jit(solution)/shard_map/ppermute | solution.py:237
  253.7 6.4 %collective-permute-start.124 = (f32[128,256]{1,0:T(8,128)S(1)}, f32[128,256]{1,0:T(8,128)S(1)}, u32[]{:S(2)}, u32[]{:S(2)}) collective-permute-start(f32[128,256]{1,0:T(8,128)S(1)} %collective-permute-done.123.refs_2_), channel_id=1, source_target_pairs={{0,2},{2,4},{4,6},{6,7},{7,5},{5,3},{3,1},{1,0},{8,10},{10,12},{12... | collective-permute-start | bytes 393224 | tf_op jit(solution)/shard_map/ppermute | solution.py:237
  257.0 6.4 %collective-permute-start.152 = (f32[128,256]{1,0:T(8,128)S(1)}, f32[128,256]{1,0:T(8,128)S(1)}, u32[]{:S(2)}, u32[]{:S(2)}) collective-permute-start(f32[128,256]{1,0:T(8,128)S(1)} %collective-permute-done.151.refs_3_), channel_id=1, source_target_pairs={{0,2},{2,4},{4,6},{6,7},{7,5},{5,3},{3,1},{1,0},{8,10},{10,12},{12... | collective-permute-start | bytes 393224 | tf_op jit(solution)/shard_map/ppermute | solution.py:237
  258.5 6.6 %collective-permute-start.166 = (f32[128,256]{1,0:T(8,128)S(1)}, f32[128,256]{1,0:T(8,128)S(1)}, u32[]{:S(2)}, u32[]{:S(2)}) collective-permute-start(f32[128,256]{1,0:T(8,128)S(1)} %collective-permute-done.165.refs_11_), channel_id=1, source_target_pairs={{0,1},{2,0},{4,2},{6,4},{7,6},{5,7},{3,5},{1,3},{8,9},{10,8},{12,1... | collective-permute-start | bytes 393224 | tf_op jit(solution)/shard_map/ppermute | solution.py:237
  261.5 6.4 %collective-permute-start.139 = (f32[128,256]{1,0:T(8,128)S(1)}, f32[128,256]{1,0:T(8,128)S(1)}, u32[]{:S(2)}, u32[]{:S(2)}) collective-permute-start(f32[128,256]{1,0:T(8,128)S(1)} %collective-permute-done.138.refs_11_), channel_id=1, source_target_pairs={{0,1},{2,0},{4,2},{6,4},{7,6},{5,7},{3,5},{1,3},{8,9},{10,8},{12,1... | collective-permute-start | bytes 393224 | tf_op jit(solution)/shard_map/ppermute | solution.py:237
  266.2 6.4 %collective-permute-start.126 = (f32[128,256]{1,0:T(8,128)S(1)}, f32[128,256]{1,0:T(8,128)S(1)}, u32[]{:S(2)}, u32[]{:S(2)}) collective-permute-start(f32[128,256]{1,0:T(8,128)S(1)} %collective-permute-done.125.refs_4_), channel_id=1, source_target_pairs={{0,2},{2,4},{4,6},{6,7},{7,5},{5,3},{3,1},{1,0},{8,10},{10,12},{12... | collective-permute-start | bytes 393224 | tf_op jit(solution)/shard_map/ppermute | solution.py:237
  268.0 6.6 %collective-permute-start.140 = (f32[128,256]{1,0:T(8,128)S(1)}, f32[128,256]{1,0:T(8,128)S(1)}, u32[]{:S(2)}, u32[]{:S(2)}) collective-permute-start(f32[128,256]{1,0:T(8,128)S(1)} %collective-permute-done.139.refs_12_), channel_id=1, source_target_pairs={{0,1},{2,0},{4,2},{6,4},{7,6},{5,7},{3,5},{1,3},{8,9},{10,8},{12,1... | collective-permute-start | bytes 393224 | tf_op jit(solution)/shard_map/ppermute | solution.py:237
  (113 other events, 655.9 us)

commit v4 on v3

--- a/solution.py
+++ b/solution.py
@@ -10,6 +10,7 @@
 RATE = 0.003
 KEEP = 1.0 - 0.003 * 0.05
 WAVES = 2
+FLOWS = 2 * WAVES
 GROUP = 4
 ANY = pl.BlockSpec(memory_space=pl.ANY)
 HBM = pl.BlockSpec(memory_space=pltpu.HBM)
@@ -17,14 +18,100 @@
 SMEM = pl.BlockSpec(memory_space=pltpu.SMEM)
 
 
-def tile_kernel(sub, wave, side, n_own, *refs):
-    fresh = sub == 0
+def tile_kernel(sub, side, n_own, *refs):
+    refs = list(refs)
+    coords, counts, place, users = (refs.pop(0) for _ in range(4))
+    slabs = [refs.pop(0) for _ in range(FLOWS * n_own)]
+    values, out_u = (refs.pop(0) for _ in range(2))
+    near = [refs.pop(0) for _ in range(FLOWS)]
+    far = [refs.pop(0) for _ in range(FLOWS)]
+    owns = [refs.pop(0) for _ in range(WAVES)]
+    held, grad, seen, sem = refs
+    here = place[0]
+    count = counts[sub]
+
+    copy = pltpu.make_async_copy(values.at[sub], seen, sem)
+    copy.start()
+    for i, tile in enumerate(slabs):
+        held[i] = tile[...]
+    grad[...] = jnp.zeros_like(grad)
+    copy.wait()
+    out_u[...] = users[...] * KEEP
+
+    def some(i, carry):
+        done = []
+        for j in range(GROUP):
+            at = i * GROUP + j
+            n = jnp.minimum(at, count - 1)
+            rate = jnp.where(at < count, RATE, 0.0)
+            a = coords[sub, 0, n]
+            b = coords[sub, 1, n]
+            owner = b >> 2
+            flow = b & 3
+            ahead = jnp.where((b & 1) == 0, here - owner, owner - here)
+            slot = flow * n_own + lax.rem(ahead + n_own, n_own)
+            rows = pl.ds(pl.multiple_of(a * side, side), side)
+            ua = users[rows, :].astype(jnp.bfloat16)
+            vb = held[slot].astype(jnp.bfloat16)
+            guess = lax.dot_general(
+                ua, vb, (((1,), (1,)), ((), ())), preferred_element_type=jnp.float32
+            )
+            resid = (seen[n].astype(jnp.float32) - guess).astype(jnp.bfloat16)
+            up = jnp.dot(resid, vb, preferred_element_type=jnp.float32)
+            ip = lax.dot_general(
+                resid, ua, (((0,), (0,)), ((), ())), preferred_element_type=jnp.float32
+            )
+            done.append((rows, slot, rate * up, rate * ip))
+        for rows, slot, up, ip in done:
+            out_u[rows, :] += up
+            grad[slot] += ip
+        return carry
+
+    lax.fori_loop(0, (count + GROUP - 1) // GROUP, some, 0)
+
+    for flow in range(FLOWS):
+        mine = flow * n_own
+        near[flow][...] = grad[mine + 1]
+        far[flow][...] = grad[mine + 2 : mine + n_own]
+        owns[flow // 2][flow & 1] = held[mine] * KEEP + grad[mine]
+
+
+def tile_step(sub, n_own, coords, counts, place, users, slabs, values):
+    side = values.shape[-1]
+    width = users.shape[1]
+
+    def tiles(*lead):
+        return jax.ShapeDtypeStruct((*lead, side, width), jnp.float32)
+
+    tails = (tiles(),) * FLOWS + (tiles(n_own - 2),) * FLOWS + (tiles(2),) * WAVES
+    return pl.pallas_call(
+        functools.partial(tile_kernel, sub, side, n_own),
+        out_shape=(jax.ShapeDtypeStruct(users.shape, jnp.float32), *tails),
+        in_specs=[SMEM, SMEM, SMEM, VMEM] + [VMEM] * len(slabs) + [HBM],
+        out_specs=(VMEM,) * (1 + len(tails)),
+        scratch_shapes=[
+            pltpu.VMEM((FLOWS * n_own, side, width), jnp.float32),
+            pltpu.VMEM((FLOWS * n_own, side, width), jnp.float32),
+            pltpu.VMEM(values.shape[1:], values.dtype),
+            pltpu.SemaphoreType.DMA,
+        ],
+        compiler_params=pltpu.CompilerParams(vmem_limit_bytes=24 * 2**20),
+        cost_estimate=pl.CostEstimate(
+            flops=16 * 3 * 2 * side * side * width,
+            bytes_accessed=16 * 2**20,
+            transcendentals=0,
+        ),
+        name=f"tiles_{sub}",
+    )(coords, counts, place, users, *slabs, values)
+
+
+def first_kernel(wave, side, n_own, *refs):
     refs = list(refs)
     coords, counts, place, users = (refs.pop(0) for _ in range(4))
     running = refs.pop(0) if wave else None
-    slabs = [refs.pop(0) for _ in range(1 if fresh else 2 * n_own)]
+    slab = refs.pop(0)
     values, out_u, near_f, near_b, far_f, far_b, own = (refs.pop(0) for _ in range(7))
-    held, grad, seen, order, sems = (refs.pop(0) for _ in range(5))
+    held, grad, seen, order, sems, mine = refs
 
     copies = []
 
@@ -33,26 +120,18 @@
         c.start()
         copies.append(c)
 
-    if fresh:
-        (mine,) = refs
-        copy(users, mine)
-        users = mine
-        for way in range(2):
-            copy(
-                slabs[0].at[:, 2 * wave + way],
-                held.at[pl.ds(way * n_own, n_own)],
-            )
-    copy(values.at[sub], seen)
-    if not fresh:
-        for i, tile in enumerate(slabs):
-            held[i] = tile[...]
+    copy(users, mine)
+    users = mine
+    for way in range(2):
+        copy(slab.at[:, 2 * wave + way], held.at[pl.ds(way * n_own, n_own)])
+    copy(values.at[0], seen)
     grad[...] = jnp.zeros_like(grad)
 
-    count = counts[sub]
+    count = counts[0]
 
     def gather(n, total):
         order[total] = n
-        hit = (n < count) & (((coords[sub, 1, n] >> 1) & 1) == wave)
+        hit = (n < count) & (((coords[0, 1, n] >> 1) & 1) == wave)
         return total + hit.astype(jnp.int32)
 
     total = lax.fori_loop(0, coords.shape[2], gather, 0)
@@ -67,13 +146,13 @@
             at = i * GROUP + j
             n = order[jnp.minimum(at, total - 1)]
             rate = jnp.where(at < total, RATE, 0.0)
-            a = coords[sub, 0, n]
-            b = coords[sub, 1, n]
+            a = coords[0, 0, n]
+            b = coords[0, 1, n]
             owner = b >> 2
             way = b & 1
             ahead = jnp.where(way == 0, here - owner, owner - here)
             slot = way * n_own + lax.rem(ahead + n_own, n_own)
-            source = way * n_own + owner if fresh else slot
+            source = way * n_own + owner
             rows = pl.ds(pl.multiple_of(a * side, side), side)
             ua = users[rows, :].astype(jnp.bfloat16)
             vb = held[source].astype(jnp.bfloat16)
@@ -98,11 +177,10 @@
     far_f[...] = grad[2:n_own]
     far_b[...] = grad[n_own + 2 : 2 * n_own]
     for way in range(2):
-        source = way * n_own + here if fresh else way * n_own
-        own[way] = held[source] * KEEP + grad[way * n_own]
-
-
-def tile_step(sub, wave, n_own, coords, counts, place, users, running, slabs, values):
+        own[way] = held[way * n_own + here] * KEEP + grad[way * n_own]
+
+
+def first_step(wave, n_own, coords, counts, place, users, running, slab, values):
     side = values.shape[-1]
     width = users.shape[1]
     tile = jax.ShapeDtypeStruct((side, width), jnp.float32)
@@ -110,7 +188,7 @@
     slots = 2 * n_own
     carried = (running,) if wave else ()
     return pl.pallas_call(
-        functools.partial(tile_kernel, sub, wave, side, n_own),
+        functools.partial(first_kernel, wave, side, n_own),
         out_shape=(
             jax.ShapeDtypeStruct(users.shape, jnp.float32),
             tile,
@@ -119,10 +197,7 @@
             far,
             jax.ShapeDtypeStruct((2, side, width), jnp.float32),
         ),
-        in_specs=[SMEM, SMEM, SMEM, VMEM if sub else HBM]
-        + [VMEM] * len(carried)
-        + [VMEM if sub else HBM] * len(slabs)
-        + [HBM],
+        in_specs=[SMEM, SMEM, SMEM, HBM] + [VMEM] * len(carried) + [HBM, HBM],
         out_specs=(VMEM,) * 6,
         input_output_aliases={4: 0} if wave else {},
         scratch_shapes=[
@@ -131,16 +206,16 @@
             pltpu.VMEM(values.shape[1:], values.dtype),
             pltpu.SMEM((coords.shape[2] + 1,), jnp.int32),
             pltpu.SemaphoreType.DMA((4,)),
-        ]
-        + ([] if sub else [pltpu.VMEM(users.shape, jnp.float32)]),
-        compiler_params=pltpu.CompilerParams(vmem_limit_bytes=(50 if sub + wave == 0 else 24) * 2**20),
+            pltpu.VMEM(users.shape, jnp.float32),
+        ],
+        compiler_params=pltpu.CompilerParams(vmem_limit_bytes=(24 if wave else 50) * 2**20),
         cost_estimate=pl.CostEstimate(
             flops=8 * 3 * 2 * side * side * width,
             bytes_accessed=8 * 2**20,
             transcendentals=0,
         ),
-        name=f"tiles_{sub}_{wave}",
-    )(coords, counts, place, users, *carried, *slabs, values)
+        name=f"tiles_0_{wave}",
+    )(coords, counts, place, users, *carried, slab, values)
 
 
 def lay_kernel(wave, n_own, carried, *refs):
@@ -203,19 +278,29 @@
         g = lax.axis_index("grp").astype(jnp.int32)
         place = jnp.where(g % 2 == 0, g // 2, n_grp - 1 - g // 2).reshape(1)
         users = user_factors
-        slab = item_factors.reshape(n_grp, 2 * WAVES, side, width)
-        slabs = [[slab] for _ in range(WAVES)]
+        slab = item_factors.reshape(n_grp, FLOWS, side, width)
+        slabs = None
         for sub in range(rounds):
             final = sub + 1 == rounds
-            after = None
-            sums = []
-            owns = []
-            for wave in range(WAVES):
-                after, *near, far_f, far_b, own = tile_step(
-                    sub, wave, n_grp, coords, counts, place, users, after, slabs[wave], values
+            if sub == 0:
+                after = None
+                sums = []
+                owns = []
+                for wave in range(WAVES):
+                    after, *near, far_f, far_b, own = first_step(
+                        wave, n_grp, coords, counts, place, users, after, slab, values
+                    )
+                    sums.append((near, (far_f, far_b)))
+                    owns.append(own)
+            else:
+                after, *tails = tile_step(
+                    sub, n_grp, coords, counts, place, users, slabs, values
                 )
-                sums.append((near, (far_f, far_b)))
-                owns.append(own)
+                owns = tails[2 * FLOWS :]
+                sums = [
+                    (tails[2 * w : 2 * w + 2], tails[FLOWS + 2 * w : FLOWS + 2 * w + 2])
+                    for w in range(WAVES)
+                ]
             if not final:
                 owns = [lax.ppermute(own, "strat", turn) for own in owns]
             owns = [[lax.optimization_barrier(own[way]) for way in range(2)] for own in owns]
@@ -235,12 +320,13 @@
                 for t in range(1, n_grp):
                     for way in range(2):
                         got[way].append(lax.ppermute(got[way][-1], "grp", ring[way]))
-                nexts.append(got[0] + got[1])
+                nexts += got[0] + got[1]
             users = after
             slabs = nexts
         items = None
         for wave in range(WAVES):
-            items = lay(wave, n_grp, place, slabs[wave], items)
+            tiles = slabs[2 * n_grp * wave : 2 * n_grp * (wave + 1)]
+            items = lay(wave, n_grp, place, tiles, items)
         return users, items.reshape(item_factors.shape)
 
     placed = (

time: 294 us -> 288 us (0.980)
  starting transfers between devices: 182 us -> 175 us
  waiting for transfers between devices: 84.6 us -> 88.5 us
    ppermute x84, waiting for transfers between devices: 44 us -> 51 us  [per_device(): got[way].append(lax.ppermute(got[way][-1], 'grp', ring[way]))]
    ppermute x76, starting transfers between devices: 90.1 us -> 85.8 us  [per_device(): parts[way] = lax.ppermute(part, 'grp', ring[way])]
    ppermute x84, starting transfers between devices: 84.4 us -> 80.7 us  [per_device(): got[way].append(lax.ppermute(got[way][-1], 'grp', ring[way]))]
    pallas_call x6 -> x4, Pallas kernels: 18.5 us -> 17.1 us  [the longest x2 8.81 us: tile_step(): pl.pallas_call(functools.partial(tile_kernel, sub, side, n_own), out_shap...]
  transfers between devices with their start and end apart: 172 -> 172, of which waited for: 122 -> 122; matrix products, arithmetic and copies ran while one was open for 1% -> 1% of each run, Pallas kernels for 3% -> 2%
where the time goes in v4:
time: 288 us
  starting transfers between devices  175 us (61%)
  waiting for transfers between devices  88.5 us (31%)
  Pallas kernels  20 us (7%)
    ppermute x76, starting transfers between devices, per_device(): parts[way] = lax.ppermute(part, 'grp', ring[way])  85.8 us
    ppermute x84, starting transfers between devices, per_device(): got[way].append(lax.ppermute(got[way][-1], 'grp', ring[way]))  80.7 us
    ppermute x84, waiting for transfers between devices, per_device(): got[way].append(lax.ppermute(got[way][-1], 'grp', ring[way]))  51 us
    ppermute x76, waiting for transfers between devices, per_device(): parts[way] = lax.ppermute(part, 'grp', ring[way])  35.5 us
    pallas_call x2, Pallas kernels, tile_step(): pl.pallas_call(functools.partial(tile_kernel, sub, side, n_own), out_shap...  8.81 us
    pallas_call x2, Pallas kernels, first_step(): pl.pallas_call(functools.partial(first_kernel, wave, side, n_own), out_sh...  8.29 us
    ppermute x8, starting transfers between devices, per_device(): parts[way] = lax.ppermute(part, ('strat', 'grp'), last[way])  6.55 us
  transfers between devices with their start and end apart: 172, of which 122 were waited for; matrix products, arithmetic and copies ran while one was open for 1% of the time, Pallas kernels for 2%

profile of v4, /device:TPU:0, one launch (start us, length us, event | category | flops | bytes accessed | tf_op | source)
XLA Modules:
  0.0 287.9 jit_solution(13949112346513310066)
XLA Ops:
  2.6 4.4 %tiles_0_0.1 = (f32[1024,256]{1,0:T(8,128)S(1)}, f32[128,256]{1,0:T(8,128)S(1)}, f32[128,256]{1,0:T(8,128)S(1)}, f32[6,128,256]{2,1,0:T(8,128)S(1)}, f32[6,128,2...) custom-call(s32[3,2,16]{2,1,0:T(2,128)S(1)} %bitcast.180, s32[3]{0:T(128)S(1)} %bitcast.184, s32[1]{0:T(128)} %bitcast.2.refs_2_.refs_0_, ...), custom_call_target="tpu_custom_call" | custom-call | flops 201326592 | bytes 8388608 | tf_op jit(solution)/shard_map/tiles_0_0/pallas_call | solution.py:190
  7.0 2.3 collective-permute-start.1
  10.1 1.5 collective-permute-start
  11.6 3.9 %tiles_0_1.1 = (f32[1024,256]{1,0:T(8,128)S(1)}, f32[128,256]{1,0:T(8,128)S(1)}, f32[128,256]{1,0:T(8,128)S(1)}, f32[6,128,256]{2,1,0:T(8,128)S(1)}, f32[6,128,2...) custom-call(s32[3,2,16]{2,1,0:T(2,128)S(1)} %bitcast.181, s32[3]{0:T(128)S(1)} %bitcast.185, ...), custom_call_target="tpu_custom_call", output_to_operand_aliasing={{0}: (4, {})} | custom-call | flops 201326592 | bytes 8388608 | tf_op jit(solution)/shard_map/tiles_0_1/pallas_call | solution.py:190
  15.5 2.0 collective-permute-start.44
  17.7 2.8 collective-permute-done.30
  20.5 1.5 collective-permute-start.16
  25.9 2.2 collective-permute-start.17
  32.8 1.5 collective-permute-start.18
  35.7 1.7 collective-permute-start.47
  42.0 1.5 collective-permute-start.48
  45.2 1.5 collective-permute-start.20
  48.4 1.5 collective-permute-start.49
  50.3 1.9 collective-permute-start.21
  53.5 1.6 collective-permute-start.50
  62.7 1.5 collective-permute-start.23
  77.8 1.4 collective-permute-start.54
  86.8 1.5 collective-permute-start.27
  89.9 1.5 collective-permute-start.56
  92.9 1.8 collective-permute-start.28
  96.1 1.5 collective-permute-start.57
  98.0 2.6 collective-permute-done.43.refs_27_
  101.0 4.8 %tiles_1.1 = (f32[1024,256]{1,0:T(8,128)S(1)}, f32[128,256]{1,0:T(8,128)S(1)}, f32[128,256]{1,0:T(8,128)S(1)}, f32[128,256]{1,0:T(8,128)S(1)}, f32[128,256]{1,0:...) custom-call(s32[3,2,16]{2,1,0:T(2,128)S(1)} %bitcast.182, ...), custom_call_target="tpu_custom_call" | custom-call | flops 402653184 | bytes 16777216 | tf_op jit(solution)/shard_map/tiles_1/pallas_call | solution.py:87
  106.3 1.6 collective-permute-start.73
  107.9 2.1 collective-permute-start.88
  110.9 2.1 collective-permute-done.73
  113.0 2.0 collective-permute-start.60
  115.1 2.1 collective-permute-start.89
  117.3 1.4 collective-permute-done.60
  118.7 2.5 collective-permute-start.61
  121.4 2.7 collective-permute-start.90
  124.4 2.5 collective-permute-start.62
  128.0 2.2 collective-permute-start.91
  130.6 2.5 collective-permute-start.63
  134.1 2.5 collective-permute-start.92
  137.1 2.4 collective-permute-start.64
  140.5 1.8 collective-permute-start.93
  148.4 1.7 collective-permute-start.66
  151.3 1.7 collective-permute-start.95
  153.1 1.6 collective-permute-start.109
  157.7 1.5 collective-permute-start.96
  166.9 1.4 collective-permute-start.69
  191.1 1.6 collective-permute-done.86.refs_19_
  193.8 1.7 collective-permute-done.115.refs_35_
  195.6 4.1 %tiles_2.1 = (f32[1024,256]{1,0:T(8,128)}, f32[128,256]{1,0:T(8,128)S(1)}, f32[128,256]{1,0:T(8,128)S(1)}, f32[128,256]{1,0:T(8,128)S(1)}, f32[128,256]{1,0:T(8,...) custom-call(s32[3,2,16]{2,1,0:T(2,128)S(1)} %bitcast.183, ...), custom_call_target="tpu_custom_call" | custom-call | flops 402653184 | bytes 16777216 | tf_op jit(solution)/shard_map/tiles_2/pallas_call | solution.py:87
  199.6 2.6 collective-permute-start.116
  202.2 2.0 collective-permute-start.144
  204.2 1.7 collective-permute-done.116
  205.9 2.0 collective-permute-start.117
  208.7 2.0 collective-permute-start.145
  212.1 1.5 collective-permute-start.118
  215.1 1.8 collective-permute-start.146
  217.9 1.8 collective-permute-start.119
  224.4 1.7 collective-permute-start.120
  230.7 1.6 collective-permute-start.121
  233.6 1.6 collective-permute-start.149
  240.1 1.5 collective-permute-start.150
  246.4 1.5 collective-permute-start.151
  249.4 1.5 collective-permute-start.124
  255.6 1.5 collective-permute-start.125
  261.7 1.5 collective-permute-start.126
  264.9 1.5 collective-permute-start.154
  284.1 1.4 lay_0.1.refs_1_
  286.3 1.4 lay_1.1
  (385 shorter events, 160.2 us)
Async XLA Ops:
  7.0 10.5 %collective-permute-start.1 = (f32[128,256]{1,0:T(8,128)S(1)}, f32[128,256]{1,0:T(8,128)S(1)}, u32[]{:S(2)}, u32[]{:S(2)}) collective-permute-start(f32[128,256]{1,0:T(8,128)S(1)} %get-tuple-element.39), channel_id=1, source_target_pairs={{0,2},{2,4},{4,6},{6,7},{7,5},{5,3},{3,1},{1,0},{8,10},{10,12},{12... | collective-permute-start | bytes 393224 | tf_op jit(solution)/shard_map/ppermute | solution.py:318
  9.3 8.2 %collective-permute-start.15 = (f32[128,256]{1,0:T(8,128)S(1)}, f32[128,256]{1,0:T(8,128)S(1)}, u32[]{:S(2)}, u32[]{:S(2)}) collective-permute-start(f32[128,256]{1,0:T(8,128)S(1)} %get-tuple-element.41), channel_id=1, source_target_pairs={{0,1},{2,0},{4,2},{6,4},{7,6},{5,7},{3,5},{1,3},{8,9},{10,8},{12,1... | collective-permute-start | bytes 393224 | tf_op jit(solution)/shard_map/ppermute | solution.py:318
  10.1 15.8 %collective-permute-start = (f32[2,128,256]{2,1,0:T(8,128)S(1)}, f32[2,128,256]{2,1,0:T(8,128)S(1)}, u32[]{:S(2)}, u32[]{:S(2)}) collective-permute-start(f32[2,128,256]{2,1,0:T(8,128)S(1)} %get-tuple-element.38), channel_id=1, source_target_pairs={{0,24},{8,0},{16,8},{24,16},{1,25},{9,1},{17,9},{25,17},{2,26},{10... | collective-permute-start | bytes 786440 | tf_op jit(solution)/shard_map/ppermute | solution.py:305
  15.5 6.5 %collective-permute-start.44 = (f32[128,256]{1,0:T(8,128)S(1)}, f32[128,256]{1,0:T(8,128)S(1)}, u32[]{:S(2)}, u32[]{:S(2)}) collective-permute-start(f32[128,256]{1,0:T(8,128)S(1)} %get-tuple-element.46), channel_id=1, source_target_pairs={{0,1},{2,0},{4,2},{6,4},{7,6},{5,7},{3,5},{1,3},{8,9},{10,8},{12,1... | collective-permute-start | bytes 393224 | tf_op jit(solution)/shard_map/ppermute | solution.py:318
  17.5 37.5 %collective-permute-start.29 = (f32[2,128,256]{2,1,0:T(8,128)S(1)}, f32[2,128,256]{2,1,0:T(8,128)S(1)}, u32[]{:S(2)}, u32[]{:S(2)}) collective-permute-start(f32[2,128,256]{2,1,0:T(8,128)S(1)} %get-tuple-element.43), channel_id=1, source_target_pairs={{0,24},{8,0},{16,8},{24,16},{1,25},{9,1},{17,9},{25,17},{2,26},{10... | collective-permute-start | bytes 786440 | tf_op jit(solution)/shard_map/ppermute | solution.py:305
  23.5 6.3 %collective-permute-start.45 = (f32[128,256]{1,0:T(8,128)S(1)}, f32[128,256]{1,0:T(8,128)S(1)}, u32[]{:S(2)}, u32[]{:S(2)}) collective-permute-start(f32[128,256]{1,0:T(8,128)S(1)} %bitcast_add_fusion.53), channel_id=1, source_target_pairs={{0,1},{2,0},{4,2},{6,4},{7,6},{5,7},{3,5},{1,3},{8,9},{10,8},{12,1... | collective-permute-start | bytes 393224 | tf_op jit(solution)/shard_map/ppermute | solution.py:318
  25.9 6.9 %collective-permute-start.17 = (f32[128,256]{1,0:T(8,128)S(1)}, f32[128,256]{1,0:T(8,128)S(1)}, u32[]{:S(2)}, u32[]{:S(2)}) collective-permute-start(f32[128,256]{1,0:T(8,128)S(1)} %bitcast_add_fusion.64), channel_id=1, source_target_pairs={{0,1},{2,0},{4,2},{6,4},{7,6},{5,7},{3,5},{1,3},{8,9},{10,8},{12,1... | collective-permute-start | bytes 393224 | tf_op jit(solution)/shard_map/ppermute | solution.py:318
  28.2 6.4 %collective-permute-start.32 = (f32[128,256]{1,0:T(8,128)S(1)}, f32[128,256]{1,0:T(8,128)S(1)}, u32[]{:S(2)}, u32[]{:S(2)}) collective-permute-start(f32[128,256]{1,0:T(8,128)S(1)} %bitcast_add_fusion.58), channel_id=1, source_target_pairs={{0,2},{2,4},{4,6},{6,7},{7,5},{5,3},{3,1},{1,0},{8,10},{10,12},{12... | collective-permute-start | bytes 393224 | tf_op jit(solution)/shard_map/ppermute | solution.py:318
  32.8 6.3 %collective-permute-start.18 = (f32[128,256]{1,0:T(8,128)S(1)}, f32[128,256]{1,0:T(8,128)S(1)}, u32[]{:S(2)}, u32[]{:S(2)}) collective-permute-start(f32[128,256]{1,0:T(8,128)S(1)} %bitcast_add_fusion.63), channel_id=1, source_target_pairs={{0,1},{2,0},{4,2},{6,4},{7,6},{5,7},{3,5},{1,3},{8,9},{10,8},{12,1... | collective-permute-start | bytes 393224 | tf_op jit(solution)/shard_map/ppermute | solution.py:318
  34.6 6.3 %collective-permute-start.33 = (f32[128,256]{1,0:T(8,128)S(1)}, f32[128,256]{1,0:T(8,128)S(1)}, u32[]{:S(2)}, u32[]{:S(2)}) collective-permute-start(f32[128,256]{1,0:T(8,128)S(1)} %bitcast_add_fusion.57), channel_id=1, source_target_pairs={{0,2},{2,4},{4,6},{6,7},{7,5},{5,3},{3,1},{1,0},{8,10},{10,12},{12... | collective-permute-start | bytes 393224 | tf_op jit(solution)/shard_map/ppermute | solution.py:318
  37.4 6.4 %collective-permute-start.5 = (f32[128,256]{1,0:T(8,128)S(1)}, f32[128,256]{1,0:T(8,128)S(1)}, u32[]{:S(2)}, u32[]{:S(2)}) collective-permute-start(f32[128,256]{1,0:T(8,128)S(1)} %bitcast_add_fusion.68), channel_id=1, source_target_pairs={{0,2},{2,4},{4,6},{6,7},{7,5},{5,3},{3,1},{1,0},{8,10},{10,12},{12... | collective-permute-start | bytes 393224 | tf_op jit(solution)/shard_map/ppermute | solution.py:318
  41.0 6.3 %collective-permute-start.34 = (f32[128,256]{1,0:T(8,128)S(1)}, f32[128,256]{1,0:T(8,128)S(1)}, u32[]{:S(2)}, u32[]{:S(2)}) collective-permute-start(f32[128,256]{1,0:T(8,128)S(1)} %bitcast_add_fusion.56), channel_id=1, source_target_pairs={{0,2},{2,4},{4,6},{6,7},{7,5},{5,3},{3,1},{1,0},{8,10},{10,12},{12... | collective-permute-start | bytes 393224 | tf_op jit(solution)/shard_map/ppermute | solution.py:318
  42.0 6.4 %collective-permute-start.48 = (f32[128,256]{1,0:T(8,128)S(1)}, f32[128,256]{1,0:T(8,128)S(1)}, u32[]{:S(2)}, u32[]{:S(2)}) collective-permute-start(f32[128,256]{1,0:T(8,128)S(1)} %bitcast_add_fusion.50), channel_id=1, source_target_pairs={{0,1},{2,0},{4,2},{6,4},{7,6},{5,7},{3,5},{1,3},{8,9},{10,8},{12,1... | collective-permute-start | bytes 393224 | tf_op jit(solution)/shard_map/ppermute | solution.py:318
  59.2 6.4 %collective-permute-start.51 = (f32[128,256]{1,0:T(8,128)S(1)}, f32[128,256]{1,0:T(8,128)S(1)}, u32[]{:S(2)}, u32[]{:S(2)}) collective-permute-start(f32[128,256]{1,0:T(8,128)S(1)} %add.285.refs_28_), channel_id=1, source_target_pairs={{0,1},{2,0},{4,2},{6,4},{7,6},{5,7},{3,5},{1,3},{8,9},{10,8},{12,1... | collective-permute-start | bytes 393224 | tf_op jit(solution)/shard_map/ppermute | solution.py:322
  65.5 6.3 %collective-permute-start.52 = (f32[128,256]{1,0:T(8,128)S(1)}, f32[128,256]{1,0:T(8,128)S(1)}, u32[]{:S(2)}, u32[]{:S(2)}) collective-permute-start(f32[128,256]{1,0:T(8,128)S(1)} %collective-permute-done.51.refs_29_), channel_id=1, source_target_pairs={{0,1},{2,0},{4,2},{6,4},{7,6},{5,7},{3,5},{1,3},{8,9},{10,8},{12,1... | collective-permute-start | bytes 393224 | tf_op jit(solution)/shard_map/ppermute | solution.py:322
  68.4 6.3 %collective-permute-start.24 = (f32[128,256]{1,0:T(8,128)S(1)}, f32[128,256]{1,0:T(8,128)S(1)}, u32[]{:S(2)}, u32[]{:S(2)}) collective-permute-start(f32[128,256]{1,0:T(8,128)S(1)} %collective-permute-done.23.refs_14_), channel_id=1, source_target_pairs={{0,1},{2,0},{4,2},{6,4},{7,6},{5,7},{3,5},{1,3},{8,9},{10,8},{12,1... | collective-permute-start | bytes 393224 | tf_op jit(solution)/shard_map/ppermute | solution.py:322
  73.6 6.4 %collective-permute-start.11 = (f32[128,256]{1,0:T(8,128)S(1)}, f32[128,256]{1,0:T(8,128)S(1)}, u32[]{:S(2)}, u32[]{:S(2)}) collective-permute-start(f32[128,256]{1,0:T(8,128)S(1)} %collective-permute-done.10.refs_7_), channel_id=1, source_target_pairs={{0,2},{2,4},{4,6},{6,7},{7,5},{5,3},{3,1},{1,0},{8,10},{10,12},{12... | collective-permute-start | bytes 393224 | tf_op jit(solution)/shard_map/ppermute | solution.py:322
  74.7 6.3 %collective-permute-start.25 = (f32[128,256]{1,0:T(8,128)S(1)}, f32[128,256]{1,0:T(8,128)S(1)}, u32[]{:S(2)}, u32[]{:S(2)}) collective-permute-start(f32[128,256]{1,0:T(8,128)S(1)} %collective-permute-done.24.refs_15_), channel_id=1, source_target_pairs={{0,1},{2,0},{4,2},{6,4},{7,6},{5,7},{3,5},{1,3},{8,9},{10,8},{12,1... | collective-permute-start | bytes 393224 | tf_op jit(solution)/shard_map/ppermute | solution.py:322
  77.0 6.4 %collective-permute-start.40 = (f32[128,256]{1,0:T(8,128)S(1)}, f32[128,256]{1,0:T(8,128)S(1)}, u32[]{:S(2)}, u32[]{:S(2)}) collective-permute-start(f32[128,256]{1,0:T(8,128)S(1)} %collective-permute-done.39.refs_23_), channel_id=1, source_target_pairs={{0,2},{2,4},{4,6},{6,7},{7,5},{5,3},{3,1},{1,0},{8,10},{10,12},{12... | collective-permute-start | bytes 393224 | tf_op jit(solution)/shard_map/ppermute | solution.py:322
  86.2 6.4 %collective-permute-start.13 = (f32[128,256]{1,0:T(8,128)S(1)}, f32[128,256]{1,0:T(8,128)S(1)}, u32[]{:S(2)}, u32[]{:S(2)}) collective-permute-start(f32[128,256]{1,0:T(8,128)S(1)} %collective-permute-done.12.refs_9_), channel_id=1, source_target_pairs={{0,2},{2,4},{4,6},{6,7},{7,5},{5,3},{3,1},{1,0},{8,10},{10,12},{12... | collective-permute-start | bytes 393224 | tf_op jit(solution)/shard_map/ppermute | solution.py:322
  89.3 6.3 %collective-permute-start.42 = (f32[128,256]{1,0:T(8,128)S(1)}, f32[128,256]{1,0:T(8,128)S(1)}, u32[]{:S(2)}, u32[]{:S(2)}) collective-permute-start(f32[128,256]{1,0:T(8,128)S(1)} %collective-permute-done.41.refs_25_), channel_id=1, source_target_pairs={{0,2},{2,4},{4,6},{6,7},{7,5},{5,3},{3,1},{1,0},{8,10},{10,12},{12... | collective-permute-start | bytes 393224 | tf_op jit(solution)/shard_map/ppermute | solution.py:322
  106.3 6.7 %collective-permute-start.73 = (f32[128,256]{1,0:T(8,128)S(1)}, f32[128,256]{1,0:T(8,128)S(1)}, u32[]{:S(2)}, u32[]{:S(2)}) collective-permute-start(f32[128,256]{1,0:T(8,128)S(1)} %get-tuple-element.52), channel_id=1, source_target_pairs={{0,1},{2,0},{4,2},{6,4},{7,6},{5,7},{3,5},{1,3},{8,9},{10,8},{12,1... | collective-permute-start | bytes 393224 | tf_op jit(solution)/shard_map/ppermute | solution.py:318
  107.9 7.1 %collective-permute-start.88 = (f32[128,256]{1,0:T(8,128)S(1)}, f32[128,256]{1,0:T(8,128)S(1)}, u32[]{:S(2)}, u32[]{:S(2)}) collective-permute-start(f32[128,256]{1,0:T(8,128)S(1)} %get-tuple-element.55), channel_id=1, source_target_pairs={{0,2},{2,4},{4,6},{6,7},{7,5},{5,3},{3,1},{1,0},{8,10},{10,12},{12... | collective-permute-start | bytes 393224 | tf_op jit(solution)/shard_map/ppermute | solution.py:318
  110.0 7.2 %collective-permute-start.58 = (f32[2,128,256]{2,1,0:T(8,128)S(1)}, f32[2,128,256]{2,1,0:T(8,128)S(1)}, u32[]{:S(2)}, u32[]{:S(2)}) collective-permute-start(f32[2,128,256]{2,1,0:T(8,128)S(1)} %get-tuple-element.49), channel_id=1, source_target_pairs={{0,24},{8,0},{16,8},{24,16},{1,25},{9,1},{17,9},{25,17},{2,26},{10... | collective-permute-start | bytes 786440 | tf_op jit(solution)/shard_map/ppermute | solution.py:305
  110.8 37.3 %collective-permute-start.87 = (f32[2,128,256]{2,1,0:T(8,128)S(1)}, f32[2,128,256]{2,1,0:T(8,128)S(1)}, u32[]{:S(2)}, u32[]{:S(2)}) collective-permute-start(f32[2,128,256]{2,1,0:T(8,128)S(1)} %get-tuple-element.54), channel_id=1, source_target_pairs={{0,24},{8,0},{16,8},{24,16},{1,25},{9,1},{17,9},{25,17},{2,26},{10... | collective-permute-start | bytes 786440 | tf_op jit(solution)/shard_map/ppermute | solution.py:305
  117.2 6.9 %collective-permute-start.103 = (f32[128,256]{1,0:T(8,128)S(1)}, f32[128,256]{1,0:T(8,128)S(1)}, u32[]{:S(2)}, u32[]{:S(2)}) collective-permute-start(f32[128,256]{1,0:T(8,128)S(1)} %bitcast_add_fusion.29), channel_id=1, source_target_pairs={{0,1},{2,0},{4,2},{6,4},{7,6},{5,7},{3,5},{1,3},{8,9},{10,8},{12,1... | collective-permute-start | bytes 393224 | tf_op jit(solution)/shard_map/ppermute | solution.py:318
  121.4 6.6 %collective-permute-start.90 = (f32[128,256]{1,0:T(8,128)S(1)}, f32[128,256]{1,0:T(8,128)S(1)}, u32[]{:S(2)}, u32[]{:S(2)}) collective-permute-start(f32[128,256]{1,0:T(8,128)S(1)} %bitcast_add_fusion.34), channel_id=1, source_target_pairs={{0,2},{2,4},{4,6},{6,7},{7,5},{5,3},{3,1},{1,0},{8,10},{10,12},{12... | collective-permute-start | bytes 393224 | tf_op jit(solution)/shard_map/ppermute | solution.py:318
  130.2 6.4 %collective-permute-start.105 = (f32[128,256]{1,0:T(8,128)S(1)}, f32[128,256]{1,0:T(8,128)S(1)}, u32[]{:S(2)}, u32[]{:S(2)}) collective-permute-start(f32[128,256]{1,0:T(8,128)S(1)} %bitcast_add_fusion.27), channel_id=1, source_target_pairs={{0,1},{2,0},{4,2},{6,4},{7,6},{5,7},{3,5},{1,3},{8,9},{10,8},{12,1... | collective-permute-start | bytes 393224 | tf_op jit(solution)/shard_map/ppermute | solution.py:318
  130.6 6.4 %collective-permute-start.63 = (f32[128,256]{1,0:T(8,128)S(1)}, f32[128,256]{1,0:T(8,128)S(1)}, u32[]{:S(2)}, u32[]{:S(2)}) collective-permute-start(f32[128,256]{1,0:T(8,128)S(1)} %bitcast_add_fusion.44), channel_id=1, source_target_pairs={{0,2},{2,4},{4,6},{6,7},{7,5},{5,3},{3,1},{1,0},{8,10},{10,12},{12... | collective-permute-start | bytes 393224 | tf_op jit(solution)/shard_map/ppermute | solution.py:318
  133.2 6.3 %collective-permute-start.77 = (f32[128,256]{1,0:T(8,128)S(1)}, f32[128,256]{1,0:T(8,128)S(1)}, u32[]{:S(2)}, u32[]{:S(2)}) collective-permute-start(f32[128,256]{1,0:T(8,128)S(1)} %bitcast_add_fusion.38), channel_id=1, source_target_pairs={{0,1},{2,0},{4,2},{6,4},{7,6},{5,7},{3,5},{1,3},{8,9},{10,8},{12,1... | collective-permute-start | bytes 393224 | tf_op jit(solution)/shard_map/ppermute | solution.py:318
  134.1 6.4 %collective-permute-start.92 = (f32[128,256]{1,0:T(8,128)S(1)}, f32[128,256]{1,0:T(8,128)S(1)}, u32[]{:S(2)}, u32[]{:S(2)}) collective-permute-start(f32[128,256]{1,0:T(8,128)S(1)} %bitcast_add_fusion.32), channel_id=1, source_target_pairs={{0,2},{2,4},{4,6},{6,7},{7,5},{5,3},{3,1},{1,0},{8,10},{10,12},{12... | collective-permute-start | bytes 393224 | tf_op jit(solution)/shard_map/ppermute | solution.py:318
  137.1 6.4 %collective-permute-start.64 = (f32[128,256]{1,0:T(8,128)S(1)}, f32[128,256]{1,0:T(8,128)S(1)}, u32[]{:S(2)}, u32[]{:S(2)}) collective-permute-start(f32[128,256]{1,0:T(8,128)S(1)} %bitcast_add_fusion.43), channel_id=1, source_target_pairs={{0,2},{2,4},{4,6},{6,7},{7,5},{5,3},{3,1},{1,0},{8,10},{10,12},{12... | collective-permute-start | bytes 393224 | tf_op jit(solution)/shard_map/ppermute | solution.py:318
  148.4 6.3 %collective-permute-start.66 = (f32[128,256]{1,0:T(8,128)S(1)}, f32[128,256]{1,0:T(8,128)S(1)}, u32[]{:S(2)}, u32[]{:S(2)}) collective-permute-start(f32[128,256]{1,0:T(8,128)S(1)} %add.292.refs_4_), channel_id=1, source_target_pairs={{0,2},{2,4},{4,6},{6,7},{7,5},{5,3},{3,1},{1,0},{8,10},{10,12},{12... | collective-permute-start | bytes 393224 | tf_op jit(solution)/shard_map/ppermute | solution.py:322
  150.1 6.4 %collective-permute-start.80 = (f32[128,256]{1,0:T(8,128)S(1)}, f32[128,256]{1,0:T(8,128)S(1)}, u32[]{:S(2)}, u32[]{:S(2)}) collective-permute-start(f32[128,256]{1,0:T(8,128)S(1)} %add.299.refs_12_), channel_id=1, source_target_pairs={{0,1},{2,0},{4,2},{6,4},{7,6},{5,7},{3,5},{1,3},{8,9},{10,8},{12,1... | collective-permute-start | bytes 393224 | tf_op jit(solution)/shard_map/ppermute | solution.py:322
  151.3 6.4 %collective-permute-start.95 = (f32[128,256]{1,0:T(8,128)S(1)}, f32[128,256]{1,0:T(8,128)S(1)}, u32[]{:S(2)}, u32[]{:S(2)}) collective-permute-start(f32[128,256]{1,0:T(8,128)S(1)} %add.306.refs_20_), channel_id=1, source_target_pairs={{0,2},{2,4},{4,6},{6,7},{7,5},{5,3},{3,1},{1,0},{8,10},{10,12},{12... | collective-permute-start | bytes 393224 | tf_op jit(solution)/shard_map/ppermute | solution.py:322
  153.1 6.3 %collective-permute-start.109 = (f32[128,256]{1,0:T(8,128)S(1)}, f32[128,256]{1,0:T(8,128)S(1)}, u32[]{:S(2)}, u32[]{:S(2)}) collective-permute-start(f32[128,256]{1,0:T(8,128)S(1)} %add.313.refs_28_), channel_id=1, source_target_pairs={{0,1},{2,0},{4,2},{6,4},{7,6},{5,7},{3,5},{1,3},{8,9},{10,8},{12,1... | collective-permute-start | bytes 393224 | tf_op jit(solution)/shard_map/ppermute | solution.py:322
  157.7 6.4 %collective-permute-start.96 = (f32[128,256]{1,0:T(8,128)S(1)}, f32[128,256]{1,0:T(8,128)S(1)}, u32[]{:S(2)}, u32[]{:S(2)}) collective-permute-start(f32[128,256]{1,0:T(8,128)S(1)} %collective-permute-done.95.refs_21_), channel_id=1, source_target_pairs={{0,2},{2,4},{4,6},{6,7},{7,5},{5,3},{3,1},{1,0},{8,10},{10,12},{12... | collective-permute-start | bytes 393224 | tf_op jit(solution)/shard_map/ppermute | solution.py:322
  159.4 6.4 %collective-permute-start.110 = (f32[128,256]{1,0:T(8,128)S(1)}, f32[128,256]{1,0:T(8,128)S(1)}, u32[]{:S(2)}, u32[]{:S(2)}) collective-permute-start(f32[128,256]{1,0:T(8,128)S(1)} %collective-permute-done.109.refs_29_), channel_id=1, source_target_pairs={{0,1},{2,0},{4,2},{6,4},{7,6},{5,7},{3,5},{1,3},{8,9},{10,8},{12,1... | collective-permute-start | bytes 393224 | tf_op jit(solution)/shard_map/ppermute | solution.py:322
  160.5 6.4 %collective-permute-start.68 = (f32[128,256]{1,0:T(8,128)S(1)}, f32[128,256]{1,0:T(8,128)S(1)}, u32[]{:S(2)}, u32[]{:S(2)}) collective-permute-start(f32[128,256]{1,0:T(8,128)S(1)} %collective-permute-done.67.refs_6_), channel_id=1, source_target_pairs={{0,2},{2,4},{4,6},{6,7},{7,5},{5,3},{3,1},{1,0},{8,10},{10,12},{12... | collective-permute-start | bytes 393224 | tf_op jit(solution)/shard_map/ppermute | solution.py:322
  162.4 6.3 %collective-permute-start.82 = (f32[128,256]{1,0:T(8,128)S(1)}, f32[128,256]{1,0:T(8,128)S(1)}, u32[]{:S(2)}, u32[]{:S(2)}) collective-permute-start(f32[128,256]{1,0:T(8,128)S(1)} %collective-permute-done.81.refs_14_), channel_id=1, source_target_pairs={{0,1},{2,0},{4,2},{6,4},{7,6},{5,7},{3,5},{1,3},{8,9},{10,8},{12,1... | collective-permute-start | bytes 393224 | tf_op jit(solution)/shard_map/ppermute | solution.py:322
  164.1 6.4 %collective-permute-start.97 = (f32[128,256]{1,0:T(8,128)S(1)}, f32[128,256]{1,0:T(8,128)S(1)}, u32[]{:S(2)}, u32[]{:S(2)}) collective-permute-start(f32[128,256]{1,0:T(8,128)S(1)} %collective-permute-done.96.refs_22_), channel_id=1, source_target_pairs={{0,2},{2,4},{4,6},{6,7},{7,5},{5,3},{3,1},{1,0},{8,10},{10,12},{12... | collective-permute-start | bytes 393224 | tf_op jit(solution)/shard_map/ppermute | solution.py:322
  165.8 6.4 %collective-permute-start.111 = (f32[128,256]{1,0:T(8,128)S(1)}, f32[128,256]{1,0:T(8,128)S(1)}, u32[]{:S(2)}, u32[]{:S(2)}) collective-permute-start(f32[128,256]{1,0:T(8,128)S(1)} %collective-permute-done.110.refs_30_), channel_id=1, source_target_pairs={{0,1},{2,0},{4,2},{6,4},{7,6},{5,7},{3,5},{1,3},{8,9},{10,8},{12,1... | collective-permute-start | bytes 393224 | tf_op jit(solution)/shard_map/ppermute | solution.py:322
  166.9 6.4 %collective-permute-start.69 = (f32[128,256]{1,0:T(8,128)S(1)}, f32[128,256]{1,0:T(8,128)S(1)}, u32[]{:S(2)}, u32[]{:S(2)}) collective-permute-start(f32[128,256]{1,0:T(8,128)S(1)} %collective-permute-done.68.refs_7_), channel_id=1, source_target_pairs={{0,2},{2,4},{4,6},{6,7},{7,5},{5,3},{3,1},{1,0},{8,10},{10,12},{12... | collective-permute-start | bytes 393224 | tf_op jit(solution)/shard_map/ppermute | solution.py:322
  173.4 6.4 %collective-permute-start.70 = (f32[128,256]{1,0:T(8,128)S(1)}, f32[128,256]{1,0:T(8,128)S(1)}, u32[]{:S(2)}, u32[]{:S(2)}) collective-permute-start(f32[128,256]{1,0:T(8,128)S(1)} %collective-permute-done.69.refs_8_), channel_id=1, source_target_pairs={{0,2},{2,4},{4,6},{6,7},{7,5},{5,3},{3,1},{1,0},{8,10},{10,12},{12... | collective-permute-start | bytes 393224 | tf_op jit(solution)/shard_map/ppermute | solution.py:322
  175.0 6.4 %collective-permute-start.84 = (f32[128,256]{1,0:T(8,128)S(1)}, f32[128,256]{1,0:T(8,128)S(1)}, u32[]{:S(2)}, u32[]{:S(2)}) collective-permute-start(f32[128,256]{1,0:T(8,128)S(1)} %collective-permute-done.83.refs_16_), channel_id=1, source_target_pairs={{0,1},{2,0},{4,2},{6,4},{7,6},{5,7},{3,5},{1,3},{8,9},{10,8},{12,1... | collective-permute-start | bytes 393224 | tf_op jit(solution)/shard_map/ppermute | solution.py:322
  176.2 6.4 %collective-permute-start.99 = (f32[128,256]{1,0:T(8,128)S(1)}, f32[128,256]{1,0:T(8,128)S(1)}, u32[]{:S(2)}, u32[]{:S(2)}) collective-permute-start(f32[128,256]{1,0:T(8,128)S(1)} %collective-permute-done.98.refs_24_), channel_id=1, source_target_pairs={{0,2},{2,4},{4,6},{6,7},{7,5},{5,3},{3,1},{1,0},{8,10},{10,12},{12... | collective-permute-start | bytes 393224 | tf_op jit(solution)/shard_map/ppermute | solution.py:322
  178.0 6.3 %collective-permute-start.113 = (f32[128,256]{1,0:T(8,128)S(1)}, f32[128,256]{1,0:T(8,128)S(1)}, u32[]{:S(2)}, u32[]{:S(2)}) collective-permute-start(f32[128,256]{1,0:T(8,128)S(1)} %collective-permute-done.112.refs_32_), channel_id=1, source_target_pairs={{0,1},{2,0},{4,2},{6,4},{7,6},{5,7},{3,5},{1,3},{8,9},{10,8},{12,1... | collective-permute-start | bytes 393224 | tf_op jit(solution)/shard_map/ppermute | solution.py:322
  179.8 6.4 %collective-permute-start.71 = (f32[128,256]{1,0:T(8,128)S(1)}, f32[128,256]{1,0:T(8,128)S(1)}, u32[]{:S(2)}, u32[]{:S(2)}) collective-permute-start(f32[128,256]{1,0:T(8,128)S(1)} %collective-permute-done.70.refs_9_), channel_id=1, source_target_pairs={{0,2},{2,4},{4,6},{6,7},{7,5},{5,3},{3,1},{1,0},{8,10},{10,12},{12... | collective-permute-start | bytes 393224 | tf_op jit(solution)/shard_map/ppermute | solution.py:322
  181.4 6.3 %collective-permute-start.85 = (f32[128,256]{1,0:T(8,128)S(1)}, f32[128,256]{1,0:T(8,128)S(1)}, u32[]{:S(2)}, u32[]{:S(2)}) collective-permute-start(f32[128,256]{1,0:T(8,128)S(1)} %collective-permute-done.84.refs_17_), channel_id=1, source_target_pairs={{0,1},{2,0},{4,2},{6,4},{7,6},{5,7},{3,5},{1,3},{8,9},{10,8},{12,1... | collective-permute-start | bytes 393224 | tf_op jit(solution)/shard_map/ppermute | solution.py:322
  202.2 6.5 %collective-permute-start.144 = (f32[128,256]{1,0:T(8,128)S(1)}, f32[128,256]{1,0:T(8,128)S(1)}, u32[]{:S(2)}, u32[]{:S(2)}) collective-permute-start(f32[128,256]{1,0:T(8,128)S(1)} %get-tuple-element.66), channel_id=1, source_target_pairs={{0,2},{2,4},{4,6},{6,7},{7,5},{5,3},{3,1},{1,0},{8,10},{10,12},{12... | collective-permute-start | bytes 393224 | tf_op jit(solution)/shard_map/ppermute | solution.py:318
  204.2 6.5 %collective-permute-start.158 = (f32[128,256]{1,0:T(8,128)S(1)}, f32[128,256]{1,0:T(8,128)S(1)}, u32[]{:S(2)}, u32[]{:S(2)}) collective-permute-start(f32[128,256]{1,0:T(8,128)S(1)} %get-tuple-element.68), channel_id=1, source_target_pairs={{0,1},{2,0},{4,2},{6,4},{7,6},{5,7},{3,5},{1,3},{8,9},{10,8},{12,1... | collective-permute-start | bytes 393224 | tf_op jit(solution)/shard_map/ppermute | solution.py:318
  208.7 6.4 %collective-permute-start.145 = (f32[128,256]{1,0:T(8,128)S(1)}, f32[128,256]{1,0:T(8,128)S(1)}, u32[]{:S(2)}, u32[]{:S(2)}) collective-permute-start(f32[128,256]{1,0:T(8,128)S(1)} %bitcast_add_fusion.11), channel_id=1, source_target_pairs={{0,2},{2,4},{4,6},{6,7},{7,5},{5,3},{3,1},{1,0},{8,10},{10,12},{12... | collective-permute-start | bytes 393224 | tf_op jit(solution)/shard_map/ppermute | solution.py:318
  215.1 6.3 %collective-permute-start.146 = (f32[128,256]{1,0:T(8,128)S(1)}, f32[128,256]{1,0:T(8,128)S(1)}, u32[]{:S(2)}, u32[]{:S(2)}) collective-permute-start(f32[128,256]{1,0:T(8,128)S(1)} %bitcast_add_fusion.10), channel_id=1, source_target_pairs={{0,2},{2,4},{4,6},{6,7},{7,5},{5,3},{3,1},{1,0},{8,10},{10,12},{12... | collective-permute-start | bytes 393224 | tf_op jit(solution)/shard_map/ppermute | solution.py:318
  217.9 6.5 %collective-permute-start.119 = (f32[128,256]{1,0:T(8,128)S(1)}, f32[128,256]{1,0:T(8,128)S(1)}, u32[]{:S(2)}, u32[]{:S(2)}) collective-permute-start(f32[128,256]{1,0:T(8,128)S(1)} %bitcast_add_fusion.21), channel_id=1, source_target_pairs={{0,2},{2,4},{4,6},{6,7},{7,5},{5,3},{3,1},{1,0},{8,10},{10,12},{12... | collective-permute-start | bytes 393224 | tf_op jit(solution)/shard_map/ppermute | solution.py:318
  219.7 6.4 %collective-permute-start.133 = (f32[128,256]{1,0:T(8,128)S(1)}, f32[128,256]{1,0:T(8,128)S(1)}, u32[]{:S(2)}, u32[]{:S(2)}) collective-permute-start(f32[128,256]{1,0:T(8,128)S(1)} %bitcast_add_fusion.15), channel_id=1, source_target_pairs={{0,1},{2,0},{4,2},{6,4},{7,6},{5,7},{3,5},{1,3},{8,9},{10,8},{12,1... | collective-permute-start | bytes 393224 | tf_op jit(solution)/shard_map/ppermute | solution.py:318
  230.7 6.3 %collective-permute-start.121 = (f32[128,256]{1,0:T(8,128)S(1)}, f32[128,256]{1,0:T(8,128)S(1)}, u32[]{:S(2)}, u32[]{:S(2)}) collective-permute-start(f32[128,256]{1,0:T(8,128)S(1)} %bitcast_add_fusion.19), channel_id=1, source_target_pairs={{0,2},{2,4},{4,6},{6,7},{7,5},{5,3},{3,1},{1,0},{8,10},{10,12},{12... | collective-permute-start | bytes 393224 | tf_op jit(solution)/shard_map/ppermute | solution.py:318
  233.6 6.5 %collective-permute-start.149 = (f32[128,256]{1,0:T(8,128)S(1)}, f32[128,256]{1,0:T(8,128)S(1)}, u32[]{:S(2)}, u32[]{:S(2)}) collective-permute-start(f32[128,256]{1,0:T(8,128)S(1)} %bitcast_add_fusion.7), channel_id=1, source_target_pairs={{0,2},{2,4},{4,6},{6,7},{7,5},{5,3},{3,1},{1,0},{8,10},{10,12},{12... | collective-permute-start | bytes 393224 | tf_op jit(solution)/shard_map/ppermute | solution.py:318
  235.2 6.4 %collective-permute-start.163 = (f32[128,256]{1,0:T(8,128)S(1)}, f32[128,256]{1,0:T(8,128)S(1)}, u32[]{:S(2)}, u32[]{:S(2)}) collective-permute-start(f32[128,256]{1,0:T(8,128)S(1)} %bitcast_add_fusion.1), channel_id=1, source_target_pairs={{0,1},{2,0},{4,2},{6,4},{7,6},{5,7},{3,5},{1,3},{8,9},{10,8},{12,1... | collective-permute-start | bytes 393224 | tf_op jit(solution)/shard_map/ppermute | solution.py:318
  240.1 6.3 %collective-permute-start.150 = (f32[128,256]{1,0:T(8,128)S(1)}, f32[128,256]{1,0:T(8,128)S(1)}, u32[]{:S(2)}, u32[]{:S(2)}) collective-permute-start(f32[128,256]{1,0:T(8,128)S(1)} %bitcast_add_fusion.6), channel_id=1, source_target_pairs={{0,2},{2,4},{4,6},{6,7},{7,5},{5,3},{3,1},{1,0},{8,10},{10,12},{12... | collective-permute-start | bytes 393224 | tf_op jit(solution)/shard_map/ppermute | solution.py:318
  241.6 6.3 %collective-permute-start.164 = (f32[128,256]{1,0:T(8,128)S(1)}, f32[128,256]{1,0:T(8,128)S(1)}, u32[]{:S(2)}, u32[]{:S(2)}) collective-permute-start(f32[128,256]{1,0:T(8,128)S(1)} %bitcast_add_fusion), channel_id=1, source_target_pairs={{0,1},{2,0},{4,2},{6,4},{7,6},{5,7},{3,5},{1,3},{8,9},{10,8},{12,1... | collective-permute-start | bytes 393224 | tf_op jit(solution)/shard_map/ppermute | solution.py:318
  243.0 6.3 %collective-permute-start.123 = (f32[128,256]{1,0:T(8,128)S(1)}, f32[128,256]{1,0:T(8,128)S(1)}, u32[]{:S(2)}, u32[]{:S(2)}) collective-permute-start(f32[128,256]{1,0:T(8,128)S(1)} %add.320.refs_1_), channel_id=1, source_target_pairs={{0,2},{2,4},{4,6},{6,7},{7,5},{5,3},{3,1},{1,0},{8,10},{10,12},{12... | collective-permute-start | bytes 393224 | tf_op jit(solution)/shard_map/ppermute | solution.py:322
  244.4 6.5 %collective-permute-start.137 = (f32[128,256]{1,0:T(8,128)S(1)}, f32[128,256]{1,0:T(8,128)S(1)}, u32[]{:S(2)}, u32[]{:S(2)}) collective-permute-start(f32[128,256]{1,0:T(8,128)S(1)} %add.327.refs_9_), channel_id=1, source_target_pairs={{0,1},{2,0},{4,2},{6,4},{7,6},{5,7},{3,5},{1,3},{8,9},{10,8},{12,1... | collective-permute-start | bytes 393224 | tf_op jit(solution)/shard_map/ppermute | solution.py:322
  260.1 6.3 %collective-permute-start.167 = (f32[128,256]{1,0:T(8,128)S(1)}, f32[128,256]{1,0:T(8,128)S(1)}, u32[]{:S(2)}, u32[]{:S(2)}) collective-permute-start(f32[128,256]{1,0:T(8,128)S(1)} %collective-permute-done.166.refs_12_), channel_id=1, source_target_pairs={{0,1},{2,0},{4,2},{6,4},{7,6},{5,7},{3,5},{1,3},{8,9},{10,8},{12,1... | collective-permute-start | bytes 393224 | tf_op jit(solution)/shard_map/ppermute | solution.py:322
  261.7 6.3 %collective-permute-start.126 = (f32[128,256]{1,0:T(8,128)S(1)}, f32[128,256]{1,0:T(8,128)S(1)}, u32[]{:S(2)}, u32[]{:S(2)}) collective-permute-start(f32[128,256]{1,0:T(8,128)S(1)} %collective-permute-done.125.refs_4_), channel_id=1, source_target_pairs={{0,2},{2,4},{4,6},{6,7},{7,5},{5,3},{3,1},{1,0},{8,10},{10,12},{12... | collective-permute-start | bytes 393224 | tf_op jit(solution)/shard_map/ppermute | solution.py:322
  (113 other events, 651.4 us)

commit v5 on v4

--- a/solution.py
+++ b/solution.py
@@ -304,11 +304,10 @@
             if not final:
                 owns = [lax.ppermute(own, "strat", turn) for own in owns]
             owns = [[lax.optimization_barrier(own[way]) for way in range(2)] for own in owns]
-            nexts = []
-            for wave in range(WAVES):
-                parts, far = sums[wave]
-                for t in range(1, n_grp):
-                    for way in range(2):
+            for t in range(1, n_grp):
+                for way in range(2):
+                    for wave in range(WAVES):
+                        parts, far = sums[wave]
                         part = parts[way]
                         if t > 1:
                             part = part + far[way][t - 2]
@@ -316,11 +315,16 @@
                             parts[way] = lax.ppermute(part, ("strat", "grp"), last[way])
                         else:
                             parts[way] = lax.ppermute(part, "grp", ring[way])
-                got = [[owns[wave][way] + parts[way]] for way in range(2)]
-                for t in range(1, n_grp):
-                    for way in range(2):
-                        got[way].append(lax.ppermute(got[way][-1], "grp", ring[way]))
-                nexts += got[0] + got[1]
+            got = [
+                [[owns[wave][way] + sums[wave][0][way]] for way in range(2)]
+                for wave in range(WAVES)
+            ]
+            for t in range(1, n_grp):
+                for way in range(2):
+                    for wave in range(WAVES):
+                        tiles = got[wave][way]
+                        tiles.append(lax.ppermute(tiles[-1], "grp", ring[way]))
+            nexts = [tile for ways in got for tiles in ways for tile in tiles]
             users = after
             slabs = nexts
         items = None

time: 288 us -> 288 us (level)
  starting transfers between devices: 175 us -> 170 us
  waiting for transfers between devices: 88.5 us -> 93.4 us
    ppermute x84, waiting for transfers between devices: 51 us -> 57.3 us  [per_device(): tiles.append(lax.ppermute(tiles[-1], 'grp', ring[way]))]
    ppermute x84, starting transfers between devices: 80.7 us -> 74.5 us  [per_device(): tiles.append(lax.ppermute(tiles[-1], 'grp', ring[way]))]
  transfers between devices with their start and end apart: 172 -> 172, of which waited for: 122 -> 132; matrix products, arithmetic and copies ran while one was open for 1% -> 1% of each run, Pallas kernels for 2% -> 2%
where the time goes in v5:
time: 288 us
  starting transfers between devices  170 us (59%)
  waiting for transfers between devices  93.4 us (32%)
  Pallas kernels  20 us (7%)
    ppermute x76, starting transfers between devices, per_device(): parts[way] = lax.ppermute(part, 'grp', ring[way])  83.6 us
    ppermute x84, starting transfers between devices, per_device(): tiles.append(lax.ppermute(tiles[-1], 'grp', ring[way]))  74.5 us
    ppermute x84, waiting for transfers between devices, per_device(): tiles.append(lax.ppermute(tiles[-1], 'grp', ring[way]))  57.3 us
    ppermute x76, waiting for transfers between devices, per_device(): parts[way] = lax.ppermute(part, 'grp', ring[way])  34.1 us
    pallas_call x2, Pallas kernels, tile_step(): pl.pallas_call(functools.partial(tile_kernel, sub, side, n_own), out_shap...  9.61 us
    ppermute x8, starting transfers between devices, per_device(): parts[way] = lax.ppermute(part, ('strat', 'grp'), last[way])  8 us
    pallas_call x2, Pallas kernels, first_step(): pl.pallas_call(functools.partial(first_kernel, wave, side, n_own), out_sh...  7.5 us
  transfers between devices with their start and end apart: 172, of which 132 were waited for; matrix products, arithmetic and copies ran while one was open for 1% of the time, Pallas kernels for 2%

profile of v5, /device:TPU:0, one launch (start us, length us, event | category | flops | bytes accessed | tf_op | source)
XLA Modules:
  0.0 287.9 jit_solution(13949112346513310066)
XLA Ops:
  2.6 4.4 %tiles_0_0.1 = (f32[1024,256]{1,0:T(8,128)S(1)}, f32[128,256]{1,0:T(8,128)S(1)}, f32[128,256]{1,0:T(8,128)S(1)}, f32[6,128,256]{2,1,0:T(8,128)S(1)}, f32[6,128,2...) custom-call(s32[3,2,16]{2,1,0:T(2,128)S(1)} %bitcast.180, s32[3]{0:T(128)S(1)} %bitcast.184, s32[1]{0:T(128)} %bitcast.2.refs_2_.refs_0_, ...), custom_call_target="tpu_custom_call" | custom-call | flops 201326592 | bytes 8388608 | tf_op jit(solution)/shard_map/tiles_0_0/pallas_call | solution.py:190
  7.0 2.3 collective-permute-start.1
  10.2 3.1 %tiles_0_1.1 = (f32[1024,256]{1,0:T(8,128)S(1)}, f32[128,256]{1,0:T(8,128)S(1)}, f32[128,256]{1,0:T(8,128)S(1)}, f32[6,128,256]{2,1,0:T(8,128)S(1)}, f32[6,128,2...) custom-call(s32[3,2,16]{2,1,0:T(2,128)S(1)} %bitcast.181, s32[3]{0:T(128)S(1)} %bitcast.185, ...), custom_call_target="tpu_custom_call", output_to_operand_aliasing={{0}: (4, {})} | custom-call | flops 201326592 | bytes 8388608 | tf_op jit(solution)/shard_map/tiles_0_1/pallas_call | solution.py:190
  13.3 2.3 collective-permute-start.30
  15.6 1.9 collective-permute-start.29
  19.0 2.1 collective-permute-start.16
  21.1 2.0 collective-permute-start.31
  24.2 2.1 collective-permute-start.3
  26.9 2.2 collective-permute-start.32
  30.5 2.2 collective-permute-start.4
  33.3 2.3 collective-permute-start.33
  40.1 1.7 collective-permute-start.34
  43.0 1.6 collective-permute-start.6
  46.6 1.5 collective-permute-start.35
  50.3 2.4 collective-permute-start.21
  53.6 1.9 collective-permute-start.50
  58.2 1.4 collective-permute-start.37
  60.4 1.5 collective-permute-done.8.refs_5_
  97.8 1.5 collective-permute-done.28.refs_19_
  99.3 1.4 collective-permute-done.43.refs_27_
  102.1 4.0 %tiles_1.1 = (f32[1024,256]{1,0:T(8,128)S(1)}, f32[128,256]{1,0:T(8,128)S(1)}, f32[128,256]{1,0:T(8,128)S(1)}, f32[128,256]{1,0:T(8,128)S(1)}, f32[128,256]{1,0:...) custom-call(s32[3,2,16]{2,1,0:T(2,128)S(1)} %bitcast.182, ...), custom_call_target="tpu_custom_call" | custom-call | flops 402653184 | bytes 16777216 | tf_op jit(solution)/shard_map/tiles_1/pallas_call | solution.py:87
  106.1 2.7 collective-permute-start.59
  108.8 2.0 collective-permute-start.88
  112.1 1.6 collective-permute-done.73
  118.0 2.0 collective-permute-done.60
  125.7 1.7 collective-permute-start.62
  128.6 1.6 collective-permute-start.91
  131.8 1.5 collective-permute-start.63
  134.8 1.9 collective-permute-start.92
  137.9 1.6 collective-permute-start.64
  140.7 1.9 collective-permute-start.93
  144.6 1.4 collective-permute-start.79
  146.0 1.6 collective-permute-start.94
  148.6 1.9 collective-permute-start.66
  151.6 1.8 collective-permute-start.95
  154.7 1.8 collective-permute-start.67
  157.9 1.6 collective-permute-start.96
  160.8 1.8 collective-permute-start.68
  163.7 1.9 collective-permute-start.97
  166.7 1.8 collective-permute-start.69
  170.1 1.8 collective-permute-start.98
  173.1 1.7 collective-permute-start.70
  176.0 1.7 collective-permute-start.99
  179.0 1.9 collective-permute-start.71
  182.0 1.9 collective-permute-start.100
  185.3 1.8 collective-permute-start.72
  188.3 1.8 collective-permute-start.101
  191.5 1.4 collective-permute-done.86.refs_19_
  193.3 2.6 collective-permute-done.115.refs_35_
  195.9 5.7 %tiles_2.1 = (f32[1024,256]{1,0:T(8,128)}, f32[128,256]{1,0:T(8,128)S(1)}, f32[128,256]{1,0:T(8,128)S(1)}, f32[128,256]{1,0:T(8,128)S(1)}, f32[128,256]{1,0:T(8,...) custom-call(s32[3,2,16]{2,1,0:T(2,128)S(1)} %bitcast.183, ...), custom_call_target="tpu_custom_call" | custom-call | flops 402653184 | bytes 16777216 | tf_op jit(solution)/shard_map/tiles_2/pallas_call | solution.py:87
  201.6 2.0 collective-permute-start.130
  203.7 2.0 collective-permute-start.158
  215.2 1.8 collective-permute-start.146
  218.1 2.0 collective-permute-start.119
  238.1 1.4 collective-permute-start.136
  241.0 1.4 collective-permute-start.164
  244.5 1.5 collective-permute-start.137
  247.3 1.5 collective-permute-start.165
  251.6 1.4 collective-permute-done.151.refs_3_
  259.8 1.6 collective-permute-start.167
  262.8 1.4 collective-permute-start.140
  269.1 1.4 collective-permute-start.141
  284.1 1.4 lay_0.1.refs_1_
  286.3 1.4 lay_1.1
  (385 shorter events, 162.1 us)
Async XLA Ops:
  7.0 8.5 %collective-permute-start.1 = (f32[128,256]{1,0:T(8,128)S(1)}, f32[128,256]{1,0:T(8,128)S(1)}, u32[]{:S(2)}, u32[]{:S(2)}) collective-permute-start(f32[128,256]{1,0:T(8,128)S(1)} %get-tuple-element.39), channel_id=1, source_target_pairs={{0,2},{2,4},{4,6},{6,7},{7,5},{5,3},{3,1},{1,0},{8,10},{10,12},{12... | collective-permute-start | bytes 393224 | tf_op jit(solution)/shard_map/ppermute | solution.py:317
  9.3 8.1 %collective-permute-start.15 = (f32[128,256]{1,0:T(8,128)S(1)}, f32[128,256]{1,0:T(8,128)S(1)}, u32[]{:S(2)}, u32[]{:S(2)}) collective-permute-start(f32[128,256]{1,0:T(8,128)S(1)} %get-tuple-element.41), channel_id=1, source_target_pairs={{0,1},{2,0},{4,2},{6,4},{7,6},{5,7},{3,5},{1,3},{8,9},{10,8},{12,1... | collective-permute-start | bytes 393224 | tf_op jit(solution)/shard_map/ppermute | solution.py:317
  9.3 17.1 %collective-permute-start = (f32[2,128,256]{2,1,0:T(8,128)S(1)}, f32[2,128,256]{2,1,0:T(8,128)S(1)}, u32[]{:S(2)}, u32[]{:S(2)}) collective-permute-start(f32[2,128,256]{2,1,0:T(8,128)S(1)} %get-tuple-element.38), channel_id=1, source_target_pairs={{0,24},{8,0},{16,8},{24,16},{1,25},{9,1},{17,9},{25,17},{2,26},{10... | collective-permute-start | bytes 786440 | tf_op jit(solution)/shard_map/ppermute | solution.py:305
  15.6 40.0 %collective-permute-start.29 = (f32[2,128,256]{2,1,0:T(8,128)S(1)}, f32[2,128,256]{2,1,0:T(8,128)S(1)}, u32[]{:S(2)}, u32[]{:S(2)}) collective-permute-start(f32[2,128,256]{2,1,0:T(8,128)S(1)} %get-tuple-element.43), channel_id=1, source_target_pairs={{0,24},{8,0},{16,8},{24,16},{1,25},{9,1},{17,9},{25,17},{2,26},{10... | collective-permute-start | bytes 786440 | tf_op jit(solution)/shard_map/ppermute | solution.py:305
  24.2 6.2 %collective-permute-start.3 = (f32[128,256]{1,0:T(8,128)S(1)}, f32[128,256]{1,0:T(8,128)S(1)}, u32[]{:S(2)}, u32[]{:S(2)}) collective-permute-start(f32[128,256]{1,0:T(8,128)S(1)} %bitcast_add_fusion.70), channel_id=1, source_target_pairs={{0,2},{2,4},{4,6},{6,7},{7,5},{5,3},{3,1},{1,0},{8,10},{10,12},{12... | collective-permute-start | bytes 393224 | tf_op jit(solution)/shard_map/ppermute | solution.py:317
  26.4 6.7 %collective-permute-start.17 = (f32[128,256]{1,0:T(8,128)S(1)}, f32[128,256]{1,0:T(8,128)S(1)}, u32[]{:S(2)}, u32[]{:S(2)}) collective-permute-start(f32[128,256]{1,0:T(8,128)S(1)} %bitcast_add_fusion.64), channel_id=1, source_target_pairs={{0,1},{2,0},{4,2},{6,4},{7,6},{5,7},{3,5},{1,3},{8,9},{10,8},{12,1... | collective-permute-start | bytes 393224 | tf_op jit(solution)/shard_map/ppermute | solution.py:317
  26.9 6.4 %collective-permute-start.32 = (f32[128,256]{1,0:T(8,128)S(1)}, f32[128,256]{1,0:T(8,128)S(1)}, u32[]{:S(2)}, u32[]{:S(2)}) collective-permute-start(f32[128,256]{1,0:T(8,128)S(1)} %bitcast_add_fusion.58), channel_id=1, source_target_pairs={{0,2},{2,4},{4,6},{6,7},{7,5},{5,3},{3,1},{1,0},{8,10},{10,12},{12... | collective-permute-start | bytes 393224 | tf_op jit(solution)/shard_map/ppermute | solution.py:317
  29.1 6.9 %collective-permute-start.46 = (f32[128,256]{1,0:T(8,128)S(1)}, f32[128,256]{1,0:T(8,128)S(1)}, u32[]{:S(2)}, u32[]{:S(2)}) collective-permute-start(f32[128,256]{1,0:T(8,128)S(1)} %bitcast_add_fusion.52), channel_id=1, source_target_pairs={{0,1},{2,0},{4,2},{6,4},{7,6},{5,7},{3,5},{1,3},{8,9},{10,8},{12,1... | collective-permute-start | bytes 393224 | tf_op jit(solution)/shard_map/ppermute | solution.py:317
  30.5 6.8 %collective-permute-start.4 = (f32[128,256]{1,0:T(8,128)S(1)}, f32[128,256]{1,0:T(8,128)S(1)}, u32[]{:S(2)}, u32[]{:S(2)}) collective-permute-start(f32[128,256]{1,0:T(8,128)S(1)} %bitcast_add_fusion.69), channel_id=1, source_target_pairs={{0,2},{2,4},{4,6},{6,7},{7,5},{5,3},{3,1},{1,0},{8,10},{10,12},{12... | collective-permute-start | bytes 393224 | tf_op jit(solution)/shard_map/ppermute | solution.py:317
  33.3 6.8 %collective-permute-start.33 = (f32[128,256]{1,0:T(8,128)S(1)}, f32[128,256]{1,0:T(8,128)S(1)}, u32[]{:S(2)}, u32[]{:S(2)}) collective-permute-start(f32[128,256]{1,0:T(8,128)S(1)} %bitcast_add_fusion.57), channel_id=1, source_target_pairs={{0,2},{2,4},{4,6},{6,7},{7,5},{5,3},{3,1},{1,0},{8,10},{10,12},{12... | collective-permute-start | bytes 393224 | tf_op jit(solution)/shard_map/ppermute | solution.py:317
  36.0 6.3 %collective-permute-start.47 = (f32[128,256]{1,0:T(8,128)S(1)}, f32[128,256]{1,0:T(8,128)S(1)}, u32[]{:S(2)}, u32[]{:S(2)}) collective-permute-start(f32[128,256]{1,0:T(8,128)S(1)} %bitcast_add_fusion.51), channel_id=1, source_target_pairs={{0,1},{2,0},{4,2},{6,4},{7,6},{5,7},{3,5},{1,3},{8,9},{10,8},{12,1... | collective-permute-start | bytes 393224 | tf_op jit(solution)/shard_map/ppermute | solution.py:317
  40.1 6.4 %collective-permute-start.34 = (f32[128,256]{1,0:T(8,128)S(1)}, f32[128,256]{1,0:T(8,128)S(1)}, u32[]{:S(2)}, u32[]{:S(2)}) collective-permute-start(f32[128,256]{1,0:T(8,128)S(1)} %bitcast_add_fusion.56), channel_id=1, source_target_pairs={{0,2},{2,4},{4,6},{6,7},{7,5},{5,3},{3,1},{1,0},{8,10},{10,12},{12... | collective-permute-start | bytes 393224 | tf_op jit(solution)/shard_map/ppermute | solution.py:317
  48.9 6.7 %collective-permute-start.7 = (f32[128,256]{1,0:T(8,128)S(1)}, f32[128,256]{1,0:T(8,128)S(1)}, u32[]{:S(2)}, u32[]{:S(2)}) collective-permute-start(f32[128,256]{1,0:T(8,128)S(1)} %bitcast_add_fusion.66), channel_id=1, source_target_pairs={{0,26},{2,28},{4,30},{6,31},{7,29},{5,27},{3,25},{1,24},{8,2},{10,... | collective-permute-start | bytes 393224 | tf_op jit(solution)/shard_map/ppermute | solution.py:315
  50.3 6.4 %collective-permute-start.21 = (f32[128,256]{1,0:T(8,128)S(1)}, f32[128,256]{1,0:T(8,128)S(1)}, u32[]{:S(2)}, u32[]{:S(2)}) collective-permute-start(f32[128,256]{1,0:T(8,128)S(1)} %bitcast_add_fusion.60), channel_id=1, source_target_pairs={{0,25},{2,24},{4,26},{6,28},{7,30},{5,31},{3,29},{1,27},{8,1},{10,... | collective-permute-start | bytes 393224 | tf_op jit(solution)/shard_map/ppermute | solution.py:315
  55.6 6.3 %collective-permute-start.8 = (f32[128,256]{1,0:T(8,128)S(1)}, f32[128,256]{1,0:T(8,128)S(1)}, u32[]{:S(2)}, u32[]{:S(2)}) collective-permute-start(f32[128,256]{1,0:T(8,128)S(1)} %add.264.refs_4_), channel_id=1, source_target_pairs={{0,2},{2,4},{4,6},{6,7},{7,5},{5,3},{3,1},{1,0},{8,10},{10,12},{12... | collective-permute-start | bytes 393224 | tf_op jit(solution)/shard_map/ppermute | solution.py:326
  56.7 6.4 %collective-permute-start.22 = (f32[128,256]{1,0:T(8,128)S(1)}, f32[128,256]{1,0:T(8,128)S(1)}, u32[]{:S(2)}, u32[]{:S(2)}) collective-permute-start(f32[128,256]{1,0:T(8,128)S(1)} %add.271.refs_12_), channel_id=1, source_target_pairs={{0,1},{2,0},{4,2},{6,4},{7,6},{5,7},{3,5},{1,3},{8,9},{10,8},{12,1... | collective-permute-start | bytes 393224 | tf_op jit(solution)/shard_map/ppermute | solution.py:326
  58.2 6.2 %collective-permute-start.37 = (f32[128,256]{1,0:T(8,128)S(1)}, f32[128,256]{1,0:T(8,128)S(1)}, u32[]{:S(2)}, u32[]{:S(2)}) collective-permute-start(f32[128,256]{1,0:T(8,128)S(1)} %add.278.refs_20_), channel_id=1, source_target_pairs={{0,2},{2,4},{4,6},{6,7},{7,5},{5,3},{3,1},{1,0},{8,10},{10,12},{12... | collective-permute-start | bytes 393224 | tf_op jit(solution)/shard_map/ppermute | solution.py:326
  59.7 6.4 %collective-permute-start.51 = (f32[128,256]{1,0:T(8,128)S(1)}, f32[128,256]{1,0:T(8,128)S(1)}, u32[]{:S(2)}, u32[]{:S(2)}) collective-permute-start(f32[128,256]{1,0:T(8,128)S(1)} %add.285.refs_28_), channel_id=1, source_target_pairs={{0,1},{2,0},{4,2},{6,4},{7,6},{5,7},{3,5},{1,3},{8,9},{10,8},{12,1... | collective-permute-start | bytes 393224 | tf_op jit(solution)/shard_map/ppermute | solution.py:326
  64.5 6.5 %collective-permute-start.38 = (f32[128,256]{1,0:T(8,128)S(1)}, f32[128,256]{1,0:T(8,128)S(1)}, u32[]{:S(2)}, u32[]{:S(2)}) collective-permute-start(f32[128,256]{1,0:T(8,128)S(1)} %collective-permute-done.37.refs_21_), channel_id=1, source_target_pairs={{0,2},{2,4},{4,6},{6,7},{7,5},{5,3},{3,1},{1,0},{8,10},{10,12},{12... | collective-permute-start | bytes 393224 | tf_op jit(solution)/shard_map/ppermute | solution.py:326
  69.0 6.5 %collective-permute-start.24 = (f32[128,256]{1,0:T(8,128)S(1)}, f32[128,256]{1,0:T(8,128)S(1)}, u32[]{:S(2)}, u32[]{:S(2)}) collective-permute-start(f32[128,256]{1,0:T(8,128)S(1)} %collective-permute-done.23.refs_14_), channel_id=1, source_target_pairs={{0,1},{2,0},{4,2},{6,4},{7,6},{5,7},{3,5},{1,3},{8,9},{10,8},{12,1... | collective-permute-start | bytes 393224 | tf_op jit(solution)/shard_map/ppermute | solution.py:326
  73.8 6.5 %collective-permute-start.11 = (f32[128,256]{1,0:T(8,128)S(1)}, f32[128,256]{1,0:T(8,128)S(1)}, u32[]{:S(2)}, u32[]{:S(2)}) collective-permute-start(f32[128,256]{1,0:T(8,128)S(1)} %collective-permute-done.10.refs_7_), channel_id=1, source_target_pairs={{0,2},{2,4},{4,6},{6,7},{7,5},{5,3},{3,1},{1,0},{8,10},{10,12},{12... | collective-permute-start | bytes 393224 | tf_op jit(solution)/shard_map/ppermute | solution.py:326
  78.4 6.5 %collective-permute-start.54 = (f32[128,256]{1,0:T(8,128)S(1)}, f32[128,256]{1,0:T(8,128)S(1)}, u32[]{:S(2)}, u32[]{:S(2)}) collective-permute-start(f32[128,256]{1,0:T(8,128)S(1)} %collective-permute-done.53.refs_31_), channel_id=1, source_target_pairs={{0,1},{2,0},{4,2},{6,4},{7,6},{5,7},{3,5},{1,3},{8,9},{10,8},{12,1... | collective-permute-start | bytes 393224 | tf_op jit(solution)/shard_map/ppermute | solution.py:326
  81.6 6.2 %collective-permute-start.26 = (f32[128,256]{1,0:T(8,128)S(1)}, f32[128,256]{1,0:T(8,128)S(1)}, u32[]{:S(2)}, u32[]{:S(2)}) collective-permute-start(f32[128,256]{1,0:T(8,128)S(1)} %collective-permute-done.25.refs_16_), channel_id=1, source_target_pairs={{0,1},{2,0},{4,2},{6,4},{7,6},{5,7},{3,5},{1,3},{8,9},{10,8},{12,1... | collective-permute-start | bytes 393224 | tf_op jit(solution)/shard_map/ppermute | solution.py:326
  83.2 6.4 %collective-permute-start.41 = (f32[128,256]{1,0:T(8,128)S(1)}, f32[128,256]{1,0:T(8,128)S(1)}, u32[]{:S(2)}, u32[]{:S(2)}) collective-permute-start(f32[128,256]{1,0:T(8,128)S(1)} %collective-permute-done.40.refs_24_), channel_id=1, source_target_pairs={{0,2},{2,4},{4,6},{6,7},{7,5},{5,3},{3,1},{1,0},{8,10},{10,12},{12... | collective-permute-start | bytes 393224 | tf_op jit(solution)/shard_map/ppermute | solution.py:326
  87.8 6.4 %collective-permute-start.27 = (f32[128,256]{1,0:T(8,128)S(1)}, f32[128,256]{1,0:T(8,128)S(1)}, u32[]{:S(2)}, u32[]{:S(2)}) collective-permute-start(f32[128,256]{1,0:T(8,128)S(1)} %collective-permute-done.26.refs_17_), channel_id=1, source_target_pairs={{0,1},{2,0},{4,2},{6,4},{7,6},{5,7},{3,5},{1,3},{8,9},{10,8},{12,1... | collective-permute-start | bytes 393224 | tf_op jit(solution)/shard_map/ppermute | solution.py:326
  111.3 37.1 %collective-permute-start.87 = (f32[2,128,256]{2,1,0:T(8,128)S(1)}, f32[2,128,256]{2,1,0:T(8,128)S(1)}, u32[]{:S(2)}, u32[]{:S(2)}) collective-permute-start(f32[2,128,256]{2,1,0:T(8,128)S(1)} %get-tuple-element.54), channel_id=1, source_target_pairs={{0,24},{8,0},{16,8},{24,16},{1,25},{9,1},{17,9},{25,17},{2,26},{10... | collective-permute-start | bytes 786440 | tf_op jit(solution)/shard_map/ppermute | solution.py:305
  113.7 6.3 %collective-permute-start.60 = (f32[128,256]{1,0:T(8,128)S(1)}, f32[128,256]{1,0:T(8,128)S(1)}, u32[]{:S(2)}, u32[]{:S(2)}) collective-permute-start(f32[128,256]{1,0:T(8,128)S(1)} %bitcast_add_fusion.47), channel_id=1, source_target_pairs={{0,2},{2,4},{4,6},{6,7},{7,5},{5,3},{3,1},{1,0},{8,10},{10,12},{12... | collective-permute-start | bytes 393224 | tf_op jit(solution)/shard_map/ppermute | solution.py:317
  114.6 6.4 %collective-permute-start.74 = (f32[128,256]{1,0:T(8,128)S(1)}, f32[128,256]{1,0:T(8,128)S(1)}, u32[]{:S(2)}, u32[]{:S(2)}) collective-permute-start(f32[128,256]{1,0:T(8,128)S(1)} %bitcast_add_fusion.41), channel_id=1, source_target_pairs={{0,1},{2,0},{4,2},{6,4},{7,6},{5,7},{3,5},{1,3},{8,9},{10,8},{12,1... | collective-permute-start | bytes 393224 | tf_op jit(solution)/shard_map/ppermute | solution.py:317
  115.9 6.8 %collective-permute-start.89 = (f32[128,256]{1,0:T(8,128)S(1)}, f32[128,256]{1,0:T(8,128)S(1)}, u32[]{:S(2)}, u32[]{:S(2)}) collective-permute-start(f32[128,256]{1,0:T(8,128)S(1)} %bitcast_add_fusion.35), channel_id=1, source_target_pairs={{0,2},{2,4},{4,6},{6,7},{7,5},{5,3},{3,1},{1,0},{8,10},{10,12},{12... | collective-permute-start | bytes 393224 | tf_op jit(solution)/shard_map/ppermute | solution.py:317
  116.8 7.2 %collective-permute-start.103 = (f32[128,256]{1,0:T(8,128)S(1)}, f32[128,256]{1,0:T(8,128)S(1)}, u32[]{:S(2)}, u32[]{:S(2)}) collective-permute-start(f32[128,256]{1,0:T(8,128)S(1)} %bitcast_add_fusion.29), channel_id=1, source_target_pairs={{0,1},{2,0},{4,2},{6,4},{7,6},{5,7},{3,5},{1,3},{8,9},{10,8},{12,1... | collective-permute-start | bytes 393224 | tf_op jit(solution)/shard_map/ppermute | solution.py:317
  121.0 6.4 %collective-permute-start.75 = (f32[128,256]{1,0:T(8,128)S(1)}, f32[128,256]{1,0:T(8,128)S(1)}, u32[]{:S(2)}, u32[]{:S(2)}) collective-permute-start(f32[128,256]{1,0:T(8,128)S(1)} %bitcast_add_fusion.40), channel_id=1, source_target_pairs={{0,1},{2,0},{4,2},{6,4},{7,6},{5,7},{3,5},{1,3},{8,9},{10,8},{12,1... | collective-permute-start | bytes 393224 | tf_op jit(solution)/shard_map/ppermute | solution.py:317
  130.2 6.5 %collective-permute-start.105 = (f32[128,256]{1,0:T(8,128)S(1)}, f32[128,256]{1,0:T(8,128)S(1)}, u32[]{:S(2)}, u32[]{:S(2)}) collective-permute-start(f32[128,256]{1,0:T(8,128)S(1)} %bitcast_add_fusion.27), channel_id=1, source_target_pairs={{0,1},{2,0},{4,2},{6,4},{7,6},{5,7},{3,5},{1,3},{8,9},{10,8},{12,1... | collective-permute-start | bytes 393224 | tf_op jit(solution)/shard_map/ppermute | solution.py:317
  150.5 6.3 %collective-permute-start.80 = (f32[128,256]{1,0:T(8,128)S(1)}, f32[128,256]{1,0:T(8,128)S(1)}, u32[]{:S(2)}, u32[]{:S(2)}) collective-permute-start(f32[128,256]{1,0:T(8,128)S(1)} %add.299.refs_12_), channel_id=1, source_target_pairs={{0,1},{2,0},{4,2},{6,4},{7,6},{5,7},{3,5},{1,3},{8,9},{10,8},{12,1... | collective-permute-start | bytes 393224 | tf_op jit(solution)/shard_map/ppermute | solution.py:326
  151.6 6.3 %collective-permute-start.95 = (f32[128,256]{1,0:T(8,128)S(1)}, f32[128,256]{1,0:T(8,128)S(1)}, u32[]{:S(2)}, u32[]{:S(2)}) collective-permute-start(f32[128,256]{1,0:T(8,128)S(1)} %add.306.refs_20_), channel_id=1, source_target_pairs={{0,2},{2,4},{4,6},{6,7},{7,5},{5,3},{3,1},{1,0},{8,10},{10,12},{12... | collective-permute-start | bytes 393224 | tf_op jit(solution)/shard_map/ppermute | solution.py:326
  156.8 6.3 %collective-permute-start.81 = (f32[128,256]{1,0:T(8,128)S(1)}, f32[128,256]{1,0:T(8,128)S(1)}, u32[]{:S(2)}, u32[]{:S(2)}) collective-permute-start(f32[128,256]{1,0:T(8,128)S(1)} %collective-permute-done.80.refs_13_), channel_id=1, source_target_pairs={{0,1},{2,0},{4,2},{6,4},{7,6},{5,7},{3,5},{1,3},{8,9},{10,8},{12,1... | collective-permute-start | bytes 393224 | tf_op jit(solution)/shard_map/ppermute | solution.py:326
  163.1 6.3 %collective-permute-start.82 = (f32[128,256]{1,0:T(8,128)S(1)}, f32[128,256]{1,0:T(8,128)S(1)}, u32[]{:S(2)}, u32[]{:S(2)}) collective-permute-start(f32[128,256]{1,0:T(8,128)S(1)} %collective-permute-done.81.refs_14_), channel_id=1, source_target_pairs={{0,1},{2,0},{4,2},{6,4},{7,6},{5,7},{3,5},{1,3},{8,9},{10,8},{12,1... | collective-permute-start | bytes 393224 | tf_op jit(solution)/shard_map/ppermute | solution.py:326
  163.7 6.4 %collective-permute-start.97 = (f32[128,256]{1,0:T(8,128)S(1)}, f32[128,256]{1,0:T(8,128)S(1)}, u32[]{:S(2)}, u32[]{:S(2)}) collective-permute-start(f32[128,256]{1,0:T(8,128)S(1)} %collective-permute-done.96.refs_22_), channel_id=1, source_target_pairs={{0,2},{2,4},{4,6},{6,7},{7,5},{5,3},{3,1},{1,0},{8,10},{10,12},{12... | collective-permute-start | bytes 393224 | tf_op jit(solution)/shard_map/ppermute | solution.py:326
  166.0 6.4 %collective-permute-start.111 = (f32[128,256]{1,0:T(8,128)S(1)}, f32[128,256]{1,0:T(8,128)S(1)}, u32[]{:S(2)}, u32[]{:S(2)}) collective-permute-start(f32[128,256]{1,0:T(8,128)S(1)} %collective-permute-done.110.refs_30_), channel_id=1, source_target_pairs={{0,1},{2,0},{4,2},{6,4},{7,6},{5,7},{3,5},{1,3},{8,9},{10,8},{12,1... | collective-permute-start | bytes 393224 | tf_op jit(solution)/shard_map/ppermute | solution.py:326
  166.7 6.4 %collective-permute-start.69 = (f32[128,256]{1,0:T(8,128)S(1)}, f32[128,256]{1,0:T(8,128)S(1)}, u32[]{:S(2)}, u32[]{:S(2)}) collective-permute-start(f32[128,256]{1,0:T(8,128)S(1)} %collective-permute-done.68.refs_7_), channel_id=1, source_target_pairs={{0,2},{2,4},{4,6},{6,7},{7,5},{5,3},{3,1},{1,0},{8,10},{10,12},{12... | collective-permute-start | bytes 393224 | tf_op jit(solution)/shard_map/ppermute | solution.py:326
  178.6 6.4 %collective-permute-start.113 = (f32[128,256]{1,0:T(8,128)S(1)}, f32[128,256]{1,0:T(8,128)S(1)}, u32[]{:S(2)}, u32[]{:S(2)}) collective-permute-start(f32[128,256]{1,0:T(8,128)S(1)} %collective-permute-done.112.refs_32_), channel_id=1, source_target_pairs={{0,1},{2,0},{4,2},{6,4},{7,6},{5,7},{3,5},{1,3},{8,9},{10,8},{12,1... | collective-permute-start | bytes 393224 | tf_op jit(solution)/shard_map/ppermute | solution.py:326
  179.0 6.3 %collective-permute-start.71 = (f32[128,256]{1,0:T(8,128)S(1)}, f32[128,256]{1,0:T(8,128)S(1)}, u32[]{:S(2)}, u32[]{:S(2)}) collective-permute-start(f32[128,256]{1,0:T(8,128)S(1)} %collective-permute-done.70.refs_9_), channel_id=1, source_target_pairs={{0,2},{2,4},{4,6},{6,7},{7,5},{5,3},{3,1},{1,0},{8,10},{10,12},{12... | collective-permute-start | bytes 393224 | tf_op jit(solution)/shard_map/ppermute | solution.py:326
  181.6 6.3 %collective-permute-start.85 = (f32[128,256]{1,0:T(8,128)S(1)}, f32[128,256]{1,0:T(8,128)S(1)}, u32[]{:S(2)}, u32[]{:S(2)}) collective-permute-start(f32[128,256]{1,0:T(8,128)S(1)} %collective-permute-done.84.refs_17_), channel_id=1, source_target_pairs={{0,1},{2,0},{4,2},{6,4},{7,6},{5,7},{3,5},{1,3},{8,9},{10,8},{12,1... | collective-permute-start | bytes 393224 | tf_op jit(solution)/shard_map/ppermute | solution.py:326
  182.0 6.3 %collective-permute-start.100 = (f32[128,256]{1,0:T(8,128)S(1)}, f32[128,256]{1,0:T(8,128)S(1)}, u32[]{:S(2)}, u32[]{:S(2)}) collective-permute-start(f32[128,256]{1,0:T(8,128)S(1)} %collective-permute-done.99.refs_25_), channel_id=1, source_target_pairs={{0,2},{2,4},{4,6},{6,7},{7,5},{5,3},{3,1},{1,0},{8,10},{10,12},{12... | collective-permute-start | bytes 393224 | tf_op jit(solution)/shard_map/ppermute | solution.py:326
  201.6 6.4 %collective-permute-start.130 = (f32[128,256]{1,0:T(8,128)S(1)}, f32[128,256]{1,0:T(8,128)S(1)}, u32[]{:S(2)}, u32[]{:S(2)}) collective-permute-start(f32[128,256]{1,0:T(8,128)S(1)} %get-tuple-element.63), channel_id=1, source_target_pairs={{0,1},{2,0},{4,2},{6,4},{7,6},{5,7},{3,5},{1,3},{8,9},{10,8},{12,1... | collective-permute-start | bytes 393224 | tf_op jit(solution)/shard_map/ppermute | solution.py:317
  203.7 7.1 %collective-permute-start.158 = (f32[128,256]{1,0:T(8,128)S(1)}, f32[128,256]{1,0:T(8,128)S(1)}, u32[]{:S(2)}, u32[]{:S(2)}) collective-permute-start(f32[128,256]{1,0:T(8,128)S(1)} %get-tuple-element.68), channel_id=1, source_target_pairs={{0,1},{2,0},{4,2},{6,4},{7,6},{5,7},{3,5},{1,3},{8,9},{10,8},{12,1... | collective-permute-start | bytes 393224 | tf_op jit(solution)/shard_map/ppermute | solution.py:317
  213.7 6.4 %collective-permute-start.132 = (f32[128,256]{1,0:T(8,128)S(1)}, f32[128,256]{1,0:T(8,128)S(1)}, u32[]{:S(2)}, u32[]{:S(2)}) collective-permute-start(f32[128,256]{1,0:T(8,128)S(1)} %bitcast_add_fusion.16), channel_id=1, source_target_pairs={{0,1},{2,0},{4,2},{6,4},{7,6},{5,7},{3,5},{1,3},{8,9},{10,8},{12,1... | collective-permute-start | bytes 393224 | tf_op jit(solution)/shard_map/ppermute | solution.py:317
  215.2 6.4 %collective-permute-start.146 = (f32[128,256]{1,0:T(8,128)S(1)}, f32[128,256]{1,0:T(8,128)S(1)}, u32[]{:S(2)}, u32[]{:S(2)}) collective-permute-start(f32[128,256]{1,0:T(8,128)S(1)} %bitcast_add_fusion.10), channel_id=1, source_target_pairs={{0,2},{2,4},{4,6},{6,7},{7,5},{5,3},{3,1},{1,0},{8,10},{10,12},{12... | collective-permute-start | bytes 393224 | tf_op jit(solution)/shard_map/ppermute | solution.py:317
  218.1 6.4 %collective-permute-start.119 = (f32[128,256]{1,0:T(8,128)S(1)}, f32[128,256]{1,0:T(8,128)S(1)}, u32[]{:S(2)}, u32[]{:S(2)}) collective-permute-start(f32[128,256]{1,0:T(8,128)S(1)} %bitcast_add_fusion.21), channel_id=1, source_target_pairs={{0,2},{2,4},{4,6},{6,7},{7,5},{5,3},{3,1},{1,0},{8,10},{10,12},{12... | collective-permute-start | bytes 393224 | tf_op jit(solution)/shard_map/ppermute | solution.py:317
  221.7 6.4 %collective-permute-start.147 = (f32[128,256]{1,0:T(8,128)S(1)}, f32[128,256]{1,0:T(8,128)S(1)}, u32[]{:S(2)}, u32[]{:S(2)}) collective-permute-start(f32[128,256]{1,0:T(8,128)S(1)} %bitcast_add_fusion.9), channel_id=1, source_target_pairs={{0,2},{2,4},{4,6},{6,7},{7,5},{5,3},{3,1},{1,0},{8,10},{10,12},{12... | collective-permute-start | bytes 393224 | tf_op jit(solution)/shard_map/ppermute | solution.py:317
  224.5 6.3 %collective-permute-start.120 = (f32[128,256]{1,0:T(8,128)S(1)}, f32[128,256]{1,0:T(8,128)S(1)}, u32[]{:S(2)}, u32[]{:S(2)}) collective-permute-start(f32[128,256]{1,0:T(8,128)S(1)} %bitcast_add_fusion.20), channel_id=1, source_target_pairs={{0,2},{2,4},{4,6},{6,7},{7,5},{5,3},{3,1},{1,0},{8,10},{10,12},{12... | collective-permute-start | bytes 393224 | tf_op jit(solution)/shard_map/ppermute | solution.py:317
  230.9 6.4 %collective-permute-start.121 = (f32[128,256]{1,0:T(8,128)S(1)}, f32[128,256]{1,0:T(8,128)S(1)}, u32[]{:S(2)}, u32[]{:S(2)}) collective-permute-start(f32[128,256]{1,0:T(8,128)S(1)} %bitcast_add_fusion.19), channel_id=1, source_target_pairs={{0,2},{2,4},{4,6},{6,7},{7,5},{5,3},{3,1},{1,0},{8,10},{10,12},{12... | collective-permute-start | bytes 393224 | tf_op jit(solution)/shard_map/ppermute | solution.py:317
  231.7 6.3 %collective-permute-start.135 = (f32[128,256]{1,0:T(8,128)S(1)}, f32[128,256]{1,0:T(8,128)S(1)}, u32[]{:S(2)}, u32[]{:S(2)}) collective-permute-start(f32[128,256]{1,0:T(8,128)S(1)} %bitcast_add_fusion.13), channel_id=1, source_target_pairs={{0,1},{2,0},{4,2},{6,4},{7,6},{5,7},{3,5},{1,3},{8,9},{10,8},{12,1... | collective-permute-start | bytes 393224 | tf_op jit(solution)/shard_map/ppermute | solution.py:317
  233.8 6.4 %collective-permute-start.149 = (f32[128,256]{1,0:T(8,128)S(1)}, f32[128,256]{1,0:T(8,128)S(1)}, u32[]{:S(2)}, u32[]{:S(2)}) collective-permute-start(f32[128,256]{1,0:T(8,128)S(1)} %bitcast_add_fusion.7), channel_id=1, source_target_pairs={{0,2},{2,4},{4,6},{6,7},{7,5},{5,3},{3,1},{1,0},{8,10},{10,12},{12... | collective-permute-start | bytes 393224 | tf_op jit(solution)/shard_map/ppermute | solution.py:317
  237.3 6.4 %collective-permute-start.122 = (f32[128,256]{1,0:T(8,128)S(1)}, f32[128,256]{1,0:T(8,128)S(1)}, u32[]{:S(2)}, u32[]{:S(2)}) collective-permute-start(f32[128,256]{1,0:T(8,128)S(1)} %bitcast_add_fusion.18), channel_id=1, source_target_pairs={{0,2},{2,4},{4,6},{6,7},{7,5},{5,3},{3,1},{1,0},{8,10},{10,12},{12... | collective-permute-start | bytes 393224 | tf_op jit(solution)/shard_map/ppermute | solution.py:317
  238.1 6.4 %collective-permute-start.136 = (f32[128,256]{1,0:T(8,128)S(1)}, f32[128,256]{1,0:T(8,128)S(1)}, u32[]{:S(2)}, u32[]{:S(2)}) collective-permute-start(f32[128,256]{1,0:T(8,128)S(1)} %bitcast_add_fusion.12), channel_id=1, source_target_pairs={{0,1},{2,0},{4,2},{6,4},{7,6},{5,7},{3,5},{1,3},{8,9},{10,8},{12,1... | collective-permute-start | bytes 393224 | tf_op jit(solution)/shard_map/ppermute | solution.py:317
  240.2 6.3 %collective-permute-start.150 = (f32[128,256]{1,0:T(8,128)S(1)}, f32[128,256]{1,0:T(8,128)S(1)}, u32[]{:S(2)}, u32[]{:S(2)}) collective-permute-start(f32[128,256]{1,0:T(8,128)S(1)} %bitcast_add_fusion.6), channel_id=1, source_target_pairs={{0,2},{2,4},{4,6},{6,7},{7,5},{5,3},{3,1},{1,0},{8,10},{10,12},{12... | collective-permute-start | bytes 393224 | tf_op jit(solution)/shard_map/ppermute | solution.py:317
  241.0 6.3 %collective-permute-start.164 = (f32[128,256]{1,0:T(8,128)S(1)}, f32[128,256]{1,0:T(8,128)S(1)}, u32[]{:S(2)}, u32[]{:S(2)}) collective-permute-start(f32[128,256]{1,0:T(8,128)S(1)} %bitcast_add_fusion), channel_id=1, source_target_pairs={{0,1},{2,0},{4,2},{6,4},{7,6},{5,7},{3,5},{1,3},{8,9},{10,8},{12,1... | collective-permute-start | bytes 393224 | tf_op jit(solution)/shard_map/ppermute | solution.py:317
  246.6 6.4 %collective-permute-start.151 = (f32[128,256]{1,0:T(8,128)S(1)}, f32[128,256]{1,0:T(8,128)S(1)}, u32[]{:S(2)}, u32[]{:S(2)}) collective-permute-start(f32[128,256]{1,0:T(8,128)S(1)} %add.334.refs_2_), channel_id=1, source_target_pairs={{0,2},{2,4},{4,6},{6,7},{7,5},{5,3},{3,1},{1,0},{8,10},{10,12},{12... | collective-permute-start | bytes 393224 | tf_op jit(solution)/shard_map/ppermute | solution.py:326
  247.3 6.4 %collective-permute-start.165 = (f32[128,256]{1,0:T(8,128)S(1)}, f32[128,256]{1,0:T(8,128)S(1)}, u32[]{:S(2)}, u32[]{:S(2)}) collective-permute-start(f32[128,256]{1,0:T(8,128)S(1)} %add.341.refs_10_), channel_id=1, source_target_pairs={{0,1},{2,0},{4,2},{6,4},{7,6},{5,7},{3,5},{1,3},{8,9},{10,8},{12,1... | collective-permute-start | bytes 393224 | tf_op jit(solution)/shard_map/ppermute | solution.py:326
  249.6 6.4 %collective-permute-start.124 = (f32[128,256]{1,0:T(8,128)S(1)}, f32[128,256]{1,0:T(8,128)S(1)}, u32[]{:S(2)}, u32[]{:S(2)}) collective-permute-start(f32[128,256]{1,0:T(8,128)S(1)} %collective-permute-done.123.refs_2_), channel_id=1, source_target_pairs={{0,2},{2,4},{4,6},{6,7},{7,5},{5,3},{3,1},{1,0},{8,10},{10,12},{12... | collective-permute-start | bytes 393224 | tf_op jit(solution)/shard_map/ppermute | solution.py:326
  253.0 6.3 %collective-permute-start.152 = (f32[128,256]{1,0:T(8,128)S(1)}, f32[128,256]{1,0:T(8,128)S(1)}, u32[]{:S(2)}, u32[]{:S(2)}) collective-permute-start(f32[128,256]{1,0:T(8,128)S(1)} %collective-permute-done.151.refs_3_), channel_id=1, source_target_pairs={{0,2},{2,4},{4,6},{6,7},{7,5},{5,3},{3,1},{1,0},{8,10},{10,12},{12... | collective-permute-start | bytes 393224 | tf_op jit(solution)/shard_map/ppermute | solution.py:326
  256.0 6.3 %collective-permute-start.125 = (f32[128,256]{1,0:T(8,128)S(1)}, f32[128,256]{1,0:T(8,128)S(1)}, u32[]{:S(2)}, u32[]{:S(2)}) collective-permute-start(f32[128,256]{1,0:T(8,128)S(1)} %collective-permute-done.124.refs_3_), channel_id=1, source_target_pairs={{0,2},{2,4},{4,6},{6,7},{7,5},{5,3},{3,1},{1,0},{8,10},{10,12},{12... | collective-permute-start | bytes 393224 | tf_op jit(solution)/shard_map/ppermute | solution.py:326
  262.2 6.3 %collective-permute-start.126 = (f32[128,256]{1,0:T(8,128)S(1)}, f32[128,256]{1,0:T(8,128)S(1)}, u32[]{:S(2)}, u32[]{:S(2)}) collective-permute-start(f32[128,256]{1,0:T(8,128)S(1)} %collective-permute-done.125.refs_4_), channel_id=1, source_target_pairs={{0,2},{2,4},{4,6},{6,7},{7,5},{5,3},{3,1},{1,0},{8,10},{10,12},{12... | collective-permute-start | bytes 393224 | tf_op jit(solution)/shard_map/ppermute | solution.py:326
  262.8 6.3 %collective-permute-start.140 = (f32[128,256]{1,0:T(8,128)S(1)}, f32[128,256]{1,0:T(8,128)S(1)}, u32[]{:S(2)}, u32[]{:S(2)}) collective-permute-start(f32[128,256]{1,0:T(8,128)S(1)} %collective-permute-done.139.refs_12_), channel_id=1, source_target_pairs={{0,1},{2,0},{4,2},{6,4},{7,6},{5,7},{3,5},{1,3},{8,9},{10,8},{12,1... | collective-permute-start | bytes 393224 | tf_op jit(solution)/shard_map/ppermute | solution.py:326
  (113 other events, 645.0 us)
